TPU v7x, 512 devices: a whole 4x4x16 slice. The times are simulated.
512 devices in a mesh: dp: 64 (over z, x), tensor: 8 (over y, core).
Axes of the slice: x: 4, y: 4, z: 16, core: 2. Of those that a mesh axis runs over, the one named last changes fastest.
Arguments:
- cache_keys: bfloat16 [256, 1024, 1024], P('dp', 'tensor')
- cache_values: bfloat16 [256, 1024, 1024], P('dp', 'tensor'), may hold values from -6 to 6
- cache_lengths: int32 [256], P('dp'), may hold values from 1 to 1024, as said below
- destination: int32 [256], P('dp'), may hold values from -1 to 127, as said below
- queries: bfloat16 [128, 8192], P('dp')
- new_keys: bfloat16 [128, 1024], P('dp')
- new_values: bfloat16 [128, 1024], P('dp'), may hold values from -6 to 6
Outputs:
- moved_keys: bfloat16 [128, 1024, 1024], P('dp', 'tensor')
- moved_values: bfloat16 [128, 1024, 1024], P('dp', 'tensor')
- attended: bfloat16 [128, 8192], P('dp')
Inputs may be any that keep to these rules, and one draw needn't show every extreme that they name: `cache_lengths`: one slot holds exactly 1024 live positions in every draw. `destination`: every survivor index 0 .. 127 is named by exactly one slot and -1 marks a pruned slot. Survivor j is hosted by replica j // 2, so every replica receives exactly 2 survivors; a slot and the survivor it becomes lie on replicas of the same aligned group of 4 replicas along dp, and within a group the survivors follow the order of their slots. A replica keeps from 0 to 4 of its slots.
All inputs are finite; a program needn't handle non-finite values.
Results may differ from a plain program's by a relative error of at most 0.0049.
Values may be sent and summed in bfloat16 or wider, within the bound.
No kernel may reach another device: no remote copies, remote signals or barrier semaphores. Data moves between devices by JAX's collectives and lax.ppermute only.
A program may use at most 64 MiB of HBM per device.

v0:
```python
import jax
import jax.numpy as jnp
from jax import lax
from jax.sharding import PartitionSpec as P

QH = 64
KVH = 8
HD = 128
ROWS_DEV = 2
GROUP = 4


floor_score = -1e30


def passed_along(block, axis, distance):
    devices = range(lax.axis_size(axis))
    route = [(i - distance, i) for i in devices if i - distance in devices]
    return lax.ppermute(block, axis, route)


def combined_all(x, axis, combine):
    everything = jax.tree.map(lambda part: lax.all_gather(part, axis), x)
    leading = jax.tree.map(lambda part: part[0], everything)

    def hop(k, so_far):
        return combine(so_far, jax.tree.map(lambda part: part[k], everything))

    return lax.fori_loop(1, lax.axis_size(axis), hop, leading)


def select_rows(picks, keys, values, lengths):
    chosen = picks.astype(jnp.bfloat16)
    keys_out = jnp.einsum("ors,slf->orlf", chosen, keys, preferred_element_type=jnp.float32).astype(
        jnp.bfloat16
    )
    values_out = jnp.einsum(
        "ors,slf->orlf", chosen, values, preferred_element_type=jnp.float32
    ).astype(jnp.bfloat16)
    lengths_out = jnp.sum(jnp.where(picks, lengths[None, None, :], 0), axis=2)
    return (keys_out, values_out, lengths_out)


def migrate_direct(cache_keys, cache_values, cache_lengths, destination):
    here = lax.axis_index("dp")
    offsets = jnp.arange(1 - GROUP, GROUP, dtype=jnp.int32)
    target_replica = jnp.floor_divide(destination, ROWS_DEV)
    target_row = jnp.remainder(destination, ROWS_DEV)
    live = destination >= 0
    row_ids = lax.iota(jnp.int32, ROWS_DEV)
    picks = live[None, None, :] & (target_replica[None, None, :] == here + offsets[:, None, None])
    picks = picks & (target_row[None, None, :] == row_ids[None, :, None])
    keys_out, values_out, lengths_out = select_rows(picks, cache_keys, cache_values, cache_lengths)
    moved_keys = keys_out[GROUP - 1]
    moved_values = values_out[GROUP - 1]
    moved_lengths = lengths_out[GROUP - 1]
    for offset in range(1 - GROUP, GROUP):
        if offset != 0:
            index = offset + GROUP - 1
            arrived_keys, arrived_values, arrived_lengths = passed_along(
                (keys_out[index], values_out[index], lengths_out[index]), "dp", offset
            )
            moved_keys = moved_keys + arrived_keys
            moved_values = moved_values + arrived_values
            moved_lengths = moved_lengths + arrived_lengths
    return (moved_keys, moved_values, moved_lengths)


def block_attention(queries, moved_keys, moved_values, moved_lengths, first):
    row_count = queries.shape[0]
    span_len = moved_keys.shape[1]
    per_group = QH // KVH
    grouped = queries.reshape(row_count, KVH, per_group, HD)
    keys = moved_keys.reshape(row_count, span_len, KVH, HD)
    values = moved_values.reshape(row_count, span_len, KVH, HD)
    scores = jnp.einsum(
        "rgqd,rlgd->rgql", grouped, keys, preferred_element_type=jnp.float32
    ) * HD ** (-0.5)
    position = first + lax.iota(jnp.int32, span_len)
    valid = (position[None, :] < moved_lengths[:, None])[:, None, None, :]
    peak = jnp.max(jnp.where(valid, scores, floor_score), axis=3)
    weights = jnp.where(valid, jnp.exp(scores - peak[..., None]), 0.0).astype(jnp.bfloat16)
    mass = jnp.sum(weights.astype(jnp.float32), axis=3)
    partial_value = jnp.einsum(
        "rgql,rlgd->rgqd", weights, values, preferred_element_type=jnp.float32
    )
    return (
        peak.reshape(row_count, QH),
        mass.reshape(row_count, QH),
        partial_value.reshape(row_count, QH, HD),
    )


def own_terms(queries, new_keys, new_values):
    row_count = queries.shape[0]
    per_group = QH // KVH
    grouped = queries.reshape(row_count, KVH, per_group, HD)
    own = jnp.einsum(
        "rgqd,rgd->rgq",
        grouped,
        new_keys.reshape(row_count, KVH, HD),
        preferred_element_type=jnp.float32,
    ) * HD ** (-0.5)
    own_values = jnp.broadcast_to(
        new_values.reshape(row_count, KVH, 1, HD).astype(jnp.float32),
        (row_count, KVH, per_group, HD),
    )
    return (own.reshape(row_count, QH), own_values.reshape(row_count, QH, HD))


def join_blocks(first_part, second_part):
    peak_first, mass_first, partial_first = first_part
    peak_second, mass_second, partial_second = second_part
    peak = jnp.maximum(peak_first, peak_second)
    fade_first = jnp.exp(peak_first - peak)
    fade_second = jnp.exp(peak_second - peak)
    mass = mass_first * fade_first + mass_second * fade_second
    partial_value = partial_first * fade_first[..., None] + partial_second * fade_second[..., None]
    return (peak, mass, partial_value)


def finish(peaks, masses, partials, own, own_values):
    top = jnp.maximum(jnp.max(peaks, axis=0), own)
    own_weight = jnp.exp(own - top)
    fades = jnp.exp(peaks - top[None])
    denominator = own_weight + jnp.sum(fades * masses, axis=0)
    numerator = own_weight[..., None] * own_values + jnp.sum(fades[..., None] * partials, axis=0)
    return (numerator / denominator[..., None]).astype(jnp.bfloat16)


def on_device(cache_keys, cache_values, cache_lengths, destination, queries, new_keys, new_values):
    moved_keys, moved_values, moved_lengths = migrate_direct(
        cache_keys, cache_values, cache_lengths, destination
    )
    row_count = queries.shape[0]
    span_len = moved_keys.shape[1]
    peak, mass, partial_value = block_attention(
        queries, moved_keys, moved_values, moved_lengths, lax.axis_index("tensor") * span_len
    )
    own, own_values = own_terms(queries, new_keys, new_values)
    peak, mass, partial_value = combined_all((peak, mass, partial_value), "tensor", join_blocks)
    result = finish(peak[None], mass[None], partial_value[None], own, own_values)
    attended = result.reshape(row_count, QH * HD)
    return (moved_keys, moved_values, attended)


def solution(mesh):
    placed = (
        P("dp", "tensor", None),
        P("dp", "tensor", None),
        P("dp"),
        P("dp"),
        P("dp", None),
        P("dp", None),
        P("dp", None),
    )
    return jax.shard_map(
        on_device,
        mesh=mesh,
        in_specs=placed,
        out_specs=(P("dp", "tensor", None), P("dp", "tensor", None), P("dp", None)),
        check_vma=False,
    )
```

profile of v0, /device:TPU:235, one launch (start us, length us, event | category | flops | bytes accessed | tf_op | source)
XLA Modules:
  0.0 187.8 jit_solution(11316931369500852363)
XLA Ops:
  2.0 2.8 %convolution_convert_fusion.1 = bf16[7,2,128,1024]{3,0,2,1:T(8,128)(2,1)S(1)} fusion(bf16[4,128,1024]{2,1,0:T(8,128)(2,1)} %param.9, pred[2,4]{1,0:T(4,128)(4,1)S(1)} %iota_compare_fusion, pred[7,4]{0,1:T(4,128)(4,1)S(1)} %compare_and_fusion), kind=kOutput, calls=%fused_computation.10 | convolution fusion | flops 16515128 | bytes 4718628 | tf_op jit(solution)/shard_map/ors,slf->orlf/dot_general | solution.py:34
  4.8 6.5 %fusion.35 = (bf16[1,2,128,1024]{3,0,2,1:T(2,128)(2,1)}, bf16[1,2,128,1024]{3,0,2,1:T(2,128)(2,1)S(1)}, bf16[1,2,128,1024]{3,0,2,1:T(2,128)(2,1)S(1)}, bf16[1,2,...) fusion(bf16[7,2,128,1024]{3,0,2,1:T(8,128)(2,1)S(1)} %convoluti, ...), kind=kLoop, calls=%fused_computation.96 | loop fusion | bytes 7340032 | tf_op jit(solution)/shard_map/slice | solution.py:54
  12.3 4.7 %collective-permute-start.5 = (bf16[2,128,1024]{2,1,0:T(8,128)(2,1)}, bf16[2,128,1024]{2,1,0:T(8,128)(2,1)}, u32[]{:S(2)}, u32[]{:S(2)}) collective-permute-start(bf16[2,128,1024]{2,1,0:T(8,128)(2,1)} %bitcast.150), channel_id=1, source_target_pairs={{0,24},{8,32},{16,40},{24,48},{32,56},{40,64},{48,72},{56,80},{64,... | collective-permute-start | bytes 1572872 | tf_op jit(solution)/shard_map/ppermute | solution.py:19
  18.0 4.0 %collective-permute-start.4 = (bf16[2,128,1024]{2,1,0:T(8,128)(2,1)}, bf16[2,128,1024]{2,1,0:T(8,128)(2,1)}, u32[]{:S(2)}, u32[]{:S(2)}) collective-permute-start(bf16[2,128,1024]{2,1,0:T(8,128)(2,1)} %bitcast.151), channel_id=1, source_target_pairs={{0,16},{8,24},{16,32},{24,40},{32,48},{40,56},{48,64},{56,72},{64,... | collective-permute-start | bytes 1572872 | tf_op jit(solution)/shard_map/ppermute | solution.py:19
  23.0 3.4 %collective-permute-start.3 = (bf16[2,128,1024]{2,1,0:T(8,128)(2,1)}, bf16[2,128,1024]{2,1,0:T(8,128)(2,1)}, u32[]{:S(2)}, u32[]{:S(2)}) collective-permute-start(bf16[2,128,1024]{2,1,0:T(8,128)(2,1)} %bitcast.152), channel_id=1, source_target_pairs={{0,8},{8,16},{16,24},{24,32},{32,40},{40,48},{48,56},{56,64},{64,7... | collective-permute-start | bytes 1572872 | tf_op jit(solution)/shard_map/ppermute | solution.py:19
  29.7 6.5 %collective-permute-start.17 = (s32[2]{0:T(128)S(1)}, s32[2]{0:T(128)S(1)}, u32[]{:S(2)}, u32[]{:S(2)}) collective-permute-start(s32[2]{0:T(128)S(1)} %get-tuple-element.185), channel_id=1, source_target_pairs={{0,24},{8,32},{16,40},{24,48},{32,56},{40,64},{48,72},{56,80},{64,... | collective-permute-start | bytes 32 | tf_op jit(solution)/shard_map/ppermute | solution.py:19
  37.9 7.1 %fusion.34 = (bf16[1,2,128,1024]{3,0,2,1:T(2,128)(2,1)}, bf16[1,2,128,1024]{3,0,2,1:T(2,128)(2,1)}, bf16[1,2,128,1024]{3,0,2,1:T(2,128)(2,1)}, bf16[1,2,128,1024...) fusion(bf16[7,2,128,1024]{3,0,2,1:T(8,128)(2,1)S(1)} %convoluti, ...), kind=kLoop, calls=%fused_computation.95 | loop fusion | bytes 7340032 | tf_op jit(solution)/shard_map/slice | solution.py:55
  47.0 2.2 %copy.172 = bf16[1,2,128,1024]{3,2,0,1:T(8,128)(2,1)} copy(bf16[1,2,128,1024]{3,0,2,1:T(2,128)(2,1)} %get-tuple-element.213) | data formatting | bytes 1048576
  53.4 2.2 %collective-permute-start.16 = (s32[2]{0:T(128)S(1)}, s32[2]{0:T(128)S(1)}, u32[]{:S(2)}, u32[]{:S(2)}) collective-permute-start(s32[2]{0:T(128)S(1)} %get-tuple-element.186), channel_id=1, source_target_pairs={{0,16},{8,24},{16,32},{24,40},{32,48},{40,56},{48,64},{56,72},{64,... | collective-permute-start | bytes 32 | tf_op jit(solution)/shard_map/ppermute | solution.py:19
  55.6 4.4 %collective-permute-done.16 = s32[2]{0:T(128)S(1)} collective-permute-done((s32[2]{0:T(128)S(1)}, s32[2]{0:T(128)S(1)}, u32[]{:S(2)}, u32[]{:S(2)}) %collective-permute-start.16) | collective-permute-done | bytes 40 | tf_op jit(solution)/shard_map/ppermute | solution.py:19
  62.0 2.4 %collective-permute-done.15 = s32[2]{0:T(128)S(1)} collective-permute-done((s32[2]{0:T(128)S(1)}, s32[2]{0:T(128)S(1)}, u32[]{:S(2)}, u32[]{:S(2)}) %collective-permute-start.15) | collective-permute-done | bytes 40 | tf_op jit(solution)/shard_map/ppermute | solution.py:19
  64.4 2.4 %collective-permute-start.14 = (s32[2]{0:T(128)S(1)}, s32[2]{0:T(128)S(1)}, u32[]{:S(2)}, u32[]{:S(2)}) collective-permute-start(s32[2]{0:T(128)S(1)} %get-tuple-element.188), channel_id=1, source_target_pairs={{8,0},{16,8},{24,16},{32,24},{40,32},{48,40},{56,48},{64,56},{72,6... | collective-permute-start | bytes 32 | tf_op jit(solution)/shard_map/ppermute | solution.py:19
  68.6 3.8 %collective-permute-start.13 = (s32[2]{0:T(128)S(1)}, s32[2]{0:T(128)S(1)}, u32[]{:S(2)}, u32[]{:S(2)}) collective-permute-start(s32[2]{0:T(128)S(1)} %get-tuple-element.189), channel_id=1, source_target_pairs={{16,0},{24,8},{32,16},{40,24},{48,32},{56,40},{64,48},{72,56},{80,... | collective-permute-start | bytes 32 | tf_op jit(solution)/shard_map/ppermute | solution.py:19
  72.4 3.9 %collective-permute-done.13 = s32[2]{0:T(128)S(1)} collective-permute-done((s32[2]{0:T(128)S(1)}, s32[2]{0:T(128)S(1)}, u32[]{:S(2)}, u32[]{:S(2)}) %collective-permute-start.13) | collective-permute-done | bytes 40 | tf_op jit(solution)/shard_map/ppermute | solution.py:19
  78.2 4.5 %collective-permute-done.12 = s32[2]{0:T(128)S(1)} collective-permute-done((s32[2]{0:T(128)S(1)}, s32[2]{0:T(128)S(1)}, u32[]{:S(2)}, u32[]{:S(2)}) %collective-permute-start.12) | collective-permute-done | bytes 40 | tf_op jit(solution)/shard_map/ppermute | solution.py:19
  86.7 6.6 %collective-permute-start.11 = (bf16[2,128,1024]{2,1,0:T(8,128)(2,1)}, bf16[2,128,1024]{2,1,0:T(8,128)(2,1)S(1)}, u32[]{:S(2)}, u32[]{:S(2)}) collective-permute-start(bf16[2,128,1024]{2,1,0:T(8,128)(2,1)} %bitcast.166), channel_id=1, source_target_pairs={{0,24},{8,32},{16,40},{24,48},{32,56},{40,64},{48,72},{56,80},{64,... | collective-permute-start | bytes 1572872 | tf_op jit(solution)/shard_map/ppermute | solution.py:19
  93.3 5.8 %collective-permute-start.10 = (bf16[2,128,1024]{2,1,0:T(8,128)(2,1)}, bf16[2,128,1024]{2,1,0:T(8,128)(2,1)S(1)}, u32[]{:S(2)}, u32[]{:S(2)}) collective-permute-start(bf16[2,128,1024]{2,1,0:T(8,128)(2,1)} %bitcast.165), channel_id=1, source_target_pairs={{0,16},{8,24},{16,32},{24,40},{32,48},{40,56},{48,64},{56,72},{64,... | collective-permute-start | bytes 1572872 | tf_op jit(solution)/shard_map/ppermute | solution.py:19
  99.1 1.9 %collective-permute-start.9 = (bf16[2,128,1024]{2,1,0:T(8,128)(2,1)}, bf16[2,128,1024]{2,1,0:T(8,128)(2,1)}, u32[]{:S(2)}, u32[]{:S(2)}) collective-permute-start(bf16[2,128,1024]{2,1,0:T(8,128)(2,1)} %bitcast.164), channel_id=1, source_target_pairs={{0,8},{8,16},{16,24},{24,32},{32,40},{40,48},{48,56},{56,64},{64,7... | collective-permute-start | bytes 1572872 | tf_op jit(solution)/shard_map/ppermute | solution.py:19
  101.1 18.2 %collective-permute-done.1 = bf16[2,128,1024]{2,1,0:T(8,128)(2,1)S(1)} collective-permute-done((bf16[2,128,1024]{2,1,0:T(8,128)(2,1)}, bf16[2,128,1024]{2,1,0:T(8,128)(2,1)S(1)}, u32[]{:S(2)}, u32[]{:S(2)}) %collective-permute-start.1) | collective-permute-done | bytes 524320 | tf_op jit(solution)/shard_map/ppermute | solution.py:19
  121.2 1.9 %collective-permute-start.7 = (bf16[2,128,1024]{2,1,0:T(8,128)(2,1)}, bf16[2,128,1024]{2,1,0:T(8,128)(2,1)}, u32[]{:S(2)}, u32[]{:S(2)}) collective-permute-start(bf16[2,128,1024]{2,1,0:T(8,128)(2,1)} %bitcast.162), channel_id=1, source_target_pairs={{16,0},{24,8},{32,16},{40,24},{48,32},{56,40},{64,48},{72,56},{80,... | collective-permute-start | bytes 1572872 | tf_op jit(solution)/shard_map/ppermute | solution.py:19
  123.1 2.2 %fusion.20 = bf16[2,128,1024]{2,1,0:T(8,128)(2,1)S(1)} fusion(bf16[2,128,1024]{2,1,0:T(8,128)(2,1)} %collective-permute-done.5, bf16[2,128,1024]{2,1,0:T(8,128)(2,1)} %collective-permute-done.4, bf16[2,128,1024]{2,1,0:T(8,128)(2,1)} %collective-permute-done.3, bf16[2,128,1024]{2,1,0:T(8,128)(2,1)} %collective-permute-done.2, ...), kind=kLoop, calls=%fused_computation.44 | loop fusion | flops 1572864 | bytes 4194304 | tf_op jit(solution)/shard_map/add | solution.py:63
  128.1 25.1 %all_gather.9 = f32[8,2,64]{2,1,0:T(2,128)S(1)} all-gather(f32[1,2,64]{2,1,0:T(2,128)S(1)} %all_gather_reshape.9), channel_id=1, replica_groups=mesh['dp'=64,'tensor'=8] {'tensor'}, dimensions={0}, use_global_device_ids=true | all-gather | bytes 4608 | tf_op jit(solution)/shard_map/all_gather | solution.py:23
  153.1 10.3 %all_gather.10 = f32[8,2,64]{2,1,0:T(2,128)S(1)} all-gather(f32[1,2,64]{2,1,0:T(2,128)S(1)} %all_gather_reshape.10), channel_id=1, replica_groups=mesh['dp'=64,'tensor'=8] {'tensor'}, dimensions={0}, use_global_device_ids=true | all-gather | bytes 4608 | tf_op jit(solution)/shard_map/all_gather | solution.py:23
  165.6 20.1 %all_gather.11 = f32[8,2,64,128]{3,2,1,0:T(8,128)S(1)} all-gather(f32[1,2,64,128]{3,2,1,0:T(8,128)S(1)} %convolution_bitcast_fusion), channel_id=1, replica_groups=mesh['dp'=64,'tensor'=8] {'tensor'}, dimensions={0}, use_global_device_ids=true | all-gather | bytes 589824 | tf_op jit(solution)/shard_map/all_gather | solution.py:23
  (101 shorter events, 34.9 us)
Async XLA Ops:
  11.4 18.0 %copy-start.10 = (s32[4]{0:T(128)S(1)}, s32[4]{0:T(128)}, u32[]{:S(2)}) copy-start(s32[4]{0:T(128)} %param.11) | copy-start | bytes 52
  11.4 24.8 %copy-start.6 = (bf16[4,128,1024]{2,1,0:T(8,128)(2,1)S(1)}, bf16[4,128,1024]{2,1,0:T(8,128)(2,1)}, u32[]{:S(2)}) copy-start(bf16[4,128,1024]{2,1,0:T(8,128)(2,1)} %param.10) | copy-start | bytes 3145732
  12.3 72.3 %collective-permute-start.5 = (bf16[2,128,1024]{2,1,0:T(8,128)(2,1)}, bf16[2,128,1024]{2,1,0:T(8,128)(2,1)}, u32[]{:S(2)}, u32[]{:S(2)}) collective-permute-start(bf16[2,128,1024]{2,1,0:T(8,128)(2,1)} %bitcast.150), channel_id=1, source_target_pairs={{0,24},{8,32},{16,40},{24,48},{32,56},{40,64},{48,72},{56,80},{64,... | collective-permute-start | bytes 1572872 | tf_op jit(solution)/shard_map/ppermute | solution.py:19
  18.0 68.7 %collective-permute-start.4 = (bf16[2,128,1024]{2,1,0:T(8,128)(2,1)}, bf16[2,128,1024]{2,1,0:T(8,128)(2,1)}, u32[]{:S(2)}, u32[]{:S(2)}) collective-permute-start(bf16[2,128,1024]{2,1,0:T(8,128)(2,1)} %bitcast.151), channel_id=1, source_target_pairs={{0,16},{8,24},{16,32},{24,40},{32,48},{40,56},{48,64},{56,72},{64,... | collective-permute-start | bytes 1572872 | tf_op jit(solution)/shard_map/ppermute | solution.py:19
  23.0 70.3 %collective-permute-start.3 = (bf16[2,128,1024]{2,1,0:T(8,128)(2,1)}, bf16[2,128,1024]{2,1,0:T(8,128)(2,1)}, u32[]{:S(2)}, u32[]{:S(2)}) collective-permute-start(bf16[2,128,1024]{2,1,0:T(8,128)(2,1)} %bitcast.152), channel_id=1, source_target_pairs={{0,8},{8,16},{16,24},{24,32},{32,40},{40,48},{48,56},{56,64},{64,7... | collective-permute-start | bytes 1572872 | tf_op jit(solution)/shard_map/ppermute | solution.py:19
  27.4 71.7 %collective-permute-start.2 = (bf16[2,128,1024]{2,1,0:T(8,128)(2,1)}, bf16[2,128,1024]{2,1,0:T(8,128)(2,1)}, u32[]{:S(2)}, u32[]{:S(2)}) collective-permute-start(bf16[2,128,1024]{2,1,0:T(8,128)(2,1)} %bitcast.153), channel_id=1, source_target_pairs={{8,0},{16,8},{24,16},{32,24},{40,32},{48,40},{56,48},{64,56},{72,6... | collective-permute-start | bytes 1572872 | tf_op jit(solution)/shard_map/ppermute | solution.py:19
  29.7 23.7 %collective-permute-start.17 = (s32[2]{0:T(128)S(1)}, s32[2]{0:T(128)S(1)}, u32[]{:S(2)}, u32[]{:S(2)}) collective-permute-start(s32[2]{0:T(128)S(1)} %get-tuple-element.185), channel_id=1, source_target_pairs={{0,24},{8,32},{16,40},{24,48},{32,56},{40,64},{48,72},{56,80},{64,... | collective-permute-start | bytes 32 | tf_op jit(solution)/shard_map/ppermute | solution.py:19
  37.9 7.1 %copy-start.11 = (bf16[2,8192]{1,0:T(2,128)(2,1)S(1)}, bf16[2,8192]{1,0:T(2,128)(2,1)}, u32[]{:S(2)}) copy-start(bf16[2,8192]{1,0:T(2,128)(2,1)} %param.13) | copy-start | bytes 98308
  52.1 111.3 %copy-start.4 = (bf16[1,2,128,1024]{3,0,2,1:T(2,128)(2,1)S(1)}, bf16[1,2,128,1024]{3,0,2,1:T(2,128)(2,1)}, u32[]{:S(2)}) copy-start(bf16[1,2,128,1024]{3,0,2,1:T(2,128)(2,1)} %get-tuple-element.212) | copy-start | bytes 1572868
  53.4 6.7 %collective-permute-start.16 = (s32[2]{0:T(128)S(1)}, s32[2]{0:T(128)S(1)}, u32[]{:S(2)}, u32[]{:S(2)}) collective-permute-start(s32[2]{0:T(128)S(1)} %get-tuple-element.186), channel_id=1, source_target_pairs={{0,16},{8,24},{16,32},{24,40},{32,48},{40,56},{48,64},{56,72},{64,... | collective-permute-start | bytes 32 | tf_op jit(solution)/shard_map/ppermute | solution.py:19
  60.1 4.3 %collective-permute-start.15 = (s32[2]{0:T(128)S(1)}, s32[2]{0:T(128)S(1)}, u32[]{:S(2)}, u32[]{:S(2)}) collective-permute-start(s32[2]{0:T(128)S(1)} %get-tuple-element.187), channel_id=1, source_target_pairs={{0,8},{8,16},{16,24},{24,32},{32,40},{40,48},{48,56},{56,64},{64,7... | collective-permute-start | bytes 32 | tf_op jit(solution)/shard_map/ppermute | solution.py:19
  64.4 4.3 %collective-permute-start.14 = (s32[2]{0:T(128)S(1)}, s32[2]{0:T(128)S(1)}, u32[]{:S(2)}, u32[]{:S(2)}) collective-permute-start(s32[2]{0:T(128)S(1)} %get-tuple-element.188), channel_id=1, source_target_pairs={{8,0},{16,8},{24,16},{32,24},{40,32},{48,40},{56,48},{64,56},{72,6... | collective-permute-start | bytes 32 | tf_op jit(solution)/shard_map/ppermute | solution.py:19
  68.6 7.7 %collective-permute-start.13 = (s32[2]{0:T(128)S(1)}, s32[2]{0:T(128)S(1)}, u32[]{:S(2)}, u32[]{:S(2)}) collective-permute-start(s32[2]{0:T(128)S(1)} %get-tuple-element.189), channel_id=1, source_target_pairs={{16,0},{24,8},{32,16},{40,24},{48,32},{56,40},{64,48},{72,56},{80,... | collective-permute-start | bytes 32 | tf_op jit(solution)/shard_map/ppermute | solution.py:19
  76.3 6.4 %collective-permute-start.12 = (s32[2]{0:T(128)S(1)}, s32[2]{0:T(128)S(1)}, u32[]{:S(2)}, u32[]{:S(2)}) collective-permute-start(s32[2]{0:T(128)S(1)} %get-tuple-element.184), channel_id=1, source_target_pairs={{24,0},{32,8},{40,16},{48,24},{56,32},{64,40},{72,48},{80,56},{88,... | collective-permute-start | bytes 32 | tf_op jit(solution)/shard_map/ppermute | solution.py:19
  82.7 36.5 %collective-permute-start.1 = (bf16[2,128,1024]{2,1,0:T(8,128)(2,1)}, bf16[2,128,1024]{2,1,0:T(8,128)(2,1)S(1)}, u32[]{:S(2)}, u32[]{:S(2)}) collective-permute-start(bf16[2,128,1024]{2,1,0:T(8,128)(2,1)} %bitcast.168), channel_id=1, source_target_pairs={{16,0},{24,8},{32,16},{40,24},{48,32},{56,40},{64,48},{72,56},{80,... | collective-permute-start | bytes 1572872 | tf_op jit(solution)/shard_map/ppermute | solution.py:19
  84.6 36.5 %collective-permute-start = (bf16[2,128,1024]{2,1,0:T(8,128)(2,1)}, bf16[2,128,1024]{2,1,0:T(8,128)(2,1)S(1)}, u32[]{:S(2)}, u32[]{:S(2)}) collective-permute-start(bf16[2,128,1024]{2,1,0:T(8,128)(2,1)} %bitcast.167), channel_id=1, source_target_pairs={{24,0},{32,8},{40,16},{48,24},{56,32},{64,40},{72,48},{80,56},{88,... | collective-permute-start | bytes 1572872 | tf_op jit(solution)/shard_map/ppermute | solution.py:19
  86.7 39.2 %collective-permute-start.11 = (bf16[2,128,1024]{2,1,0:T(8,128)(2,1)}, bf16[2,128,1024]{2,1,0:T(8,128)(2,1)S(1)}, u32[]{:S(2)}, u32[]{:S(2)}) collective-permute-start(bf16[2,128,1024]{2,1,0:T(8,128)(2,1)} %bitcast.166), channel_id=1, source_target_pairs={{0,24},{8,32},{16,40},{24,48},{32,56},{40,64},{48,72},{56,80},{64,... | collective-permute-start | bytes 1572872 | tf_op jit(solution)/shard_map/ppermute | solution.py:19
  93.3 70.1 %collective-permute-start.10 = (bf16[2,128,1024]{2,1,0:T(8,128)(2,1)}, bf16[2,128,1024]{2,1,0:T(8,128)(2,1)S(1)}, u32[]{:S(2)}, u32[]{:S(2)}) collective-permute-start(bf16[2,128,1024]{2,1,0:T(8,128)(2,1)} %bitcast.165), channel_id=1, source_target_pairs={{0,16},{8,24},{16,32},{24,40},{32,48},{40,56},{48,64},{56,72},{64,... | collective-permute-start | bytes 1572872 | tf_op jit(solution)/shard_map/ppermute | solution.py:19
  99.1 64.3 %collective-permute-start.9 = (bf16[2,128,1024]{2,1,0:T(8,128)(2,1)}, bf16[2,128,1024]{2,1,0:T(8,128)(2,1)}, u32[]{:S(2)}, u32[]{:S(2)}) collective-permute-start(bf16[2,128,1024]{2,1,0:T(8,128)(2,1)} %bitcast.164), channel_id=1, source_target_pairs={{0,8},{8,16},{16,24},{24,32},{32,40},{40,48},{48,56},{56,64},{64,7... | collective-permute-start | bytes 1572872 | tf_op jit(solution)/shard_map/ppermute | solution.py:19
  119.2 44.2 %collective-permute-start.8 = (bf16[2,128,1024]{2,1,0:T(8,128)(2,1)}, bf16[2,128,1024]{2,1,0:T(8,128)(2,1)}, u32[]{:S(2)}, u32[]{:S(2)}) collective-permute-start(bf16[2,128,1024]{2,1,0:T(8,128)(2,1)} %bitcast.163), channel_id=1, source_target_pairs={{8,0},{16,8},{24,16},{32,24},{40,32},{48,40},{56,48},{64,56},{72,6... | collective-permute-start | bytes 1572872 | tf_op jit(solution)/shard_map/ppermute | solution.py:19
  121.2 42.3 %collective-permute-start.7 = (bf16[2,128,1024]{2,1,0:T(8,128)(2,1)}, bf16[2,128,1024]{2,1,0:T(8,128)(2,1)}, u32[]{:S(2)}, u32[]{:S(2)}) collective-permute-start(bf16[2,128,1024]{2,1,0:T(8,128)(2,1)} %bitcast.162), channel_id=1, source_target_pairs={{16,0},{24,8},{32,16},{40,24},{48,32},{56,40},{64,48},{72,56},{80,... | collective-permute-start | bytes 1572872 | tf_op jit(solution)/shard_map/ppermute | solution.py:19
  125.3 61.6 %copy-start.7 = (bf16[2,128,1024]{2,1,0:T(8,128)(2,1)}, bf16[2,128,1024]{2,1,0:T(8,128)(2,1)S(1)}, u32[]{:S(2)}) copy-start(bf16[2,128,1024]{2,1,0:T(8,128)(2,1)S(1)} %fusion.20) | copy-start | bytes 1572868
  125.9 37.6 %collective-permute-start.6 = (bf16[2,128,1024]{2,1,0:T(8,128)(2,1)S(1)}, bf16[2,128,1024]{2,1,0:T(8,128)(2,1)}, u32[]{:S(2)}, u32[]{:S(2)}) collective-permute-start(bf16[2,128,1024]{2,1,0:T(8,128)(2,1)S(1)} %bitcast.161), channel_id=1, source_target_pairs={{24,0},{32,8},{40,16},{48,24},{56,32},{64,40},{72,48},{80,56},{88,... | collective-permute-start | bytes 1572872 | tf_op jit(solution)/shard_map/ppermute | solution.py:19
  165.3 22.5 %copy-start.5 = (bf16[2,128,1024]{2,1,0:T(8,128)(2,1)}, bf16[2,128,1024]{2,1,0:T(8,128)(2,1)S(1)}, u32[]{:S(2)}) copy-start(bf16[2,128,1024]{2,1,0:T(8,128)(2,1)S(1)} %fusion.15) | copy-start | bytes 1572868
  (6 other events, 33.0 us)
where the time goes:
time: 189 us; the launch traced here: 188 us
  starting transfers between devices  56.7 us (30%)
  blocking collectives  55.4 us (29%)
  waiting for transfers between devices  35.3 us (19%)
  local copies, waits for them, and re-layouts  26.3 us (14%)
  other arithmetic  7.67 us (4%)
  matrix products  5.26 us (3%)
    ppermute x18, starting transfers between devices, passed_along(): return lax.ppermute(block, axis, route)  56.7 us
    all_gather x3, blocking collectives, combined_all(): everything = jax.tree.map(lambda part: lax.all_gather(part, axis), x)  55.4 us
    ppermute x18, waiting for transfers between devices, passed_along(): return lax.ppermute(block, axis, route)  35.3 us
    unnamed x39, local copies, waits for them, and re-layouts  12.1 us
    slice x1, local copies, waits for them, and re-layouts, migrate_direct(): moved_values = values_out[GROUP - 1]  7.06 us
    slice x1, local copies, waits for them, and re-layouts, migrate_direct(): moved_keys = keys_out[GROUP - 1]  6.55 us
  transfers between devices with their start and end apart: 18, of which 6 were waited for; matrix products, arithmetic and copies ran while one was open for 12% of the time, Pallas kernels for 0%

commit v1 on v0

v1 whole, which is shorter than its diff:
```python
import functools

import jax
import jax.numpy as jnp
from jax import lax
from jax.experimental import pallas as pl
from jax.experimental.pallas import tpu as pltpu
from jax.sharding import Mesh
from jax.sharding import PartitionSpec as P

QH = 64
KVH = 8
HD = 128
SLOTS = 4
ROWS = 2
GROUP = 4
PER = QH // KVH
TENSOR = 8
SPAN = 128
WIDE = KVH * HD
SCALE = HD ** -0.5
FLOOR = -1e30

STAT = ROWS * QH
CHUNK = STAT + QH
ASK = ROWS * QH + 16

EDGE_A = ((0, 1), (1, 0), (2, 3), (3, 2))
EDGE_B = ((1, 2), (2, 1))
EDGE_C = ((1, 3), (2, 0))
RELAY = ((0, 3), (3, 0))

SMEM = pl.BlockSpec(memory_space=pltpu.SMEM)
VMEM = pl.BlockSpec(memory_space=pltpu.VMEM)
ANY = pl.BlockSpec(memory_space=pl.ANY)


def places(dest_ref, slot, first):
    local = dest_ref[slot] - first
    live = dest_ref[slot] >= 0
    return jnp.where(live, lax.shift_right_arithmetic(local, 1), -1), lax.bitwise_and(local, 1)


def copy_all(pairs):
    for guard, copies in pairs:
        @pl.when(guard)
        def _():
            for copy in copies:
                copy.start()
    for guard, copies in pairs:
        @pl.when(guard)
        def _():
            for copy in copies:
                copy.wait()


def send_kernel(wanted, meta_ref, dest_ref, keys_ref, values_ref, *rest):
    outs, sem = rest[:-1], rest[-1]
    z, x = meta_ref[0], meta_ref[1]
    first = z * (GROUP * ROWS)
    pairs = []
    for slot in range(SLOTS):
        host, row = places(dest_ref, slot, first)
        live = host >= 0
        edge = lax.bitwise_xor(host, x)
        for index, (out, (rows, edges)) in enumerate(zip(outs, wanted)):
            guard = edge == edges[0]
            for other in edges[1:]:
                guard = guard | (edge == other)
            guard = guard & live
            if len(rows) == 1:
                guard = guard & (row == rows[0])
                base = 0
            else:
                base = row * 2
            pairs.append((guard, [
                pltpu.make_async_copy(keys_ref.at[slot], out.at[base], sem.at[index, slot, 0]),
                pltpu.make_async_copy(values_ref.at[slot], out.at[base + 1], sem.at[index, slot, 1]),
            ]))
    copy_all(pairs)


def send_buffers(meta, destination, keys, values, wanted):
    return pl.pallas_call(
        functools.partial(send_kernel, wanted),
        out_shape=[jax.ShapeDtypeStruct((2 * len(rows), SPAN, WIDE), jnp.bfloat16) for rows, _ in wanted],
        in_specs=[SMEM, SMEM, ANY, ANY],
        out_specs=[ANY] * len(wanted),
        scratch_shapes=[pltpu.SemaphoreType.DMA((len(wanted), SLOTS, 2))],
        cost_estimate=pl.CostEstimate(flops=0, bytes_accessed=2 * 2**20, transcendentals=0),
    )(meta, destination, keys, values)


def split_three(x):
    high = x.astype(jnp.bfloat16)
    rest = x - high.astype(jnp.float32)
    middle = rest.astype(jnp.bfloat16)
    low = (rest - middle.astype(jnp.float32)).astype(jnp.bfloat16)
    return high.astype(jnp.float32), middle.astype(jnp.float32), low.astype(jnp.float32)


def attend_kernel(meta_ref, dest_ref, length_ref, asked_ref, keys_ref, values_ref, out_ref, keys, values, sem):
    z, x, t = meta_ref[0], meta_ref[1], meta_ref[2]
    first = z * (GROUP * ROWS)
    copies = []
    for slot in range(SLOTS):
        copies.append(pltpu.make_async_copy(keys_ref.at[slot], keys.at[slot], sem.at[0, slot]))
        copies.append(pltpu.make_async_copy(values_ref.at[slot], values.at[slot], sem.at[1, slot]))
    for copy in copies:
        copy.start()
    out_ref[...] = jnp.zeros(out_ref.shape, out_ref.dtype)
    head = lax.broadcasted_iota(jnp.int32, (QH, WIDE), 0)
    lane = lax.broadcasted_iota(jnp.int32, (QH, WIDE), 1)
    diagonal = (head // PER) == (lane // HD)
    position = t * SPAN + lax.broadcasted_iota(jnp.int32, (QH, SPAN), 1)
    column = lax.broadcasted_iota(jnp.int32, (QH, HD), 1)
    for copy in copies:
        copy.wait()
    results = []
    for slot in range(SLOTS):
        host, row = places(dest_ref, slot, first)
        at = pl.multiple_of(jnp.maximum(row, 0) * QH, QH)
        safe = jnp.clip(host, 0, GROUP - 1)
        query = asked_ref[safe, pl.ds(at, QH), :]
        spread = jnp.where(diagonal, jnp.concatenate([query] * KVH, axis=1), jnp.zeros((), jnp.bfloat16))
        scores = lax.dot_general(
            spread, keys[slot], (((1,), (1,)), ((), ())), preferred_element_type=jnp.float32
        ) * SCALE
        valid = position < length_ref[slot]
        peak = jnp.max(jnp.where(valid, scores, FLOOR), axis=1, keepdims=True)
        weights = jnp.where(valid, jnp.exp(scores - peak), 0.0).astype(jnp.bfloat16)
        mass = jnp.sum(weights.astype(jnp.float32), axis=1, keepdims=True)
        full = jnp.dot(weights, values[slot], preferred_element_type=jnp.float32)
        partial = jnp.concatenate(
            [full[g * PER:(g + 1) * PER, g * HD:(g + 1) * HD] for g in range(KVH)], axis=0
        ).astype(jnp.bfloat16)
        stats = jnp.zeros((QH, HD), jnp.float32)
        for k, piece in enumerate(split_three(peak) + split_three(mass)):
            stats = jnp.where(column == row * 8 + k, piece, stats)
        results.append((host, safe, row, at, partial, stats.astype(jnp.bfloat16)))
    for host, safe, row, at, partial, stats in results:
        @pl.when(host >= 0)
        def _(safe=safe, row=row, at=at, partial=partial, stats=stats):
            out_ref[safe, pl.ds(at, QH), :] = partial
            held = out_ref[safe, STAT:CHUNK, :]
            mine = (column >= row * 8) & (column < row * 8 + 8)
            out_ref[safe, STAT:CHUNK, :] = jnp.where(mine, stats, held)


def attend(meta, destination, lengths, asked, keys, values):
    return pl.pallas_call(
        attend_kernel,
        out_shape=jax.ShapeDtypeStruct((GROUP, CHUNK, HD), jnp.bfloat16),
        in_specs=[SMEM, SMEM, SMEM, VMEM, ANY, ANY],
        out_specs=VMEM,
        scratch_shapes=[
            pltpu.VMEM((SLOTS, SPAN, WIDE), jnp.bfloat16),
            pltpu.VMEM((SLOTS, SPAN, WIDE), jnp.bfloat16),
            pltpu.SemaphoreType.DMA((2, SLOTS)),
        ],
        compiler_params=pltpu.CompilerParams(vmem_limit_bytes=16 * 2**20),
        cost_estimate=pl.CostEstimate(flops=2**27, bytes_accessed=2 * 2**20, transcendentals=2**15),
    )(meta, destination, lengths, asked, keys, values)


def origin(group_ref, wanted):
    replica, slot = jnp.int32(0), jnp.int32(0)
    for s in range(GROUP):
        for k in range(SLOTS):
            hit = group_ref[s * SLOTS + k] == wanted
            replica = jnp.where(hit, s, replica)
            slot = jnp.where(hit, k, slot)
    return replica, slot


def pick_kernel(meta_ref, group_ref, got_ref, out_ref):
    z, x = meta_ref[0], meta_ref[1]
    base = z * (GROUP * ROWS) + x * ROWS
    column = lax.broadcasted_iota(jnp.int32, (QH, HD), 1)
    sources = [origin(group_ref, base + row)[0] for row in range(ROWS)]
    for row, source in enumerate(sources):
        out_ref[row * QH:(row + 1) * QH, :] = got_ref[source, row * QH:(row + 1) * QH, :]
    out_ref[STAT:CHUNK, :] = jnp.where(
        column < 8, got_ref[sources[0], STAT:CHUNK, :], got_ref[sources[1], STAT:CHUNK, :]
    )


def pick(meta, group, got):
    return pl.pallas_call(
        pick_kernel,
        out_shape=jax.ShapeDtypeStruct((CHUNK, HD), jnp.bfloat16),
        in_specs=[SMEM, SMEM, VMEM],
        out_specs=VMEM,
    )(meta, group, got)


def finish_kernel(blocks_ref, queries_ref, new_keys_ref, new_values_ref, out_ref):
    for row in range(ROWS):
        def per_head(ref):
            block = ref[row].astype(jnp.float32)
            return jnp.concatenate(
                [jnp.broadcast_to(block[g:g + 1, :], (PER, HD)) for g in range(KVH)], axis=0
            )

        query = queries_ref[row].astype(jnp.float32)
        own = jnp.sum(query * per_head(new_keys_ref), axis=1, keepdims=True) * SCALE
        peaks, masses = [], []
        for b in range(TENSOR):
            stats = blocks_ref[b, STAT:CHUNK, :].astype(jnp.float32)
            piece = [stats[:, row * 8 + k:row * 8 + k + 1] for k in range(6)]
            peaks.append((piece[0] + piece[1]) + piece[2])
            masses.append((piece[3] + piece[4]) + piece[5])
        top = functools.reduce(jnp.maximum, peaks, own)
        own_weight = jnp.exp(own - top)
        denominator = own_weight
        numerator = own_weight * per_head(new_values_ref)
        for b in range(TENSOR):
            fade = jnp.exp(peaks[b] - top)
            denominator = denominator + fade * masses[b]
            numerator = numerator + fade * blocks_ref[b, row * QH:(row + 1) * QH, :].astype(jnp.float32)
        out_ref[row] = (numerator / denominator).astype(jnp.bfloat16)


def finish(blocks, queries, new_keys, new_values):
    return pl.pallas_call(
        finish_kernel,
        out_shape=jax.ShapeDtypeStruct((ROWS, QH, HD), jnp.bfloat16),
        in_specs=[VMEM] * 4,
        out_specs=VMEM,
    )(blocks, queries, new_keys, new_values)


def place_kernel(meta_ref, group_ref, keys_ref, values_ref, a0_ref, a1_ref, b_ref, c0_ref, c1_ref,
                 moved_keys_ref, moved_values_ref, sem):
    z, x = meta_ref[0], meta_ref[1]
    base = z * (GROUP * ROWS) + x * ROWS
    pairs = []
    for row in range(ROWS):
        replica, slot = origin(group_ref, base + row)
        edge = lax.bitwise_xor(replica, x)
        out_keys, out_values = moved_keys_ref.at[row], moved_values_ref.at[row]
        near = (a0_ref, a1_ref)[row]
        far = (c0_ref, c1_ref)[row]
        for which, key_block, value_block in (
            (0, keys_ref.at[slot], values_ref.at[slot]),
            (1, near.at[0], near.at[1]),
            (3, b_ref.at[2 * row], b_ref.at[2 * row + 1]),
            (2, far.at[0], far.at[1]),
        ):
            pairs.append((edge == which, [
                pltpu.make_async_copy(key_block, out_keys, sem.at[row, which, 0]),
                pltpu.make_async_copy(value_block, out_values, sem.at[row, which, 1]),
            ]))
    copy_all(pairs)


def place(meta, group, keys, values, a0, a1, b, c0, c1):
    moved = jax.ShapeDtypeStruct((ROWS, SPAN, WIDE), jnp.bfloat16)
    return pl.pallas_call(
        place_kernel,
        out_shape=[moved, moved],
        in_specs=[SMEM, SMEM] + [ANY] * 7,
        out_specs=[ANY, ANY],
        scratch_shapes=[pltpu.SemaphoreType.DMA((ROWS, 4, 2))],
        cost_estimate=pl.CostEstimate(flops=0, bytes_accessed=2 * 2**20, transcendentals=0),
    )(meta, group, keys, values, a0, a1, b, c0, c1)


def on_device(keys, values, lengths, destination, queries, new_keys, new_values):
    z, x, t = (lax.axis_index(name) for name in ("z", "x", "t"))
    meta = jnp.stack([z, x, t]).astype(jnp.int32)
    first = z * (GROUP * ROWS)
    a1, b = send_buffers(meta, destination, keys, values, (((1,), (1, 2)), ((0, 1), (3,))))
    a0, c0 = send_buffers(meta, destination, keys, values, (((0,), (1,)), ((0,), (2,))))
    a1 = lax.ppermute(a1, "x", EDGE_A)
    b = lax.ppermute(b, "x", EDGE_B)
    c0 = lax.ppermute(c0, "x", EDGE_C)
    a0 = lax.ppermute(a0, "x", EDGE_A)
    c1 = lax.ppermute(a1, "x", RELAY)

    own_queries = queries.reshape(ROWS * QH, HD)
    told = jnp.where(destination >= 0, destination - first, -1).astype(jnp.bfloat16)
    told = jnp.pad(told[None, :], ((0, 15), (0, HD - SLOTS)))
    asked = lax.all_gather(jnp.concatenate([own_queries, told], axis=0), "x")
    group = asked[:, ROWS * QH, :SLOTS].astype(jnp.int32).reshape(GROUP * SLOTS)
    group = jnp.where(group >= 0, group + first, -1)
    sent = attend(meta, destination, lengths, asked, keys, values)
    got = lax.all_to_all(sent, "x", 0, 0)
    mine = pick(meta, group, got)
    blocks = lax.all_gather(mine, "t")
    attended = finish(
        blocks,
        own_queries.reshape(ROWS, QH, HD),
        new_keys.reshape(ROWS, KVH, HD),
        new_values.reshape(ROWS, KVH, HD),
    )
    moved_keys, moved_values = place(meta, group, keys, values, a0, a1, b, c0, c1)
    return moved_keys, moved_values, attended.reshape(ROWS, QH * HD)


def solution(mesh):
    groups = Mesh(mesh.devices.reshape(-1, GROUP, TENSOR), ("z", "x", "t"))
    dp = ("z", "x")
    return jax.shard_map(
        on_device,
        mesh=groups,
        in_specs=(P(dp, "t", None), P(dp, "t", None), P(dp), P(dp), P(dp, None), P(dp, None), P(dp, None)),
        out_specs=(P(dp, "t", None), P(dp, "t", None), P(dp, None)),
        check_vma=False,
    )
```

time: 189 us -> 185 us (0.979)
  the two profiles are of different devices: /device:TPU:235 before, /device:TPU:1 now
where the time goes in v1:
time: 185 us
  starting transfers between devices  81.3 us (44%)
  blocking collectives  49.7 us (27%)
  Pallas kernels  42.7 us (23%)
  local copies, waits for them, and re-layouts  6.27 us (3%)
  waiting for transfers between devices  3.22 us (2%)
    ppermute x1, starting transfers between devices, on_device(): a0 = lax.ppermute(a0, 'x', EDGE_A)  69.9 us
    pallas_call x1, Pallas kernels, place(): pl.pallas_call(place_kernel, out_shape=[moved, moved], in_specs=[SMEM, SM...  33.7 us
    all_gather x1, blocking collectives, on_device(): asked = lax.all_gather(jnp.concatenate([own_queries, told], axis=0), 'x')  30 us
    all_gather x1, blocking collectives, on_device(): blocks = lax.all_gather(mine, 't')  19.7 us
    unnamed x22, local copies, waits for them, and re-layouts  5.01 us
    ppermute x1, starting transfers between devices, on_device(): a1 = lax.ppermute(a1, 'x', EDGE_A)  3.95 us
  transfers between devices with their start and end apart: 6, of which 1 were waited for; matrix products, arithmetic and copies ran while one was open for 2% of the time, Pallas kernels for 4%

profile of v1, /device:TPU:1, one launch (start us, length us, event | category | flops | bytes accessed | tf_op | source)
XLA Modules:
  0.0 184.7 jit_solution(10687015702809977240)
XLA Ops:
  0.6 0.6 pad_add_fusion.meta_ref
  1.2 0.9 shard_map.95
  2.1 4.0 %collective-permute-start.1 = (bf16[2,128,1024]{2,1,0:T(8,128)(2,1)}, bf16[2,128,1024]{2,1,0:T(8,128)(2,1)}, u32[]{:S(2)}, u32[]{:S(2)}) collective-permute-start(bf16[2,128,1024]{2,1,0:T(8,128)(2,1)} %get-tuple-element.10), channel_id=1, source_target_pairs={{0,8},{8,0},{16,24},{24,16},{1,9},{9,1},{17,25},{25,17},{2,10},{10... | collective-permute-start | bytes 1572872 | tf_op jit(solution)/shard_map/ppermute | solution.py:275
  6.1 0.9 collective-permute-start.2
  7.0 0.9 shard_map.94
  7.9 69.9 %collective-permute-start = (bf16[2,128,1024]{2,1,0:T(8,128)(2,1)}, bf16[2,128,1024]{2,1,0:T(8,128)(2,1)}, u32[]{:S(2)}, u32[]{:S(2)}) collective-permute-start(bf16[2,128,1024]{2,1,0:T(8,128)(2,1)} %get-tuple-element.9), channel_id=1, source_target_pairs={{0,8},{8,0},{16,24},{24,16},{1,9},{9,1},{17,25},{25,17},{2,10},{10... | collective-permute-start | bytes 1572872 | tf_op jit(solution)/shard_map/ppermute | solution.py:278
  77.8 1.3 collective-permute-start.3
  79.2 0.6 copy-done.3
  79.8 1.9 %collective-permute-start.4 = (bf16[2,128,1024]{2,1,0:T(8,128)(2,1)}, bf16[2,128,1024]{2,1,0:T(8,128)(2,1)}, u32[]{:S(2)}, u32[]{:S(2)}) collective-permute-start(bf16[2,128,1024]{2,1,0:T(8,128)(2,1)} %collective-permute-done.1.a1_ref), channel_id=1, source_target_pairs={{0,24},{24,0},{1,25},{25,1},{2,26},{26,2},{3,27},{27,3},{4,28},{28... | collective-permute-start | bytes 1572872 | tf_op jit(solution)/shard_map/ppermute | solution.py:279
  81.8 30.0 %all-gather = bf16[576,128]{1,0:T(8,128)(2,1)S(1)} all-gather(bf16[144,128]{1,0:T(8,128)(2,1)S(1)} %fusion.1), channel_id=2, replica_groups=mesh['z'=16,'x'=4,'t'=8] {'x'}, dimensions={0}, use_global_device_ids=true | all-gather | bytes 184320 | tf_op jit(solution)/shard_map/all_gather | solution.py:284
  111.7 0.6 copy-done.2
  112.4 3.2 %shard_map.97 = bf16[4,192,128]{2,1,0:T(8,128)(2,1)} custom-call(s32[3]{0:T(128)S(1)} %copy-done.2, s32[4]{0:T(128)S(1)} %copy-done.3, s32[4]{0:T(128)S(1)} %copy-done.4, bf16[4,144,128]{2,1,0:T(8,128)(2,1)S(1)} %bitcast.21, bf16[4,128,1024]{2,1,0:T(8,128)(2,1)S(1)} %copy-done, bf16[4,128,1024]{2,1,0:T(8,128)(2,1)S(1)} %copy-done.1), custom_call_target="tpu_custom_call" | custom-call | flops 134217728 | bytes 2097152 | tf_op jit(solution)/shard_map/pallas_call | solution.py:151
  115.6 3.4 %all-to-all-start = ((bf16[4,192,128]{2,1,0:T(8,128)(2,1)}), bf16[4,192,128]{2,1,0:T(8,128)(2,1)S(1)}, u32[]{:S(2)}, u32[]{:S(2)}) async-start(bf16[4,192,128]{2,1,0:T(8,128)(2,1)} %shard_map.97), calls=%async_computation | async-start | bytes 393216 | tf_op jit(solution)/shard_map/all_to_all | solution.py:288
  119.0 0.6 copy.19
  119.7 0.6 select_n.12.group_ref
  120.3 0.6 copy_bitcast_fusion.2
  120.9 3.2 %all-to-all-done.got_ref = bf16[4,192,128]{2,1,0:T(8,128)(2,1)S(1)} async-done(((bf16[4,192,128]{2,1,0:T(8,128)(2,1)}), bf16[4,192,128]{2,1,0:T(8,128)(2,1)S(1)}, u32[]{:S(2)}, u32[]{:S(2)}) %all-to-all-start) | async-done | bytes 196640 | tf_op jit(solution)/shard_map/all_to_all | solution.py:288
  124.1 0.7 copy-done.6
  124.8 1.6 shard_map.98
  126.4 19.7 %all-gather.1 = bf16[1536,128]{1,0:T(8,128)(2,1)} all-gather(bf16[192,128]{1,0:T(8,128)(2,1)} %shard_map.98), channel_id=3, replica_groups=mesh['z'=16,'x'=4,'t'=8] {'t'}, dimensions={0}, use_global_device_ids=true | all-gather | bytes 442368 | tf_op jit(solution)/shard_map/all_gather | solution.py:290
  146.1 2.4 %shard_map.99 = bf16[2,64,128]{2,1,0:T(8,128)(2,1)} custom-call(bf16[8,192,128]{2,1,0:T(8,128)(2,1)} %bitcast.23, bf16[2,64,128]{2,1,0:T(8,128)(2,1)} %bitcast.24, bf16[2,8,128]{2,1,0:T(8,128)(2,1)} %get-tuple-element.16.new_keys_ref, bf16[2,8,128]{2,1,0:T(8,128)(2,1)} %get-tuple-element.15.new_values_ref), custom_call_target="tpu_custom_call" | custom-call | tf_op jit(solution)/shard_map/pallas_call | solution.py:225
  148.6 1.4 copy.18
  150.0 1.0 copy-done.5
  151.0 33.7 %shard_map.96 = (bf16[2,128,1024]{2,1,0:T(8,128)(2,1)}, bf16[2,128,1024]{2,1,0:T(8,128)(2,1)}) custom-call(s32[3]{0:T(128)} %pad_add_fusion.meta_ref, s32[16]{0:T(128)} %select_n.12.group_ref, bf16[4,128,1024]{2,1,0:T(8,128)(2,1)} %keys_ref.7, bf16[4,128,1024]{2,1,0:T(8,128)(2,1)} %values_ref.7, bf16[2,128,1024]{2,1,0:T(8,128)(2,1)} %collective-permute-done.a0_ref, ...), custom_call_target="tpu_custom_call" | custom-call | bytes 2097152 | tf_op jit(solution)/shard_map/pallas_call | solution.py:259
  (25 shorter events, 0.2 us)
Async XLA Ops:
  2.1 77.7 %collective-permute-start.1 = (bf16[2,128,1024]{2,1,0:T(8,128)(2,1)}, bf16[2,128,1024]{2,1,0:T(8,128)(2,1)}, u32[]{:S(2)}, u32[]{:S(2)}) collective-permute-start(bf16[2,128,1024]{2,1,0:T(8,128)(2,1)} %get-tuple-element.10), channel_id=1, source_target_pairs={{0,8},{8,0},{16,24},{24,16},{1,9},{9,1},{17,25},{25,17},{2,10},{10... | collective-permute-start | bytes 1572872 | tf_op jit(solution)/shard_map/ppermute | solution.py:275
  6.1 73.0 %copy-start.7 = (bf16[2,8192]{1,0:T(2,128)(2,1)S(1)}, bf16[2,8192]{1,0:T(2,128)(2,1)}, u32[]{:S(2)}) copy-start(bf16[2,8192]{1,0:T(2,128)(2,1)} %param.11) | copy-start | bytes 98308
  6.1 105.6 %copy-start = (bf16[4,128,1024]{2,1,0:T(8,128)(2,1)S(1)}, bf16[4,128,1024]{2,1,0:T(8,128)(2,1)}, u32[]{:S(2)}) copy-start(bf16[4,128,1024]{2,1,0:T(8,128)(2,1)} %keys_ref.7) | copy-start | bytes 3145732
  6.1 105.6 %copy-start.1 = (bf16[4,128,1024]{2,1,0:T(8,128)(2,1)S(1)}, bf16[4,128,1024]{2,1,0:T(8,128)(2,1)}, u32[]{:S(2)}) copy-start(bf16[4,128,1024]{2,1,0:T(8,128)(2,1)} %values_ref.7) | copy-start | bytes 3145732
  6.1 143.9 %collective-permute-start.2 = (bf16[4,128,1024]{2,1,0:T(8,128)(2,1)}, bf16[4,128,1024]{2,1,0:T(8,128)(2,1)S(1)}, u32[]{:S(2)}, u32[]{:S(2)}) collective-permute-start(bf16[4,128,1024]{2,1,0:T(8,128)(2,1)} %get-tuple-element.11), channel_id=1, source_target_pairs={{8,16},{16,8},{9,17},{17,9},{10,18},{18,10},{11,19},{19,11},{12,20... | collective-permute-start | bytes 3145736 | tf_op jit(solution)/shard_map/ppermute | solution.py:276
  7.9 142.1 %collective-permute-start = (bf16[2,128,1024]{2,1,0:T(8,128)(2,1)}, bf16[2,128,1024]{2,1,0:T(8,128)(2,1)}, u32[]{:S(2)}, u32[]{:S(2)}) collective-permute-start(bf16[2,128,1024]{2,1,0:T(8,128)(2,1)} %get-tuple-element.9), channel_id=1, source_target_pairs={{0,8},{8,0},{16,24},{24,16},{1,9},{9,1},{17,25},{25,17},{2,10},{10... | collective-permute-start | bytes 1572872 | tf_op jit(solution)/shard_map/ppermute | solution.py:278
  77.8 72.2 %collective-permute-start.3 = (bf16[2,128,1024]{2,1,0:T(8,128)(2,1)}, bf16[2,128,1024]{2,1,0:T(8,128)(2,1)}, u32[]{:S(2)}, u32[]{:S(2)}) collective-permute-start(bf16[2,128,1024]{2,1,0:T(8,128)(2,1)} %get-tuple-element.12), channel_id=1, source_target_pairs={{8,24},{16,0},{9,25},{17,1},{10,26},{18,2},{11,27},{19,3},{12,28},... | collective-permute-start | bytes 1572872 | tf_op jit(solution)/shard_map/ppermute | solution.py:277
  79.1 0.7 copy-start.3
  79.8 70.2 %collective-permute-start.4 = (bf16[2,128,1024]{2,1,0:T(8,128)(2,1)}, bf16[2,128,1024]{2,1,0:T(8,128)(2,1)}, u32[]{:S(2)}, u32[]{:S(2)}) collective-permute-start(bf16[2,128,1024]{2,1,0:T(8,128)(2,1)} %collective-permute-done.1.a1_ref), channel_id=1, source_target_pairs={{0,24},{24,0},{1,25},{25,1},{2,26},{26,2},{3,27},{27,3},{4,28},{28... | collective-permute-start | bytes 1572872 | tf_op jit(solution)/shard_map/ppermute | solution.py:279
  111.7 0.6 copy-start.2
  111.7 0.7 copy-start.4
  115.6 8.5 %all-to-all-start = ((bf16[4,192,128]{2,1,0:T(8,128)(2,1)}), bf16[4,192,128]{2,1,0:T(8,128)(2,1)S(1)}, u32[]{:S(2)}, u32[]{:S(2)}) async-start(bf16[4,192,128]{2,1,0:T(8,128)(2,1)} %shard_map.97), calls=%async_computation | async-start | bytes 393216 | tf_op jit(solution)/shard_map/all_to_all | solution.py:288
  119.6 0.7 copy-start.9
  119.6 0.7 copy-start.8
  124.1 0.7 copy-start.6
  150.0 1.0 copy-start.5

commit v2 on v0

v2 whole, which is shorter than its diff:
```python
import functools

import jax
import jax.numpy as jnp
from jax import lax
from jax.experimental import pallas as pl
from jax.experimental.pallas import tpu as pltpu
from jax.sharding import Mesh
from jax.sharding import PartitionSpec as P

QH = 64
KVH = 8
HD = 128
SLOTS = 4
ROWS = 2
GROUP = 4
PER = QH // KVH
TENSOR = 8
SPAN = 128
WIDE = KVH * HD
SCALE = HD ** -0.5
FLOOR = -1e30

STAT = ROWS * QH
PARTIAL = STAT + QH
NOTE = 16

EDGE_A = ((0, 1), (1, 0), (2, 3), (3, 2))
EDGE_B = ((1, 2), (2, 1))
EDGE_C = ((1, 3), (2, 0))
RELAY = ((0, 3), (3, 0))
ASK_C = ((3, 1), (0, 2))

FULL = 60 * 2**20
PART = 16 * 2**20

SMEM = pl.BlockSpec(memory_space=pltpu.SMEM)
VMEM = pl.BlockSpec(memory_space=pltpu.VMEM)
HBM = pl.BlockSpec(memory_space=pltpu.HBM)


def replica_index():
    return lax.axis_index("x")


def first_survivor():
    return lax.axis_index("z") * (GROUP * ROWS)


def places(dest_ref, slot, first):
    local = dest_ref[slot] - first
    live = dest_ref[slot] >= 0
    return jnp.where(live, lax.shift_right_arithmetic(local, 1), -1), lax.bitwise_and(local, 1)


def send_kernel(dest_ref, length_ref, keys_ref, values_ref, a1_ref, a2_ref, b_ref,
                keys, values, note, load_sem, sem, note_sem):
    first, x = first_survivor(), replica_index()
    loads = []
    for slot in range(SLOTS):
        loads.append((
            pltpu.make_async_copy(keys_ref.at[slot], keys.at[slot], load_sem.at[0, slot]),
            pltpu.make_async_copy(values_ref.at[slot], values.at[slot], load_sem.at[1, slot]),
        ))
    for pair in loads:
        for load in pair:
            load.start()
    line = lax.broadcasted_iota(jnp.int32, (NOTE, WIDE), 0)
    guarded = []
    told = [jnp.zeros((NOTE, WIDE), jnp.int32) for _ in range(2)]
    for slot in range(SLOTS):
        host, row = places(dest_ref, slot, first)
        edge = jnp.where(host >= 0, lax.bitwise_xor(host, x), -1)
        along_a = (edge == 1) | (edge == 2)
        along_b = edge == 3
        length = length_ref[slot]
        for n, along in enumerate((along_a, along_b)):
            base = jnp.where(along, row * 3, NOTE)
            for k, value in enumerate((dest_ref[slot] - first + 1, lax.shift_right_logical(length, 4), lax.bitwise_and(length, 15))):
                told[n] = jnp.where(line == base + k, value, told[n])
        for which in range(ROWS):
            mine = row == which
            for guard, out, base in (
                (mine & along_a, (a1_ref, a2_ref)[which], 0),
                (mine & along_b, b_ref, 2 * SPAN * which),
            ):
                guarded.append((guard, slot, [
                    pltpu.make_async_copy(keys.at[slot], out.at[pl.ds(base, SPAN)], sem.at[slot, 0]),
                    pltpu.make_async_copy(values.at[slot], out.at[pl.ds(base + SPAN, SPAN)], sem.at[slot, 1]),
                ]))
    for n in range(2):
        note[n] = told[n].astype(jnp.float32).astype(jnp.bfloat16)
    notes = [
        pltpu.make_async_copy(note.at[0], a2_ref.at[pl.ds(2 * SPAN, NOTE)], note_sem.at[0]),
        pltpu.make_async_copy(note.at[1], b_ref.at[pl.ds(4 * SPAN, NOTE)], note_sem.at[1]),
    ]
    for copy in notes:
        copy.start()
    for slot in range(SLOTS):
        for load in loads[slot]:
            load.wait()
        start_guarded([(guard, copies) for guard, owner, copies in guarded if owner == slot])
    wait_guarded([(guard, copies) for guard, _, copies in guarded])
    for copy in notes:
        copy.wait()


def send_buffers(destination, lengths, keys, values):
    buffer = lambda rows: jax.ShapeDtypeStruct((rows, WIDE), jnp.bfloat16)
    return pl.pallas_call(
        send_kernel,
        out_shape=[buffer(2 * SPAN + NOTE), buffer(2 * SPAN + NOTE), buffer(4 * SPAN + NOTE)],
        in_specs=[SMEM, SMEM, HBM, HBM],
        out_specs=[HBM] * 3,
        scratch_shapes=[
            pltpu.VMEM((SLOTS, SPAN, WIDE), jnp.bfloat16),
            pltpu.VMEM((SLOTS, SPAN, WIDE), jnp.bfloat16),
            pltpu.VMEM((2, NOTE, WIDE), jnp.bfloat16),
            pltpu.SemaphoreType.DMA((2, SLOTS)),
            pltpu.SemaphoreType.DMA((SLOTS, 2)),
            pltpu.SemaphoreType.DMA((2,)),
        ],
        compiler_params=pltpu.CompilerParams(vmem_limit_bytes=FULL),
        cost_estimate=pl.CostEstimate(flops=0, bytes_accessed=4 * 2**20, transcendentals=0),
    )(destination, lengths, keys, values)


def gate_kernel(*refs):
    pass


def gate(held, awaited):
    return pl.pallas_call(
        gate_kernel,
        out_shape=[jax.ShapeDtypeStruct(one.shape, one.dtype) for one in held],
        in_specs=[HBM] * (len(held) + len(awaited)),
        out_specs=[HBM] * len(held),
        input_output_aliases={n: n for n in range(len(held))},
        compiler_params=pltpu.CompilerParams(vmem_limit_bytes=FULL),
        cost_estimate=pl.CostEstimate(flops=0, bytes_accessed=0, transcendentals=0),
    )(*held, *awaited)


def start_guarded(guarded):
    for guard, copies in guarded:
        @pl.when(guard)
        def _(copies=copies):
            for copy in copies:
                copy.start()


def wait_guarded(guarded):
    for guard, copies in guarded:
        @pl.when(guard)
        def _(copies=copies):
            for copy in copies:
                copy.wait()


def split_three(x):
    high = x.astype(jnp.bfloat16)
    rest = x - high.astype(jnp.float32)
    middle = rest.astype(jnp.bfloat16)
    low = (rest - middle.astype(jnp.float32)).astype(jnp.bfloat16)
    return high.astype(jnp.float32), middle.astype(jnp.float32), low.astype(jnp.float32)


def heads_of(ref, row):
    block = ref[...].astype(jnp.float32)
    return jnp.concatenate([block[row:row + 1, h * HD:(h + 1) * HD] for h in range(QH)], axis=0)


def spread_heads(query):
    head = lax.broadcasted_iota(jnp.int32, (QH, WIDE), 0)
    lane = lax.broadcasted_iota(jnp.int32, (QH, WIDE), 1)
    wide = jnp.concatenate([query] * KVH, axis=1)
    return jnp.where((head // PER) == (lane // HD), wide, 0.0).astype(jnp.bfloat16)


def block_attention(query, keys, values, length):
    position = lax.axis_index("t") * SPAN + lax.broadcasted_iota(jnp.int32, (QH, SPAN), 1)
    scores = lax.dot_general(
        spread_heads(query), keys, (((1,), (1,)), ((), ())), preferred_element_type=jnp.float32
    ) * SCALE
    valid = position < length
    peak = jnp.max(jnp.where(valid, scores, FLOOR), axis=1, keepdims=True)
    weights = jnp.where(valid, jnp.exp(scores - peak), 0.0).astype(jnp.bfloat16)
    mass = jnp.sum(weights.astype(jnp.float32), axis=1, keepdims=True)
    full = jnp.dot(weights, values, preferred_element_type=jnp.float32)
    partial = jnp.concatenate([full[g * PER:(g + 1) * PER, g * HD:(g + 1) * HD] for g in range(KVH)], axis=0)
    return peak, mass, partial.astype(jnp.bfloat16)


def statistics(row, peak, mass, held):
    column = lax.broadcasted_iota(jnp.int32, (QH, HD), 1)
    for k, piece in enumerate(split_three(peak) + split_three(mass)):
        held = jnp.where(column == row * 8 + k, piece, held)
    return held


def early_kernel(dest_ref, length_ref, asked_ref, queries_ref, new_keys_ref, new_values_ref, keys_ref, values_ref,
                 far_ref, own_ref, own_values_ref, keys, values, sem):
    first, x = first_survivor(), replica_index()
    line = lax.broadcasted_iota(jnp.int32, (NOTE, HD), 0)
    told = jnp.zeros((NOTE, HD), jnp.int32)
    far = []
    guarded = []
    for row in range(ROWS):
        found, length = jnp.int32(-1), jnp.int32(0)
        wanted = lax.bitwise_xor(x, 2) * ROWS + row + first
        for slot in range(SLOTS):
            hit = dest_ref[slot] == wanted
            found = jnp.where(hit, slot, found)
            length = jnp.where(hit, length_ref[slot], length)
        told = jnp.where((line == row * 3) & (found >= 0), wanted - first + 1, told)
        slot = jnp.maximum(found, 0)
        guarded.append((found >= 0, [
            pltpu.make_async_copy(keys_ref.at[slot], keys.at[row], sem.at[row, 0]),
            pltpu.make_async_copy(values_ref.at[slot], values.at[row], sem.at[row, 1]),
        ]))
        far.append((found, length))
    start_guarded(guarded)
    far_ref[PARTIAL:, :] = told.astype(jnp.float32).astype(jnp.bfloat16)
    far_ref[STAT:PARTIAL, :] = jnp.zeros((QH, HD), jnp.bfloat16)
    for row in range(ROWS):
        def per_head(ref):
            block = ref[...].astype(jnp.float32)
            return jnp.concatenate([
                jnp.broadcast_to(block[row:row + 1, g * HD:(g + 1) * HD], (PER, HD)) for g in range(KVH)
            ], axis=0)

        own = jnp.sum(heads_of(queries_ref, row) * per_head(new_keys_ref), axis=1, keepdims=True) * SCALE
        own_ref[row] = jnp.broadcast_to(own, (QH, HD))
        own_values_ref[row] = per_head(new_values_ref)
    wait_guarded(guarded)
    for row, (found, length) in enumerate(far):
        @pl.when(found >= 0)
        def _(row=row, length=length):
            peak, mass, partial = block_attention(heads_of(asked_ref, row), keys[row], values[row], length)
            far_ref[row * QH:(row + 1) * QH, :] = partial
            held = far_ref[STAT:PARTIAL, :].astype(jnp.float32)
            far_ref[STAT:PARTIAL, :] = statistics(row, peak, mass, held).astype(jnp.bfloat16)


def early(destination, lengths, asked, queries, new_keys, new_values, keys, values):
    own = jax.ShapeDtypeStruct((ROWS, QH, HD), jnp.float32)
    return pl.pallas_call(
        early_kernel,
        out_shape=[jax.ShapeDtypeStruct((PARTIAL + NOTE, HD), jnp.bfloat16), own, own],
        in_specs=[SMEM, SMEM] + [VMEM] * 4 + [HBM] * 2,
        out_specs=[VMEM] * 3,
        scratch_shapes=[
            pltpu.VMEM((ROWS, SPAN, WIDE), jnp.bfloat16),
            pltpu.VMEM((ROWS, SPAN, WIDE), jnp.bfloat16),
            pltpu.SemaphoreType.DMA((ROWS, 2)),
        ],
        compiler_params=pltpu.CompilerParams(vmem_limit_bytes=FULL),
        cost_estimate=pl.CostEstimate(flops=2**26, bytes_accessed=2**20, transcendentals=2**14),
    )(destination, lengths, asked, queries, new_keys, new_values, keys, values)


def attend_kernel(dest_ref, length_ref, queries_ref, keys_ref, values_ref, a1_ref, a2_ref, b_ref, far_ref,
                  out_ref, moved_keys_ref, moved_values_ref, stage, sem, moved_sem):
    first, x = first_survivor(), replica_index()
    note_a = a2_ref[2 * SPAN:, :HD].astype(jnp.float32)
    note_b = b_ref[4 * SPAN:, :HD].astype(jnp.float32)
    line = lax.broadcasted_iota(jnp.int32, (NOTE, HD), 0)
    rows = []
    guarded = []
    for row in range(ROWS):
        wanted = x * ROWS + row
        here, slot, length = jnp.bool_(False), jnp.int32(0), jnp.int32(0)
        for k in range(SLOTS):
            hit = dest_ref[k] == wanted + first
            here = here | hit
            slot = jnp.where(hit, k, slot)
            length = jnp.where(hit, length_ref[k], length)

        def read(note, k):
            return jnp.max(jnp.where(line == row * 3 + k, note, 0.0)).astype(jnp.int32)

        in_a, in_b = read(note_a, 0) == wanted + 1, read(note_b, 0) == wanted + 1
        length = jnp.where(in_a, read(note_a, 1) * 16 + read(note_a, 2), length)
        length = jnp.where(in_b, read(note_b, 1) * 16 + read(note_b, 2), length)
        rows.append((here | in_a | in_b, length))
        base = 2 * SPAN * row
        whole = stage.at[pl.ds(base, 2 * SPAN)]
        guarded.append((here, [
            pltpu.make_async_copy(keys_ref.at[slot], stage.at[pl.ds(base, SPAN)], sem.at[row, 0]),
            pltpu.make_async_copy(values_ref.at[slot], stage.at[pl.ds(base + SPAN, SPAN)], sem.at[row, 1]),
        ]))
        guarded.append((in_a, [
            pltpu.make_async_copy((a1_ref, a2_ref)[row].at[pl.ds(0, 2 * SPAN)], whole, sem.at[row, 0])
        ]))
        guarded.append((in_b, [pltpu.make_async_copy(b_ref.at[pl.ds(base, 2 * SPAN)], whole, sem.at[row, 0])]))
    start_guarded(guarded)
    out_ref[...] = far_ref[:PARTIAL, :]
    wait_guarded(guarded)
    moves = []
    for row, (near, _) in enumerate(rows):
        base = 2 * SPAN * row
        moves.append((near, [
            pltpu.make_async_copy(stage.at[pl.ds(base, SPAN)], moved_keys_ref.at[row], moved_sem.at[row, 0]),
            pltpu.make_async_copy(stage.at[pl.ds(base + SPAN, SPAN)], moved_values_ref.at[row], moved_sem.at[row, 1]),
        ]))
    start_guarded(moves)
    results = [
        block_attention(
            heads_of(queries_ref, row), stage[2 * SPAN * row:2 * SPAN * row + SPAN],
            stage[2 * SPAN * row + SPAN:2 * SPAN * (row + 1)], length,
        )
        for row, (_, length) in enumerate(rows)
    ]
    for row, ((near, _), (peak, mass, partial)) in enumerate(zip(rows, results)):
        @pl.when(near)
        def _(row=row, peak=peak, mass=mass, partial=partial):
            out_ref[row * QH:(row + 1) * QH, :] = partial
            held = out_ref[STAT:PARTIAL, :].astype(jnp.float32)
            out_ref[STAT:PARTIAL, :] = statistics(row, peak, mass, held).astype(jnp.bfloat16)
    wait_guarded(moves)


def attend(destination, lengths, queries, keys, values, a1, a2, b, far):
    moved = jax.ShapeDtypeStruct((ROWS, SPAN, WIDE), jnp.bfloat16)
    return pl.pallas_call(
        attend_kernel,
        out_shape=[jax.ShapeDtypeStruct((PARTIAL, HD), jnp.bfloat16), moved, moved],
        in_specs=[SMEM, SMEM, VMEM, HBM, HBM, HBM, VMEM, VMEM, VMEM],
        out_specs=[VMEM, HBM, HBM],
        scratch_shapes=[
            pltpu.VMEM((4 * SPAN, WIDE), jnp.bfloat16),
            pltpu.SemaphoreType.DMA((ROWS, 2)),
            pltpu.SemaphoreType.DMA((ROWS, 2)),
        ],
        compiler_params=pltpu.CompilerParams(vmem_limit_bytes=PART),
        cost_estimate=pl.CostEstimate(flops=2**34, bytes_accessed=2 * 2**20, transcendentals=2**14),
    )(destination, lengths, queries, keys, values, a1, a2, b, far)


def finish_kernel(far_ref, blocks_ref, own_ref, own_values_ref, c1_ref, c2_ref, keys_in_ref, values_in_ref,
                  attended_ref, moved_keys_ref, moved_values_ref, sem):
    x = replica_index()
    note = far_ref[PARTIAL:, :].astype(jnp.float32)
    line = lax.broadcasted_iota(jnp.int32, (NOTE, HD), 0)
    guarded = []
    for row, buffer in enumerate((c1_ref, c2_ref)):
        told = jnp.max(jnp.where(line == row * 3, note, 0.0)).astype(jnp.int32)
        guarded.append((told == x * ROWS + row + 1, [
            pltpu.make_async_copy(buffer.at[pl.ds(0, SPAN)], moved_keys_ref.at[row], sem.at[row, 0]),
            pltpu.make_async_copy(buffer.at[pl.ds(SPAN, SPAN)], moved_values_ref.at[row], sem.at[row, 1]),
        ]))
    start_guarded(guarded)
    column = lax.broadcasted_iota(jnp.int32, (QH, HD), 1)
    own = jnp.where(column < 8, own_ref[0], own_ref[1])
    joined = []
    for b in range(TENSOR):
        stats = blocks_ref[b, STAT:PARTIAL, :].astype(jnp.float32)
        joined.append((stats + pltpu.roll(stats, HD - 1, 1)) + pltpu.roll(stats, HD - 2, 1))
    top = functools.reduce(jnp.maximum, joined, own)
    own_weight = jnp.exp(own - top)
    fades = [jnp.exp(part - top) for part in joined]
    denominator = own_weight
    for part, fade in zip(joined, fades):
        denominator = denominator + fade * pltpu.roll(part, HD - 3, 1)
    parts = []
    for row in range(ROWS):
        pick = slice(row * 8, row * 8 + 1)
        total = own_weight[:, pick] * own_values_ref[row]
        for b in range(TENSOR):
            total = total + fades[b][:, pick] * blocks_ref[b, row * QH:(row + 1) * QH, :].astype(jnp.float32)
        parts.append(total / denominator[:, pick])
    for head in range(QH):
        both = jnp.concatenate([part[head:head + 1] for part in parts], axis=0)
        attended_ref[:, head * HD:(head + 1) * HD] = both.astype(jnp.bfloat16)
    wait_guarded(guarded)


def finish(far, blocks, own, own_values, c1, c2, moved_keys, moved_values):
    moved = jax.ShapeDtypeStruct((ROWS, SPAN, WIDE), jnp.bfloat16)
    return pl.pallas_call(
        finish_kernel,
        out_shape=[jax.ShapeDtypeStruct((ROWS, QH * HD), jnp.bfloat16), moved, moved],
        in_specs=[VMEM] * 6 + [HBM] * 2,
        out_specs=[VMEM, HBM, HBM],
        input_output_aliases={6: 1, 7: 2},
        scratch_shapes=[pltpu.SemaphoreType.DMA((ROWS, 2))],
        compiler_params=pltpu.CompilerParams(vmem_limit_bytes=PART),
        cost_estimate=pl.CostEstimate(flops=2**20, bytes_accessed=2**20, transcendentals=2**16),
    )(far, blocks, own, own_values, c1, c2, moved_keys, moved_values)


def on_device(keys, values, lengths, destination, queries, new_keys, new_values):
    asked = lax.ppermute(queries, "x", ASK_C)
    a1, a2, b = gate(send_buffers(destination, lengths, keys, values), (asked,))
    a1 = lax.ppermute(a1, "x", EDGE_A)
    a2 = lax.ppermute(a2, "x", EDGE_A)
    b = lax.ppermute(b, "x", EDGE_B)
    far, own, own_values = early(destination, lengths, asked, queries, new_keys, new_values, keys, values)
    far = lax.ppermute(far, "x", EDGE_C)
    c1 = lax.ppermute(a1, "x", RELAY)
    c2 = lax.ppermute(a2, "x", RELAY)
    partial, moved_keys, moved_values = attend(destination, lengths, queries, keys, values, a1, a2, b, far)
    blocks = lax.all_gather(partial, "t")
    attended, moved_keys, moved_values = finish(far, blocks, own, own_values, c1, c2, moved_keys, moved_values)
    return moved_keys, moved_values, attended


def solution(mesh):
    groups = Mesh(mesh.devices.reshape(-1, GROUP, TENSOR), ("z", "x", "t"))
    dp = ("z", "x")
    return jax.shard_map(
        on_device,
        mesh=groups,
        in_specs=(P(dp, "t", None), P(dp, "t", None), P(dp), P(dp), P(dp, None), P(dp, None), P(dp, None)),
        out_specs=(P(dp, "t", None), P(dp, "t", None), P(dp, None)),
        check_vma=False,
    )
```

time: 189 us -> 61.5 us (0.33)
  the two profiles are of different devices: /device:TPU:235 before, /device:TPU:1 now
where the time goes in v2:
time: 61.5 us; the launch traced here: 61 us
  starting transfers between devices  20.3 us (33%)
  blocking collectives  18.1 us (29%)
  waiting for transfers between devices  12.8 us (21%)
  Pallas kernels  8.29 us (13%)
  between operations  0.85 us (1%)
  local copies, waits for them, and re-layouts  0.65 us (1%)
    all_gather x1, blocking collectives, on_device(): blocks = lax.all_gather(partial, 't')  18.1 us
    ppermute x1, waiting for transfers between devices, on_device(): a2 = lax.ppermute(a2, 'x', EDGE_A)  8.76 us
    ppermute x1, starting transfers between devices, on_device(): asked = lax.ppermute(queries, 'x', ASK_C)  5.48 us
    ppermute x1, waiting for transfers between devices, on_device(): a1 = lax.ppermute(a1, 'x', EDGE_A)  4.08 us
    ppermute x1, starting transfers between devices, on_device(): a1 = lax.ppermute(a1, 'x', EDGE_A)  4.02 us
    ppermute x1, starting transfers between devices, on_device(): c1 = lax.ppermute(a1, 'x', RELAY)  3.28 us
    ppermute x1, starting transfers between devices, on_device(): c2 = lax.ppermute(a2, 'x', RELAY)  3.28 us
    pallas_call x1, Pallas kernels, send_buffers(): pl.pallas_call(send_kernel, out_shape=[buffer(2 * SPAN + NOTE), buffer(2...  3.18 us
  transfers between devices with their start and end apart: 7, of which 2 were waited for; matrix products, arithmetic and copies ran while one was open for 0% of the time, Pallas kernels for 12%

profile of v2, /device:TPU:1, one launch (start us, length us, event | category | flops | bytes accessed | tf_op | source)
XLA Modules:
  0.0 61.0 jit_solution(17335426819380526542)
XLA Ops:
  0.6 5.5 %collective-permute-start = (bf16[2,8192]{1,0:T(2,128)(2,1)}, bf16[2,8192]{1,0:T(2,128)(2,1)S(1)}, u32[]{:S(2)}, u32[]{:S(2)}) collective-permute-start(bf16[2,8192]{1,0:T(2,128)(2,1)} %queries_ref.3), channel_id=1, source_target_pairs={{24,8},{0,16},{25,9},{1,17},{26,10},{2,18},{27,11},{3,19},{28,12},... | collective-permute-start | bytes 98312 | tf_op jit(solution)/shard_map/ppermute | solution.py:393
  6.1 3.2 %shard_map.95 = (bf16[272,1024]{1,0:T(8,128)(2,1)}, bf16[272,1024]{1,0:T(8,128)(2,1)}, bf16[528,1024]{1,0:T(8,128)(2,1)}) custom-call(s32[4]{0:T(128)} %dest_ref.5, s32[4]{0:T(128)} %length_ref.5, bf16[4,128,1024]{2,1,0:T(8,128)(2,1)} %keys_ref.5, bf16[4,128,1024]{2,1,0:T(8,128)(2,1)} %values_ref.5), custom_call_target="tpu_custom_call" | custom-call | bytes 4194304 | tf_op jit(solution)/shard_map/pallas_call | solution.py:110
  9.3 0.0 copy-start.7
  9.3 0.6 copy-done.7
  9.9 0.7 %collective-permute-start.4 = (bf16[528,1024]{1,0:T(8,128)(2,1)}, bf16[528,1024]{1,0:T(8,128)(2,1)S(1)}, u32[]{:S(2)}, u32[]{:S(2)}) collective-permute-start(bf16[528,1024]{1,0:T(8,128)(2,1)} %get-tuple-element.24), channel_id=1, source_target_pairs={{8,16},{16,8},{9,17},{17,9},{10,18},{18,10},{11,19},{19,11},{12,20... | collective-permute-start | bytes 3244040 | tf_op jit(solution)/shard_map/ppermute | solution.py:397
  10.7 4.0 %collective-permute-start.2 = (bf16[272,1024]{1,0:T(8,128)(2,1)}, bf16[272,1024]{1,0:T(8,128)(2,1)S(1)}, u32[]{:S(2)}, u32[]{:S(2)}) collective-permute-start(bf16[272,1024]{1,0:T(8,128)(2,1)} %get-tuple-element.22), channel_id=1, source_target_pairs={{0,8},{8,0},{16,24},{24,16},{1,9},{9,1},{17,25},{25,17},{2,10},{10... | collective-permute-start | bytes 1671176 | tf_op jit(solution)/shard_map/ppermute | solution.py:395
  14.7 0.0 copy-start
  14.7 0.0 copy-start.1
  14.7 0.0 copy-start.4
  14.7 0.0 copy-start.5
  14.7 0.0 copy-start.6
  14.8 2.1 %collective-permute-start.3 = (bf16[272,1024]{1,0:T(8,128)(2,1)}, bf16[272,1024]{1,0:T(8,128)(2,1)}, u32[]{:S(2)}, u32[]{:S(2)}) collective-permute-start(bf16[272,1024]{1,0:T(8,128)(2,1)} %get-tuple-element.23), channel_id=1, source_target_pairs={{0,8},{8,0},{16,24},{24,16},{1,9},{9,1},{17,25},{25,17},{2,10},{10... | collective-permute-start | bytes 1671176 | tf_op jit(solution)/shard_map/ppermute | solution.py:396
  16.8 1.6 %shard_map.94 = (bf16[208,128]{1,0:T(8,128)(2,1)}, f32[2,64,128]{2,1,0:T(8,128)}, f32[2,64,128]{2,1,0:T(8,128)}) custom-call(s32[4]{0:T(128)} %dest_ref.5, s32[4]{0:T(128)} %length_ref.5, bf16[2,8192]{1,0:T(2,128)(2,1)} %copy-done.7, bf16[2,8192]{1,0:T(2,128)(2,1)} %queries_ref.3, bf16[2,1024]{1,0:T(2,128)(2,1)} %new_keys_ref.1, ...), custom_call_target="tpu_custom_call" | custom-call | flops 67108864 | bytes 1048576 | tf_op jit(solution)/shard_map/pallas_call | solution.py:247
  18.5 1.4 %collective-permute-start.1 = (bf16[208,128]{1,0:T(8,128)(2,1)}, bf16[208,128]{1,0:T(8,128)(2,1)S(1)}, u32[]{:S(2)}, u32[]{:S(2)}) collective-permute-start(bf16[208,128]{1,0:T(8,128)(2,1)} %get-tuple-element.18), channel_id=1, source_target_pairs={{8,24},{16,0},{9,25},{17,1},{10,26},{18,2},{11,27},{19,3},{12,28},... | collective-permute-start | bytes 159752 | tf_op jit(solution)/shard_map/ppermute | solution.py:399
  19.9 4.1 %collective-permute-done.2.a1_ref = bf16[272,1024]{1,0:T(8,128)(2,1)S(1)} collective-permute-done((bf16[272,1024]{1,0:T(8,128)(2,1)}, bf16[272,1024]{1,0:T(8,128)(2,1)S(1)}, u32[]{:S(2)}, u32[]{:S(2)}) %collective-permute-start.2) | collective-permute-done | bytes 557088 | tf_op jit(solution)/shard_map/ppermute | solution.py:395
  24.0 3.3 %collective-permute-start.5 = (bf16[272,1024]{1,0:T(8,128)(2,1)S(1)}, bf16[272,1024]{1,0:T(8,128)(2,1)S(1)}, u32[]{:S(2)}, u32[]{:S(2)}) collective-permute-start(bf16[272,1024]{1,0:T(8,128)(2,1)S(1)} %collective-permute-done.2.a1_ref), channel_id=1, source_target_pairs={{0,24},{24,0},{1,25},{25,1},{2,26},{26,2},{3,27},{27,3},{4,28},{28... | collective-permute-start | bytes 1671176 | tf_op jit(solution)/shard_map/ppermute | solution.py:400
  27.3 8.8 %collective-permute-done.3.a2_ref = bf16[272,1024]{1,0:T(8,128)(2,1)} collective-permute-done((bf16[272,1024]{1,0:T(8,128)(2,1)}, bf16[272,1024]{1,0:T(8,128)(2,1)}, u32[]{:S(2)}, u32[]{:S(2)}) %collective-permute-start.3) | collective-permute-done | bytes 557088 | tf_op jit(solution)/shard_map/ppermute | solution.py:396
  36.0 3.3 %collective-permute-start.6 = (bf16[272,1024]{1,0:T(8,128)(2,1)}, bf16[272,1024]{1,0:T(8,128)(2,1)S(1)}, u32[]{:S(2)}, u32[]{:S(2)}) collective-permute-start(bf16[272,1024]{1,0:T(8,128)(2,1)} %collective-permute-done.3.a2_ref), channel_id=1, source_target_pairs={{0,24},{24,0},{1,25},{25,1},{2,26},{26,2},{3,27},{27,3},{4,28},{28... | collective-permute-start | bytes 1671176 | tf_op jit(solution)/shard_map/ppermute | solution.py:401
  39.3 0.0 collective-permute-done.1.far_ref
  39.4 2.4 %shard_map.97 = (bf16[192,128]{1,0:T(8,128)(2,1)S(1)}, bf16[2,128,1024]{2,1,0:T(8,128)(2,1)}, bf16[2,128,1024]{2,1,0:T(8,128)(2,1)}) custom-call(s32[4]{0:T(128)S(1)} %copy-done.5, s32[4]{0:T(128)S(1)} %copy-done.6, bf16[2,8192]{1,0:T(2,128)(2,1)S(1)} %copy-done.4, bf16[4,128,1024]{2,1,0:T(8,128)(2,1)S(1)} %copy-done, bf16[4,128,1024]{2,1,0:T(8,128)(2,1)S(1)} %copy-done.1, ...), custom_call_target="tpu_custom_call" | custom-call | flops 17179869184 | bytes 2097152 | tf_op jit(solution)/shard_map/pallas_call | solution.py:325
  41.8 18.1 %all-gather = bf16[1536,128]{1,0:T(8,128)(2,1)S(1)} all-gather(bf16[192,128]{1,0:T(8,128)(2,1)S(1)} %get-tuple-element.25), channel_id=2, replica_groups=mesh['z'=16,'x'=4,'t'=8] {'t'}, dimensions={0}, use_global_device_ids=true | all-gather | bytes 442368 | tf_op jit(solution)/shard_map/all_gather | solution.py:403
  59.9 0.0 collective-permute-done.5.c1_ref
  59.9 0.0 collective-permute-done.6.c2_ref
  59.9 1.1 %shard_map.98 = (bf16[2,8192]{1,0:T(2,128)(2,1)}, bf16[2,128,1024]{2,1,0:T(8,128)(2,1)}, bf16[2,128,1024]{2,1,0:T(8,128)(2,1)}) custom-call(bf16[208,128]{1,0:T(8,128)(2,1)S(1)} %collective-permute-done.1.far_ref, bf16[8,192,128]{2,1,0:T(8,128)(2,1)S(1)} %bitcast.1, f32[2,64,128]{2,1,0:T(8,128)S(1)} %copy-done.2, ...), custom_call_target="tpu_custom_call", output_to_operand_aliasing={{1}: (6, {}), {2}: (7, {})} | custom-call | flops 1048576 | bytes 1048576 | tf_op jit(solution)/shard_map/pallas_call | solution.py:380
  (12 shorter events, 0.0 us)
Async XLA Ops:
  0.6 8.7 %collective-permute-start = (bf16[2,8192]{1,0:T(2,128)(2,1)}, bf16[2,8192]{1,0:T(2,128)(2,1)S(1)}, u32[]{:S(2)}, u32[]{:S(2)}) collective-permute-start(bf16[2,8192]{1,0:T(2,128)(2,1)} %queries_ref.3), channel_id=1, source_target_pairs={{24,8},{0,16},{25,9},{1,17},{26,10},{2,18},{27,11},{3,19},{28,12},... | collective-permute-start | bytes 98312 | tf_op jit(solution)/shard_map/ppermute | solution.py:393
  9.3 0.6 %copy-start.7 = (bf16[2,8192]{1,0:T(2,128)(2,1)}, bf16[2,8192]{1,0:T(2,128)(2,1)S(1)}, u32[]{:S(2)}) copy-start(bf16[2,8192]{1,0:T(2,128)(2,1)S(1)} %collective-permute-done.asked_ref.refs_3_) | copy-start | bytes 98308
  9.9 29.4 %collective-permute-start.4 = (bf16[528,1024]{1,0:T(8,128)(2,1)}, bf16[528,1024]{1,0:T(8,128)(2,1)S(1)}, u32[]{:S(2)}, u32[]{:S(2)}) collective-permute-start(bf16[528,1024]{1,0:T(8,128)(2,1)} %get-tuple-element.24), channel_id=1, source_target_pairs={{8,16},{16,8},{9,17},{17,9},{10,18},{18,10},{11,19},{19,11},{12,20... | collective-permute-start | bytes 3244040 | tf_op jit(solution)/shard_map/ppermute | solution.py:397
  10.7 13.3 %collective-permute-start.2 = (bf16[272,1024]{1,0:T(8,128)(2,1)}, bf16[272,1024]{1,0:T(8,128)(2,1)S(1)}, u32[]{:S(2)}, u32[]{:S(2)}) collective-permute-start(bf16[272,1024]{1,0:T(8,128)(2,1)} %get-tuple-element.22), channel_id=1, source_target_pairs={{0,8},{8,0},{16,24},{24,16},{1,9},{9,1},{17,25},{25,17},{2,10},{10... | collective-permute-start | bytes 1671176 | tf_op jit(solution)/shard_map/ppermute | solution.py:395
  14.7 24.6 %copy-start = (bf16[4,128,1024]{2,1,0:T(8,128)(2,1)S(1)}, bf16[4,128,1024]{2,1,0:T(8,128)(2,1)}, u32[]{:S(2)}) copy-start(bf16[4,128,1024]{2,1,0:T(8,128)(2,1)} %keys_ref.5) | copy-start | bytes 3145732
  14.7 24.6 %copy-start.1 = (bf16[4,128,1024]{2,1,0:T(8,128)(2,1)S(1)}, bf16[4,128,1024]{2,1,0:T(8,128)(2,1)}, u32[]{:S(2)}) copy-start(bf16[4,128,1024]{2,1,0:T(8,128)(2,1)} %values_ref.5) | copy-start | bytes 3145732
  14.7 24.6 %copy-start.4 = (bf16[2,8192]{1,0:T(2,128)(2,1)S(1)}, bf16[2,8192]{1,0:T(2,128)(2,1)}, u32[]{:S(2)}) copy-start(bf16[2,8192]{1,0:T(2,128)(2,1)} %queries_ref.3) | copy-start | bytes 98308
  14.7 24.6 %copy-start.5 = (s32[4]{0:T(128)S(1)}, s32[4]{0:T(128)}, u32[]{:S(2)}) copy-start(s32[4]{0:T(128)} %dest_ref.5) | copy-start | bytes 52
  14.7 24.6 %copy-start.6 = (s32[4]{0:T(128)S(1)}, s32[4]{0:T(128)}, u32[]{:S(2)}) copy-start(s32[4]{0:T(128)} %length_ref.5) | copy-start | bytes 52
  14.8 21.3 %collective-permute-start.3 = (bf16[272,1024]{1,0:T(8,128)(2,1)}, bf16[272,1024]{1,0:T(8,128)(2,1)}, u32[]{:S(2)}, u32[]{:S(2)}) collective-permute-start(bf16[272,1024]{1,0:T(8,128)(2,1)} %get-tuple-element.23), channel_id=1, source_target_pairs={{0,8},{8,0},{16,24},{24,16},{1,9},{9,1},{17,25},{25,17},{2,10},{10... | collective-permute-start | bytes 1671176 | tf_op jit(solution)/shard_map/ppermute | solution.py:396
  18.5 41.5 %copy-start.2 = (f32[2,64,128]{2,1,0:T(8,128)S(1)}, f32[2,64,128]{2,1,0:T(8,128)}, u32[]{:S(2)}) copy-start(f32[2,64,128]{2,1,0:T(8,128)} %get-tuple-element.26.own_ref) | copy-start | bytes 196612
  18.5 41.5 %copy-start.3 = (f32[2,64,128]{2,1,0:T(8,128)S(1)}, f32[2,64,128]{2,1,0:T(8,128)}, u32[]{:S(2)}) copy-start(f32[2,64,128]{2,1,0:T(8,128)} %get-tuple-element.27.own_values_ref) | copy-start | bytes 196612
  18.5 20.8 %collective-permute-start.1 = (bf16[208,128]{1,0:T(8,128)(2,1)}, bf16[208,128]{1,0:T(8,128)(2,1)S(1)}, u32[]{:S(2)}, u32[]{:S(2)}) collective-permute-start(bf16[208,128]{1,0:T(8,128)(2,1)} %get-tuple-element.18), channel_id=1, source_target_pairs={{8,24},{16,0},{9,25},{17,1},{10,26},{18,2},{11,27},{19,3},{12,28},... | collective-permute-start | bytes 159752 | tf_op jit(solution)/shard_map/ppermute | solution.py:399
  24.0 35.9 %collective-permute-start.5 = (bf16[272,1024]{1,0:T(8,128)(2,1)S(1)}, bf16[272,1024]{1,0:T(8,128)(2,1)S(1)}, u32[]{:S(2)}, u32[]{:S(2)}) collective-permute-start(bf16[272,1024]{1,0:T(8,128)(2,1)S(1)} %collective-permute-done.2.a1_ref), channel_id=1, source_target_pairs={{0,24},{24,0},{1,25},{25,1},{2,26},{26,2},{3,27},{27,3},{4,28},{28... | collective-permute-start | bytes 1671176 | tf_op jit(solution)/shard_map/ppermute | solution.py:400
  36.0 23.9 %collective-permute-start.6 = (bf16[272,1024]{1,0:T(8,128)(2,1)}, bf16[272,1024]{1,0:T(8,128)(2,1)S(1)}, u32[]{:S(2)}, u32[]{:S(2)}) collective-permute-start(bf16[272,1024]{1,0:T(8,128)(2,1)} %collective-permute-done.3.a2_ref), channel_id=1, source_target_pairs={{0,24},{24,0},{1,25},{25,1},{2,26},{26,2},{3,27},{27,3},{4,28},{28... | collective-permute-start | bytes 1671176 | tf_op jit(solution)/shard_map/ppermute | solution.py:401

commit v3 on v2

--- a/solution.py
+++ b/solution.py
@@ -22,9 +22,9 @@
 FLOOR = -1e30
 
 STAT = ROWS * QH
-PARTIAL = STAT + QH
+STATS = 6
+PARTIAL = STAT + 16
 NOTE = 16
-
 EDGE_A = ((0, 1), (1, 0), (2, 3), (3, 2))
 EDGE_B = ((1, 2), (2, 1))
 EDGE_C = ((1, 3), (2, 0))
@@ -53,7 +53,18 @@
     return jnp.where(live, lax.shift_right_arithmetic(local, 1), -1), lax.bitwise_and(local, 1)
 
 
-def send_kernel(dest_ref, length_ref, keys_ref, values_ref, a1_ref, a2_ref, b_ref,
+def along_a_places(row, a1_ref, a2_ref):
+    if row == 0:
+        return a1_ref.at[pl.ds(0, SPAN)], a1_ref.at[pl.ds(SPAN, SPAN)]
+    return a1_ref.at[pl.ds(2 * SPAN, SPAN)], a2_ref.at[pl.ds(0, SPAN)]
+
+
+def along_b_places(row, b1_ref, b2_ref):
+    buffer = (b1_ref, b2_ref)[row]
+    return buffer.at[pl.ds(0, SPAN)], buffer.at[pl.ds(SPAN, SPAN)]
+
+
+def send_kernel(dest_ref, length_ref, keys_ref, values_ref, queries_ref, a1_ref, a2_ref, b1_ref, b2_ref, ask_ref,
                 keys, values, note, load_sem, sem, note_sem):
     first, x = first_survivor(), replica_index()
     loads = []
@@ -80,20 +91,21 @@
                 told[n] = jnp.where(line == base + k, value, told[n])
         for which in range(ROWS):
             mine = row == which
-            for guard, out, base in (
-                (mine & along_a, (a1_ref, a2_ref)[which], 0),
-                (mine & along_b, b_ref, 2 * SPAN * which),
+            for guard, to_keys, to_values in (
+                (mine & along_a,) + along_a_places(which, a1_ref, a2_ref),
+                (mine & along_b,) + along_b_places(which, b1_ref, b2_ref),
             ):
                 guarded.append((guard, slot, [
-                    pltpu.make_async_copy(keys.at[slot], out.at[pl.ds(base, SPAN)], sem.at[slot, 0]),
-                    pltpu.make_async_copy(values.at[slot], out.at[pl.ds(base + SPAN, SPAN)], sem.at[slot, 1]),
+                    pltpu.make_async_copy(keys.at[slot], to_keys, sem.at[slot, 0]),
+                    pltpu.make_async_copy(values.at[slot], to_values, sem.at[slot, 1]),
                 ]))
     for n in range(2):
         note[n] = told[n].astype(jnp.float32).astype(jnp.bfloat16)
     notes = [
-        pltpu.make_async_copy(note.at[0], a2_ref.at[pl.ds(2 * SPAN, NOTE)], note_sem.at[0]),
-        pltpu.make_async_copy(note.at[1], b_ref.at[pl.ds(4 * SPAN, NOTE)], note_sem.at[1]),
+        pltpu.make_async_copy(note.at[0], a2_ref.at[pl.ds(SPAN, NOTE)], note_sem.at[0]),
+        pltpu.make_async_copy(note.at[1], b2_ref.at[pl.ds(2 * SPAN, NOTE)], note_sem.at[1]),
     ]
+    notes.append(pltpu.make_async_copy(queries_ref, ask_ref, note_sem.at[2]))
     for copy in notes:
         copy.start()
     for slot in range(SLOTS):
@@ -105,40 +117,27 @@
         copy.wait()
 
 
-def send_buffers(destination, lengths, keys, values):
+def send_buffers(destination, lengths, keys, values, queries):
     buffer = lambda rows: jax.ShapeDtypeStruct((rows, WIDE), jnp.bfloat16)
     return pl.pallas_call(
         send_kernel,
-        out_shape=[buffer(2 * SPAN + NOTE), buffer(2 * SPAN + NOTE), buffer(4 * SPAN + NOTE)],
-        in_specs=[SMEM, SMEM, HBM, HBM],
-        out_specs=[HBM] * 3,
+        out_shape=[
+            buffer(3 * SPAN), buffer(SPAN + NOTE), buffer(2 * SPAN), buffer(2 * SPAN + NOTE),
+            jax.ShapeDtypeStruct(queries.shape, queries.dtype),
+        ],
+        in_specs=[SMEM, SMEM, HBM, HBM, VMEM],
+        out_specs=[HBM] * 5,
         scratch_shapes=[
             pltpu.VMEM((SLOTS, SPAN, WIDE), jnp.bfloat16),
             pltpu.VMEM((SLOTS, SPAN, WIDE), jnp.bfloat16),
             pltpu.VMEM((2, NOTE, WIDE), jnp.bfloat16),
             pltpu.SemaphoreType.DMA((2, SLOTS)),
             pltpu.SemaphoreType.DMA((SLOTS, 2)),
-            pltpu.SemaphoreType.DMA((2,)),
+            pltpu.SemaphoreType.DMA((3,)),
         ],
         compiler_params=pltpu.CompilerParams(vmem_limit_bytes=FULL),
         cost_estimate=pl.CostEstimate(flops=0, bytes_accessed=4 * 2**20, transcendentals=0),
-    )(destination, lengths, keys, values)
-
-
-def gate_kernel(*refs):
-    pass
-
-
-def gate(held, awaited):
-    return pl.pallas_call(
-        gate_kernel,
-        out_shape=[jax.ShapeDtypeStruct(one.shape, one.dtype) for one in held],
-        in_specs=[HBM] * (len(held) + len(awaited)),
-        out_specs=[HBM] * len(held),
-        input_output_aliases={n: n for n in range(len(held))},
-        compiler_params=pltpu.CompilerParams(vmem_limit_bytes=FULL),
-        cost_estimate=pl.CostEstimate(flops=0, bytes_accessed=0, transcendentals=0),
-    )(*held, *awaited)
+    )(destination, lengths, keys, values, queries)
 
 
 def start_guarded(guarded):
@@ -191,11 +190,22 @@
     return peak, mass, partial.astype(jnp.bfloat16)
 
 
-def statistics(row, peak, mass, held):
-    column = lax.broadcasted_iota(jnp.int32, (QH, HD), 1)
-    for k, piece in enumerate(split_three(peak) + split_three(mass)):
-        held = jnp.where(column == row * 8 + k, piece, held)
-    return held
+def flip(columns):
+    lane = lax.broadcasted_iota(jnp.int32, (QH, HD), 1)
+    block = jnp.zeros((QH, HD), jnp.float32)
+    for n, column in columns.items():
+        block = jnp.where(lane == n, column, block)
+    return jnp.transpose(jnp.concatenate([block, jnp.zeros((HD - QH, HD), jnp.float32)], axis=0))
+
+
+def statistics(row, peak, mass):
+    columns = {row * STATS + k: piece for k, piece in enumerate(split_three(peak) + split_three(mass))}
+    return flip(columns)[:16].astype(jnp.bfloat16)
+
+
+def mine(row):
+    line = lax.broadcasted_iota(jnp.int32, (16, HD), 0)
+    return (line >= row * STATS) & (line < (row + 1) * STATS)
 
 
 def early_kernel(dest_ref, length_ref, asked_ref, queries_ref, new_keys_ref, new_values_ref, keys_ref, values_ref,
@@ -221,7 +231,8 @@
         far.append((found, length))
     start_guarded(guarded)
     far_ref[PARTIAL:, :] = told.astype(jnp.float32).astype(jnp.bfloat16)
-    far_ref[STAT:PARTIAL, :] = jnp.zeros((QH, HD), jnp.bfloat16)
+    far_ref[STAT:PARTIAL, :] = jnp.zeros((16, HD), jnp.bfloat16)
+    own = {}
     for row in range(ROWS):
         def per_head(ref):
             block = ref[...].astype(jnp.float32)
@@ -229,24 +240,26 @@
                 jnp.broadcast_to(block[row:row + 1, g * HD:(g + 1) * HD], (PER, HD)) for g in range(KVH)
             ], axis=0)
 
-        own = jnp.sum(heads_of(queries_ref, row) * per_head(new_keys_ref), axis=1, keepdims=True) * SCALE
-        own_ref[row] = jnp.broadcast_to(own, (QH, HD))
+        own[row] = jnp.sum(heads_of(queries_ref, row) * per_head(new_keys_ref), axis=1, keepdims=True) * SCALE
         own_values_ref[row] = per_head(new_values_ref)
+    own_ref[...] = flip(own)[:8]
     wait_guarded(guarded)
     for row, (found, length) in enumerate(far):
         @pl.when(found >= 0)
         def _(row=row, length=length):
             peak, mass, partial = block_attention(heads_of(asked_ref, row), keys[row], values[row], length)
             far_ref[row * QH:(row + 1) * QH, :] = partial
-            held = far_ref[STAT:PARTIAL, :].astype(jnp.float32)
-            far_ref[STAT:PARTIAL, :] = statistics(row, peak, mass, held).astype(jnp.bfloat16)
+            far_ref[STAT:PARTIAL, :] = jnp.where(mine(row), statistics(row, peak, mass), far_ref[STAT:PARTIAL, :])
 
 
 def early(destination, lengths, asked, queries, new_keys, new_values, keys, values):
-    own = jax.ShapeDtypeStruct((ROWS, QH, HD), jnp.float32)
     return pl.pallas_call(
         early_kernel,
-        out_shape=[jax.ShapeDtypeStruct((PARTIAL + NOTE, HD), jnp.bfloat16), own, own],
+        out_shape=[
+            jax.ShapeDtypeStruct((PARTIAL + NOTE, HD), jnp.bfloat16),
+            jax.ShapeDtypeStruct((8, HD), jnp.float32),
+            jax.ShapeDtypeStruct((ROWS, QH, HD), jnp.float32),
+        ],
         in_specs=[SMEM, SMEM] + [VMEM] * 4 + [HBM] * 2,
         out_specs=[VMEM] * 3,
         scratch_shapes=[
@@ -254,16 +267,16 @@
             pltpu.VMEM((ROWS, SPAN, WIDE), jnp.bfloat16),
             pltpu.SemaphoreType.DMA((ROWS, 2)),
         ],
-        compiler_params=pltpu.CompilerParams(vmem_limit_bytes=FULL),
-        cost_estimate=pl.CostEstimate(flops=2**26, bytes_accessed=2**20, transcendentals=2**14),
+        compiler_params=pltpu.CompilerParams(vmem_limit_bytes=PART),
+        cost_estimate=pl.CostEstimate(flops=2**32, bytes_accessed=2**20, transcendentals=2**14),
     )(destination, lengths, asked, queries, new_keys, new_values, keys, values)
 
 
-def attend_kernel(dest_ref, length_ref, queries_ref, keys_ref, values_ref, a1_ref, a2_ref, b_ref, far_ref,
-                  out_ref, moved_keys_ref, moved_values_ref, stage, sem, moved_sem):
+def attend_kernel(dest_ref, length_ref, queries_ref, keys_ref, values_ref, a1_ref, a2_ref, b1_ref, b2_ref, far_ref,
+                  out_ref, moved_keys_ref, moved_values_ref, stage, pack, sem, moved_sem):
     first, x = first_survivor(), replica_index()
-    note_a = a2_ref[2 * SPAN:, :HD].astype(jnp.float32)
-    note_b = b_ref[4 * SPAN:, :HD].astype(jnp.float32)
+    note_a = a2_ref[SPAN:, :HD].astype(jnp.float32)
+    note_b = b2_ref[2 * SPAN:, :HD].astype(jnp.float32)
     line = lax.broadcasted_iota(jnp.int32, (NOTE, HD), 0)
     rows = []
     guarded = []
@@ -284,17 +297,17 @@
         length = jnp.where(in_b, read(note_b, 1) * 16 + read(note_b, 2), length)
         rows.append((here | in_a | in_b, length))
         base = 2 * SPAN * row
-        whole = stage.at[pl.ds(base, 2 * SPAN)]
-        guarded.append((here, [
-            pltpu.make_async_copy(keys_ref.at[slot], stage.at[pl.ds(base, SPAN)], sem.at[row, 0]),
-            pltpu.make_async_copy(values_ref.at[slot], stage.at[pl.ds(base + SPAN, SPAN)], sem.at[row, 1]),
-        ]))
-        guarded.append((in_a, [
-            pltpu.make_async_copy((a1_ref, a2_ref)[row].at[pl.ds(0, 2 * SPAN)], whole, sem.at[row, 0])
-        ]))
-        guarded.append((in_b, [pltpu.make_async_copy(b_ref.at[pl.ds(base, 2 * SPAN)], whole, sem.at[row, 0])]))
+        for guard, from_keys, from_values in (
+            (here, keys_ref.at[slot], values_ref.at[slot]),
+            (in_a,) + along_a_places(row, a1_ref, a2_ref),
+            (in_b,) + along_b_places(row, b1_ref, b2_ref),
+        ):
+            guarded.append((guard, [
+                pltpu.make_async_copy(from_keys, stage.at[pl.ds(base, SPAN)], sem.at[row, 0]),
+                pltpu.make_async_copy(from_values, stage.at[pl.ds(base + SPAN, SPAN)], sem.at[row, 1]),
+            ]))
     start_guarded(guarded)
-    out_ref[...] = far_ref[:PARTIAL, :]
+    pack[...] = far_ref[:PARTIAL, :]
     wait_guarded(guarded)
     moves = []
     for row, (near, _) in enumerate(rows):
@@ -314,27 +327,29 @@
     for row, ((near, _), (peak, mass, partial)) in enumerate(zip(rows, results)):
         @pl.when(near)
         def _(row=row, peak=peak, mass=mass, partial=partial):
-            out_ref[row * QH:(row + 1) * QH, :] = partial
-            held = out_ref[STAT:PARTIAL, :].astype(jnp.float32)
-            out_ref[STAT:PARTIAL, :] = statistics(row, peak, mass, held).astype(jnp.bfloat16)
+            pack[row * QH:(row + 1) * QH, :] = partial
+            pack[STAT:PARTIAL, :] = jnp.where(mine(row), statistics(row, peak, mass), pack[STAT:PARTIAL, :])
+    for peer in range(TENSOR):
+        out_ref[peer] = pack[...]
     wait_guarded(moves)
 
 
-def attend(destination, lengths, queries, keys, values, a1, a2, b, far):
+def attend(destination, lengths, queries, keys, values, a1, a2, b1, b2, far):
     moved = jax.ShapeDtypeStruct((ROWS, SPAN, WIDE), jnp.bfloat16)
     return pl.pallas_call(
         attend_kernel,
-        out_shape=[jax.ShapeDtypeStruct((PARTIAL, HD), jnp.bfloat16), moved, moved],
-        in_specs=[SMEM, SMEM, VMEM, HBM, HBM, HBM, VMEM, VMEM, VMEM],
+        out_shape=[jax.ShapeDtypeStruct((TENSOR, PARTIAL, HD), jnp.bfloat16), moved, moved],
+        in_specs=[SMEM, SMEM, VMEM, HBM, HBM, HBM, VMEM, HBM, VMEM, VMEM],
         out_specs=[VMEM, HBM, HBM],
         scratch_shapes=[
             pltpu.VMEM((4 * SPAN, WIDE), jnp.bfloat16),
+            pltpu.VMEM((PARTIAL, HD), jnp.bfloat16),
             pltpu.SemaphoreType.DMA((ROWS, 2)),
             pltpu.SemaphoreType.DMA((ROWS, 2)),
         ],
         compiler_params=pltpu.CompilerParams(vmem_limit_bytes=PART),
-        cost_estimate=pl.CostEstimate(flops=2**34, bytes_accessed=2 * 2**20, transcendentals=2**14),
-    )(destination, lengths, queries, keys, values, a1, a2, b, far)
+        cost_estimate=pl.CostEstimate(flops=2**32, bytes_accessed=2 * 2**20, transcendentals=2**14),
+    )(destination, lengths, queries, keys, values, a1, a2, b1, b2, far)
 
 
 def finish_kernel(far_ref, blocks_ref, own_ref, own_values_ref, c1_ref, c2_ref, keys_in_ref, values_in_ref,
@@ -343,32 +358,37 @@
     note = far_ref[PARTIAL:, :].astype(jnp.float32)
     line = lax.broadcasted_iota(jnp.int32, (NOTE, HD), 0)
     guarded = []
-    for row, buffer in enumerate((c1_ref, c2_ref)):
+    for row in range(ROWS):
         told = jnp.max(jnp.where(line == row * 3, note, 0.0)).astype(jnp.int32)
+        from_keys, from_values = along_a_places(row, c1_ref, c2_ref)
         guarded.append((told == x * ROWS + row + 1, [
-            pltpu.make_async_copy(buffer.at[pl.ds(0, SPAN)], moved_keys_ref.at[row], sem.at[row, 0]),
-            pltpu.make_async_copy(buffer.at[pl.ds(SPAN, SPAN)], moved_values_ref.at[row], sem.at[row, 1]),
+            pltpu.make_async_copy(from_keys, moved_keys_ref.at[row], sem.at[row, 0]),
+            pltpu.make_async_copy(from_values, moved_values_ref.at[row], sem.at[row, 1]),
         ]))
     start_guarded(guarded)
-    column = lax.broadcasted_iota(jnp.int32, (QH, HD), 1)
-    own = jnp.where(column < 8, own_ref[0], own_ref[1])
-    joined = []
-    for b in range(TENSOR):
-        stats = blocks_ref[b, STAT:PARTIAL, :].astype(jnp.float32)
-        joined.append((stats + pltpu.roll(stats, HD - 1, 1)) + pltpu.roll(stats, HD - 2, 1))
-    top = functools.reduce(jnp.maximum, joined, own)
-    own_weight = jnp.exp(own - top)
-    fades = [jnp.exp(part - top) for part in joined]
-    denominator = own_weight
-    for part, fade in zip(joined, fades):
-        denominator = denominator + fade * pltpu.roll(part, HD - 3, 1)
+    stats = [blocks_ref[b, STAT:PARTIAL, :].astype(jnp.float32) for b in range(TENSOR)]
+    columns = []
+    for row in range(ROWS):
+        at = row * STATS
+        peaks = [(one[at:at + 1] + one[at + 1:at + 2]) + one[at + 2:at + 3] for one in stats]
+        masses = [(one[at + 3:at + 4] + one[at + 4:at + 5]) + one[at + 5:at + 6] for one in stats]
+        own = own_ref[row:row + 1, :]
+        top = functools.reduce(jnp.maximum, peaks, own)
+        fades = [jnp.exp(peak - top) for peak in peaks]
+        own_weight = jnp.exp(own - top)
+        denominator = own_weight
+        for fade, mass in zip(fades, masses):
+            denominator = denominator + fade * mass
+        columns += [one / denominator for one in fades + [own_weight]]
+    columns.append(jnp.zeros((HD - len(columns), HD), jnp.float32))
+    shares = jnp.transpose(jnp.concatenate(columns, axis=0))[:QH]
     parts = []
     for row in range(ROWS):
-        pick = slice(row * 8, row * 8 + 1)
-        total = own_weight[:, pick] * own_values_ref[row]
+        at = row * (TENSOR + 1)
+        total = shares[:, at + TENSOR:at + TENSOR + 1] * own_values_ref[row]
         for b in range(TENSOR):
-            total = total + fades[b][:, pick] * blocks_ref[b, row * QH:(row + 1) * QH, :].astype(jnp.float32)
-        parts.append(total / denominator[:, pick])
+            total = total + shares[:, at + b:at + b + 1] * blocks_ref[b, row * QH:(row + 1) * QH, :].astype(jnp.float32)
+        parts.append(total)
     for head in range(QH):
         both = jnp.concatenate([part[head:head + 1] for part in parts], axis=0)
         attended_ref[:, head * HD:(head + 1) * HD] = both.astype(jnp.bfloat16)
@@ -390,17 +410,18 @@
 
 
 def on_device(keys, values, lengths, destination, queries, new_keys, new_values):
-    asked = lax.ppermute(queries, "x", ASK_C)
-    a1, a2, b = gate(send_buffers(destination, lengths, keys, values), (asked,))
+    a1, a2, b1, b2, ask = send_buffers(destination, lengths, keys, values, queries)
+    asked = lax.ppermute(ask, "x", ASK_C)
     a1 = lax.ppermute(a1, "x", EDGE_A)
     a2 = lax.ppermute(a2, "x", EDGE_A)
-    b = lax.ppermute(b, "x", EDGE_B)
+    b1 = lax.ppermute(b1, "x", EDGE_B)
+    b2 = lax.ppermute(b2, "x", EDGE_B)
     far, own, own_values = early(destination, lengths, asked, queries, new_keys, new_values, keys, values)
     far = lax.ppermute(far, "x", EDGE_C)
     c1 = lax.ppermute(a1, "x", RELAY)
     c2 = lax.ppermute(a2, "x", RELAY)
-    partial, moved_keys, moved_values = attend(destination, lengths, queries, keys, values, a1, a2, b, far)
-    blocks = lax.all_gather(partial, "t")
+    partial, moved_keys, moved_values = attend(destination, lengths, queries, keys, values, a1, a2, b1, b2, far)
+    blocks = lax.all_to_all(partial, "t", 0, 0)
     attended, moved_keys, moved_values = finish(far, blocks, own, own_values, c1, c2, moved_keys, moved_values)
     return moved_keys, moved_values, attended
 

time: 61.5 us -> 56.9 us (0.925)
  blocking collectives: 18.1 us -> 0 us
  starting transfers between devices: 20.3 us -> 38.1 us
  waiting for transfers between devices: 12.8 us -> 9.34 us
  Pallas kernels: 8.29 us -> 7.66 us
    all_gather x1 -> x0, blocking collectives: 18.1 us -> none  [on_device(): blocks = lax.all_gather(partial, 't')]
    ppermute x1, waiting for transfers between devices: 8.76 us -> 0.01 us  [on_device(): a2 = lax.ppermute(a2, 'x', EDGE_A)]
    all_to_all x0 -> x1, starting transfers between devices: none -> 8.61 us  [on_device(): blocks = lax.all_to_all(partial, 't', 0, 0)]
    ppermute x1, starting transfers between devices: 3.28 us -> 8.6 us  [on_device(): c1 = lax.ppermute(a1, 'x', RELAY)]
    all_to_all x0 -> x1, waiting for transfers between devices: none -> 4.38 us  [on_device(): blocks = lax.all_to_all(partial, 't', 0, 0)]
    ppermute x2 -> x3, starting transfers between devices: 6.2 us -> 9.33 us  [the longest x1 7.94 us: on_device(): asked = lax.ppermute(ask, 'x', ASK_C)]
    ppermute x1, waiting for transfers between devices: 4.08 us -> 1.55 us  [on_device(): a1 = lax.ppermute(a1, 'x', EDGE_A)]
    ppermute x1, waiting for transfers between devices: 0.01 us -> 2.43 us  [on_device(): c2 = lax.ppermute(a2, 'x', RELAY)]
  transfers between devices with their start and end apart: 7 -> 9, of which waited for: 2 -> 4; matrix products, arithmetic and copies ran while one was open for 0% -> 0% of each run, Pallas kernels for 12% -> 7%
where the time goes in v3:
time: 56.9 us; the launch traced here: 56 us
  starting transfers between devices  38.1 us (67%)
  waiting for transfers between devices  9.34 us (16%)
  Pallas kernels  7.66 us (13%)
  between operations  0.85 us (1%)
    all_to_all x1, starting transfers between devices, on_device(): blocks = lax.all_to_all(partial, 't', 0, 0)  8.61 us
    ppermute x1, starting transfers between devices, on_device(): c1 = lax.ppermute(a1, 'x', RELAY)  8.6 us
    ppermute x1, starting transfers between devices, on_device(): asked = lax.ppermute(ask, 'x', ASK_C)  7.94 us
    all_to_all x1, waiting for transfers between devices, on_device(): blocks = lax.all_to_all(partial, 't', 0, 0)  4.38 us
    ppermute x1, starting transfers between devices, on_device(): a1 = lax.ppermute(a1, 'x', EDGE_A)  4.25 us
    ppermute x1, starting transfers between devices, on_device(): c2 = lax.ppermute(a2, 'x', RELAY)  4.07 us
    pallas_call x1, Pallas kernels, attend(): pl.pallas_call(attend_kernel, out_shape=[jax.ShapeDtypeStruct((TENSOR, PA...  3.15 us
    pallas_call x1, Pallas kernels, send_buffers(): pl.pallas_call(send_kernel, out_shape=[buffer(3 * SPAN), buffer(SPAN + NO...  2.64 us
  transfers between devices with their start and end apart: 9, of which 4 were waited for; matrix products, arithmetic and copies ran while one was open for 0% of the time, Pallas kernels for 7%

profile of v3, /device:TPU:1, one launch (start us, length us, event | category | flops | bytes accessed | tf_op | source)
XLA Modules:
  0.0 56.0 jit_solution(12077452142549995900)
XLA Ops:
  0.7 2.6 %shard_map.94 = (bf16[384,1024]{1,0:T(8,128)(2,1)}, bf16[144,1024]{1,0:T(8,128)(2,1)}, bf16[256,1024]{1,0:T(8,128)(2,1)}, bf16[272,1024]{1,0:T(8,128)(2,1)}, bf16[2,8192]{1,0:T(2,128)(2,1)}) custom-call(s32[4]{0:T(128)} %dest_ref.5, s32[4]{0:T(128)} %length_ref.5, bf16[4,128,1024]{2,1,0:T(8,128)(2,1)} %keys_ref.5, bf16[4,128,1024]{2,1,0:T(8,128)(2,1)} %values_ref.5, ...), custom_call_target="tpu_custom_call" | custom-call | bytes 4194304 | tf_op jit(solution)/shard_map/pallas_call | solution.py:122
  3.3 0.0 copy-start.6
  3.3 0.0 copy-start.5
  3.3 4.3 %collective-permute-start.2 = (bf16[384,1024]{1,0:T(8,128)(2,1)}, bf16[384,1024]{1,0:T(8,128)(2,1)S(1)}, u32[]{:S(2)}, u32[]{:S(2)}) collective-permute-start(bf16[384,1024]{1,0:T(8,128)(2,1)} %get-tuple-element.19), channel_id=1, source_target_pairs={{0,8},{8,0},{16,24},{24,16},{1,9},{9,1},{17,25},{25,17},{2,10},{10... | collective-permute-start | bytes 2359304 | tf_op jit(solution)/shard_map/ppermute | solution.py:415
  7.6 0.7 %collective-permute-start.5 = (bf16[272,1024]{1,0:T(8,128)(2,1)}, bf16[272,1024]{1,0:T(8,128)(2,1)S(1)}, u32[]{:S(2)}, u32[]{:S(2)}) collective-permute-start(bf16[272,1024]{1,0:T(8,128)(2,1)} %get-tuple-element.22), channel_id=1, source_target_pairs={{8,16},{16,8},{9,17},{17,9},{10,18},{18,10},{11,19},{19,11},{12,20... | collective-permute-start | bytes 1671176 | tf_op jit(solution)/shard_map/ppermute | solution.py:418
  8.3 0.7 %collective-permute-start.4 = (bf16[256,1024]{1,0:T(8,128)(2,1)}, bf16[256,1024]{1,0:T(8,128)(2,1)S(1)}, u32[]{:S(2)}, u32[]{:S(2)}) collective-permute-start(bf16[256,1024]{1,0:T(8,128)(2,1)} %get-tuple-element.21), channel_id=1, source_target_pairs={{8,16},{16,8},{9,17},{17,9},{10,18},{18,10},{11,19},{19,11},{12,20... | collective-permute-start | bytes 1572872 | tf_op jit(solution)/shard_map/ppermute | solution.py:417
  9.0 0.0 copy-start.3
  9.0 0.0 copy-start.4
  9.0 7.9 %collective-permute-start = (bf16[2,8192]{1,0:T(2,128)(2,1)}, bf16[2,8192]{1,0:T(2,128)(2,1)S(1)}, u32[]{:S(2)}, u32[]{:S(2)}) collective-permute-start(bf16[2,8192]{1,0:T(2,128)(2,1)} %get-tuple-element.17), channel_id=1, source_target_pairs={{24,8},{0,16},{25,9},{1,17},{26,10},{2,18},{27,11},{3,19},{28,12},... | collective-permute-start | bytes 98312 | tf_op jit(solution)/shard_map/ppermute | solution.py:414
  17.0 1.9 %collective-permute-start.3 = (bf16[144,1024]{1,0:T(8,128)(2,1)}, bf16[144,1024]{1,0:T(8,128)(2,1)}, u32[]{:S(2)}, u32[]{:S(2)}) collective-permute-start(bf16[144,1024]{1,0:T(8,128)(2,1)} %get-tuple-element.20), channel_id=1, source_target_pairs={{0,8},{8,0},{16,24},{24,16},{1,9},{9,1},{17,25},{25,17},{2,10},{10... | collective-permute-start | bytes 884744 | tf_op jit(solution)/shard_map/ppermute | solution.py:416
  18.9 1.5 %collective-permute-done.2.a1_ref = bf16[384,1024]{1,0:T(8,128)(2,1)S(1)} collective-permute-done((bf16[384,1024]{1,0:T(8,128)(2,1)}, bf16[384,1024]{1,0:T(8,128)(2,1)S(1)}, u32[]{:S(2)}, u32[]{:S(2)}) %collective-permute-start.2) | collective-permute-done | bytes 786464 | tf_op jit(solution)/shard_map/ppermute | solution.py:415
  20.5 8.6 %collective-permute-start.6 = (bf16[384,1024]{1,0:T(8,128)(2,1)S(1)}, bf16[384,1024]{1,0:T(8,128)(2,1)S(1)}, u32[]{:S(2)}, u32[]{:S(2)}) collective-permute-start(bf16[384,1024]{1,0:T(8,128)(2,1)S(1)} %collective-permute-done.2.a1_ref), channel_id=1, source_target_pairs={{0,24},{24,0},{1,25},{25,1},{2,26},{26,2},{3,27},{27,3},{4,28},{28... | collective-permute-start | bytes 2359304 | tf_op jit(solution)/shard_map/ppermute | solution.py:421
  29.1 0.0 collective-permute-done.asked_ref
  29.1 0.8 %shard_map.95 = (bf16[160,128]{1,0:T(8,128)(2,1)S(1)}, f32[8,128]{1,0:T(8,128)S(1)}, f32[2,64,128]{2,1,0:T(8,128)S(1)}) custom-call(s32[4]{0:T(128)S(1)} %copy-done.3, s32[4]{0:T(128)S(1)} %copy-done.4, bf16[2,8192]{1,0:T(2,128)(2,1)S(1)} %collective-permute-done.asked_ref, bf16[2,8192]{1,0:T(2,128)(2,1)S(1)} %copy-done.2, bf16[2,1024]{1,0:T(2,128)(2,1)S(1)} %copy-done.5, ...), custom_call_target="tpu_custom_call" | custom-call | flops 4294967296 | bytes 1048576 | tf_op jit(solution)/shard_map/pallas_call | solution.py:256
  29.9 1.3 %collective-permute-start.1 = (bf16[160,128]{1,0:T(8,128)(2,1)S(1)}, bf16[160,128]{1,0:T(8,128)(2,1)S(1)}, u32[]{:S(2)}, u32[]{:S(2)}) collective-permute-start(bf16[160,128]{1,0:T(8,128)(2,1)S(1)} %get-tuple-element.18), channel_id=1, source_target_pairs={{8,24},{16,0},{9,25},{17,1},{10,26},{18,2},{11,27},{19,3},{12,28},... | collective-permute-start | bytes 122888 | tf_op jit(solution)/shard_map/ppermute | solution.py:420
  31.2 0.0 collective-permute-done.3.a2_ref
  31.2 4.1 %collective-permute-start.7 = (bf16[144,1024]{1,0:T(8,128)(2,1)}, bf16[144,1024]{1,0:T(8,128)(2,1)S(1)}, u32[]{:S(2)}, u32[]{:S(2)}) collective-permute-start(bf16[144,1024]{1,0:T(8,128)(2,1)} %collective-permute-done.3.a2_ref), channel_id=1, source_target_pairs={{0,24},{24,0},{1,25},{25,1},{2,26},{26,2},{3,27},{27,3},{4,28},{28... | collective-permute-start | bytes 884744 | tf_op jit(solution)/shard_map/ppermute | solution.py:422
  35.3 1.0 %collective-permute-done.1.far_ref = bf16[160,128]{1,0:T(8,128)(2,1)S(1)} collective-permute-done((bf16[160,128]{1,0:T(8,128)(2,1)S(1)}, bf16[160,128]{1,0:T(8,128)(2,1)S(1)}, u32[]{:S(2)}, u32[]{:S(2)}) %collective-permute-start.1) | collective-permute-done | bytes 40992 | tf_op jit(solution)/shard_map/ppermute | solution.py:420
  36.3 0.0 collective-permute-done.4.b1_ref
  36.3 3.1 %shard_map.96 = (bf16[8,144,128]{2,1,0:T(8,128)(2,1)}, bf16[2,128,1024]{2,1,0:T(8,128)(2,1)}, bf16[2,128,1024]{2,1,0:T(8,128)(2,1)}) custom-call(s32[4]{0:T(128)S(1)} %copy-done.3, s32[4]{0:T(128)S(1)} %copy-done.4, bf16[2,8192]{1,0:T(2,128)(2,1)S(1)} %copy-done.2, bf16[4,128,1024]{2,1,0:T(8,128)(2,1)S(1)} %copy-done, bf16[4,128,1024]{2,1,0:T(8,128)(2,1)S(1)} %copy-done.1, ...), custom_call_target="tpu_custom_call" | custom-call | flops 4294967296 | bytes 2097152 | tf_op jit(solution)/shard_map/pallas_call | solution.py:339
  39.5 8.6 %all-to-all-start = ((bf16[8,144,128]{2,1,0:T(8,128)(2,1)}), bf16[8,144,128]{2,1,0:T(8,128)(2,1)S(1)}, u32[]{:S(2)}, u32[]{:S(2)}) async-start(bf16[8,144,128]{2,1,0:T(8,128)(2,1)} %get-tuple-element.23), calls=%async_computation | async-start | bytes 589824 | tf_op jit(solution)/shard_map/all_to_all | solution.py:424
  48.1 2.4 %collective-permute-done.7.c2_ref = bf16[144,1024]{1,0:T(8,128)(2,1)S(1)} collective-permute-done((bf16[144,1024]{1,0:T(8,128)(2,1)}, bf16[144,1024]{1,0:T(8,128)(2,1)S(1)}, u32[]{:S(2)}, u32[]{:S(2)}) %collective-permute-start.7) | collective-permute-done | bytes 294944 | tf_op jit(solution)/shard_map/ppermute | solution.py:422
  50.5 4.4 %all-to-all-done.blocks_ref = bf16[8,144,128]{2,1,0:T(8,128)(2,1)S(1)} async-done(((bf16[8,144,128]{2,1,0:T(8,128)(2,1)}), bf16[8,144,128]{2,1,0:T(8,128)(2,1)S(1)}, u32[]{:S(2)}, u32[]{:S(2)}) %all-to-all-start) | async-done | bytes 294944 | tf_op jit(solution)/shard_map/all_to_all | solution.py:424
  54.9 1.1 %shard_map.97 = (bf16[2,8192]{1,0:T(2,128)(2,1)}, bf16[2,128,1024]{2,1,0:T(8,128)(2,1)}, bf16[2,128,1024]{2,1,0:T(8,128)(2,1)}) custom-call(bf16[160,128]{1,0:T(8,128)(2,1)S(1)} %collective-permute-done.1.far_ref, bf16[8,144,128]{2,1,0:T(8,128)(2,1)S(1)} %all-to-all-done.blocks_ref, ...), custom_call_target="tpu_custom_call", output_to_operand_aliasing={{1}: (6, {}), {2}: (7, {})} | custom-call | flops 1048576 | bytes 1048576 | tf_op jit(solution)/shard_map/pallas_call | solution.py:400
  (12 shorter events, 0.0 us)
Async XLA Ops:
  0.6 28.4 %copy-start.2 = (bf16[2,8192]{1,0:T(2,128)(2,1)S(1)}, bf16[2,8192]{1,0:T(2,128)(2,1)}, u32[]{:S(2)}) copy-start(bf16[2,8192]{1,0:T(2,128)(2,1)} %queries_ref.5) | copy-start | bytes 98308
  0.6 28.4 %copy-start = (bf16[4,128,1024]{2,1,0:T(8,128)(2,1)S(1)}, bf16[4,128,1024]{2,1,0:T(8,128)(2,1)}, u32[]{:S(2)}) copy-start(bf16[4,128,1024]{2,1,0:T(8,128)(2,1)} %keys_ref.5) | copy-start | bytes 3145732
  0.7 28.4 %copy-start.1 = (bf16[4,128,1024]{2,1,0:T(8,128)(2,1)S(1)}, bf16[4,128,1024]{2,1,0:T(8,128)(2,1)}, u32[]{:S(2)}) copy-start(bf16[4,128,1024]{2,1,0:T(8,128)(2,1)} %values_ref.5) | copy-start | bytes 3145732
  3.3 25.8 %copy-start.6 = (bf16[2,1024]{1,0:T(2,128)(2,1)S(1)}, bf16[2,1024]{1,0:T(2,128)(2,1)}, u32[]{:S(2)}) copy-start(bf16[2,1024]{1,0:T(2,128)(2,1)} %new_values_ref.1) | copy-start | bytes 12292
  3.3 25.8 %copy-start.5 = (bf16[2,1024]{1,0:T(2,128)(2,1)S(1)}, bf16[2,1024]{1,0:T(2,128)(2,1)}, u32[]{:S(2)}) copy-start(bf16[2,1024]{1,0:T(2,128)(2,1)} %new_keys_ref.1) | copy-start | bytes 12292
  3.3 17.1 %collective-permute-start.2 = (bf16[384,1024]{1,0:T(8,128)(2,1)}, bf16[384,1024]{1,0:T(8,128)(2,1)S(1)}, u32[]{:S(2)}, u32[]{:S(2)}) collective-permute-start(bf16[384,1024]{1,0:T(8,128)(2,1)} %get-tuple-element.19), channel_id=1, source_target_pairs={{0,8},{8,0},{16,24},{24,16},{1,9},{9,1},{17,25},{25,17},{2,10},{10... | collective-permute-start | bytes 2359304 | tf_op jit(solution)/shard_map/ppermute | solution.py:415
  7.6 28.7 %collective-permute-start.5 = (bf16[272,1024]{1,0:T(8,128)(2,1)}, bf16[272,1024]{1,0:T(8,128)(2,1)S(1)}, u32[]{:S(2)}, u32[]{:S(2)}) collective-permute-start(bf16[272,1024]{1,0:T(8,128)(2,1)} %get-tuple-element.22), channel_id=1, source_target_pairs={{8,16},{16,8},{9,17},{17,9},{10,18},{18,10},{11,19},{19,11},{12,20... | collective-permute-start | bytes 1671176 | tf_op jit(solution)/shard_map/ppermute | solution.py:418
  8.3 28.0 %collective-permute-start.4 = (bf16[256,1024]{1,0:T(8,128)(2,1)}, bf16[256,1024]{1,0:T(8,128)(2,1)S(1)}, u32[]{:S(2)}, u32[]{:S(2)}) collective-permute-start(bf16[256,1024]{1,0:T(8,128)(2,1)} %get-tuple-element.21), channel_id=1, source_target_pairs={{8,16},{16,8},{9,17},{17,9},{10,18},{18,10},{11,19},{19,11},{12,20... | collective-permute-start | bytes 1572872 | tf_op jit(solution)/shard_map/ppermute | solution.py:417
  9.0 20.1 %copy-start.3 = (s32[4]{0:T(128)S(1)}, s32[4]{0:T(128)}, u32[]{:S(2)}) copy-start(s32[4]{0:T(128)} %dest_ref.5) | copy-start | bytes 52
  9.0 20.1 %copy-start.4 = (s32[4]{0:T(128)S(1)}, s32[4]{0:T(128)}, u32[]{:S(2)}) copy-start(s32[4]{0:T(128)} %length_ref.5) | copy-start | bytes 52
  9.0 20.0 %collective-permute-start = (bf16[2,8192]{1,0:T(2,128)(2,1)}, bf16[2,8192]{1,0:T(2,128)(2,1)S(1)}, u32[]{:S(2)}, u32[]{:S(2)}) collective-permute-start(bf16[2,8192]{1,0:T(2,128)(2,1)} %get-tuple-element.17), channel_id=1, source_target_pairs={{24,8},{0,16},{25,9},{1,17},{26,10},{2,18},{27,11},{3,19},{28,12},... | collective-permute-start | bytes 98312 | tf_op jit(solution)/shard_map/ppermute | solution.py:414
  17.0 14.3 %collective-permute-start.3 = (bf16[144,1024]{1,0:T(8,128)(2,1)}, bf16[144,1024]{1,0:T(8,128)(2,1)}, u32[]{:S(2)}, u32[]{:S(2)}) collective-permute-start(bf16[144,1024]{1,0:T(8,128)(2,1)} %get-tuple-element.20), channel_id=1, source_target_pairs={{0,8},{8,0},{16,24},{24,16},{1,9},{9,1},{17,25},{25,17},{2,10},{10... | collective-permute-start | bytes 884744 | tf_op jit(solution)/shard_map/ppermute | solution.py:416
  20.5 34.4 %collective-permute-start.6 = (bf16[384,1024]{1,0:T(8,128)(2,1)S(1)}, bf16[384,1024]{1,0:T(8,128)(2,1)S(1)}, u32[]{:S(2)}, u32[]{:S(2)}) collective-permute-start(bf16[384,1024]{1,0:T(8,128)(2,1)S(1)} %collective-permute-done.2.a1_ref), channel_id=1, source_target_pairs={{0,24},{24,0},{1,25},{25,1},{2,26},{26,2},{3,27},{27,3},{4,28},{28... | collective-permute-start | bytes 2359304 | tf_op jit(solution)/shard_map/ppermute | solution.py:421
  29.9 6.4 %collective-permute-start.1 = (bf16[160,128]{1,0:T(8,128)(2,1)S(1)}, bf16[160,128]{1,0:T(8,128)(2,1)S(1)}, u32[]{:S(2)}, u32[]{:S(2)}) collective-permute-start(bf16[160,128]{1,0:T(8,128)(2,1)S(1)} %get-tuple-element.18), channel_id=1, source_target_pairs={{8,24},{16,0},{9,25},{17,1},{10,26},{18,2},{11,27},{19,3},{12,28},... | collective-permute-start | bytes 122888 | tf_op jit(solution)/shard_map/ppermute | solution.py:420
  31.2 19.2 %collective-permute-start.7 = (bf16[144,1024]{1,0:T(8,128)(2,1)}, bf16[144,1024]{1,0:T(8,128)(2,1)S(1)}, u32[]{:S(2)}, u32[]{:S(2)}) collective-permute-start(bf16[144,1024]{1,0:T(8,128)(2,1)} %collective-permute-done.3.a2_ref), channel_id=1, source_target_pairs={{0,24},{24,0},{1,25},{25,1},{2,26},{26,2},{3,27},{27,3},{4,28},{28... | collective-permute-start | bytes 884744 | tf_op jit(solution)/shard_map/ppermute | solution.py:422
  39.5 15.4 %all-to-all-start = ((bf16[8,144,128]{2,1,0:T(8,128)(2,1)}), bf16[8,144,128]{2,1,0:T(8,128)(2,1)S(1)}, u32[]{:S(2)}, u32[]{:S(2)}) async-start(bf16[8,144,128]{2,1,0:T(8,128)(2,1)} %get-tuple-element.23), calls=%async_computation | async-start | bytes 589824 | tf_op jit(solution)/shard_map/all_to_all | solution.py:424

commit v4 on v3

--- a/solution.py
+++ b/solution.py
@@ -31,6 +31,8 @@
 RELAY = ((0, 3), (3, 0))
 ASK_C = ((3, 1), (0, 2))
 
+CUT = 64
+
 FULL = 60 * 2**20
 PART = 16 * 2**20
 
@@ -53,15 +55,19 @@
     return jnp.where(live, lax.shift_right_arithmetic(local, 1), -1), lax.bitwise_and(local, 1)
 
 
-def along_a_places(row, a1_ref, a2_ref):
+def along_a_pieces(row, a1_ref, a2_ref):
     if row == 0:
-        return a1_ref.at[pl.ds(0, SPAN)], a1_ref.at[pl.ds(SPAN, SPAN)]
-    return a1_ref.at[pl.ds(2 * SPAN, SPAN)], a2_ref.at[pl.ds(0, SPAN)]
-
-
-def along_b_places(row, b1_ref, b2_ref):
+        return [(0, 0, SPAN, a1_ref.at[pl.ds(0, SPAN)]), (1, 0, SPAN, a1_ref.at[pl.ds(SPAN, SPAN)])]
+    return [
+        (0, 0, CUT, a1_ref.at[pl.ds(2 * SPAN, CUT)]),
+        (0, CUT, SPAN - CUT, a2_ref.at[pl.ds(0, SPAN - CUT)]),
+        (1, 0, SPAN, a2_ref.at[pl.ds(SPAN - CUT, SPAN)]),
+    ]
+
+
+def along_b_pieces(row, b1_ref, b2_ref):
     buffer = (b1_ref, b2_ref)[row]
-    return buffer.at[pl.ds(0, SPAN)], buffer.at[pl.ds(SPAN, SPAN)]
+    return [(0, 0, SPAN, buffer.at[pl.ds(0, SPAN)]), (1, 0, SPAN, buffer.at[pl.ds(SPAN, SPAN)])]
 
 
 def send_kernel(dest_ref, length_ref, keys_ref, values_ref, queries_ref, a1_ref, a2_ref, b1_ref, b2_ref, ask_ref,
@@ -91,18 +97,18 @@
                 told[n] = jnp.where(line == base + k, value, told[n])
         for which in range(ROWS):
             mine = row == which
-            for guard, to_keys, to_values in (
-                (mine & along_a,) + along_a_places(which, a1_ref, a2_ref),
-                (mine & along_b,) + along_b_places(which, b1_ref, b2_ref),
+            for guard, parts in (
+                (mine & along_a, along_a_pieces(which, a1_ref, a2_ref)),
+                (mine & along_b, along_b_pieces(which, b1_ref, b2_ref)),
             ):
                 guarded.append((guard, slot, [
-                    pltpu.make_async_copy(keys.at[slot], to_keys, sem.at[slot, 0]),
-                    pltpu.make_async_copy(values.at[slot], to_values, sem.at[slot, 1]),
+                    pltpu.make_async_copy((keys, values)[n].at[slot].at[pl.ds(at, size)], place, sem.at[slot, i])
+                    for i, (n, at, size, place) in enumerate(parts)
                 ]))
     for n in range(2):
         note[n] = told[n].astype(jnp.float32).astype(jnp.bfloat16)
     notes = [
-        pltpu.make_async_copy(note.at[0], a2_ref.at[pl.ds(SPAN, NOTE)], note_sem.at[0]),
+        pltpu.make_async_copy(note.at[0], a2_ref.at[pl.ds(2 * SPAN - CUT, NOTE)], note_sem.at[0]),
         pltpu.make_async_copy(note.at[1], b2_ref.at[pl.ds(2 * SPAN, NOTE)], note_sem.at[1]),
     ]
     notes.append(pltpu.make_async_copy(queries_ref, ask_ref, note_sem.at[2]))
@@ -122,7 +128,7 @@
     return pl.pallas_call(
         send_kernel,
         out_shape=[
-            buffer(3 * SPAN), buffer(SPAN + NOTE), buffer(2 * SPAN), buffer(2 * SPAN + NOTE),
+            buffer(2 * SPAN + CUT), buffer(2 * SPAN - CUT + NOTE), buffer(2 * SPAN), buffer(2 * SPAN + NOTE),
             jax.ShapeDtypeStruct(queries.shape, queries.dtype),
         ],
         in_specs=[SMEM, SMEM, HBM, HBM, VMEM],
@@ -132,7 +138,7 @@
             pltpu.VMEM((SLOTS, SPAN, WIDE), jnp.bfloat16),
             pltpu.VMEM((2, NOTE, WIDE), jnp.bfloat16),
             pltpu.SemaphoreType.DMA((2, SLOTS)),
-            pltpu.SemaphoreType.DMA((SLOTS, 2)),
+            pltpu.SemaphoreType.DMA((SLOTS, 3)),
             pltpu.SemaphoreType.DMA((3,)),
         ],
         compiler_params=pltpu.CompilerParams(vmem_limit_bytes=FULL),
@@ -275,7 +281,7 @@
 def attend_kernel(dest_ref, length_ref, queries_ref, keys_ref, values_ref, a1_ref, a2_ref, b1_ref, b2_ref, far_ref,
                   out_ref, moved_keys_ref, moved_values_ref, stage, pack, sem, moved_sem):
     first, x = first_survivor(), replica_index()
-    note_a = a2_ref[SPAN:, :HD].astype(jnp.float32)
+    note_a = a2_ref[2 * SPAN - CUT:, :HD].astype(jnp.float32)
     note_b = b2_ref[2 * SPAN:, :HD].astype(jnp.float32)
     line = lax.broadcasted_iota(jnp.int32, (NOTE, HD), 0)
     rows = []
@@ -297,14 +303,14 @@
         length = jnp.where(in_b, read(note_b, 1) * 16 + read(note_b, 2), length)
         rows.append((here | in_a | in_b, length))
         base = 2 * SPAN * row
-        for guard, from_keys, from_values in (
-            (here, keys_ref.at[slot], values_ref.at[slot]),
-            (in_a,) + along_a_places(row, a1_ref, a2_ref),
-            (in_b,) + along_b_places(row, b1_ref, b2_ref),
+        for guard, parts in (
+            (here, [(0, 0, SPAN, keys_ref.at[slot]), (1, 0, SPAN, values_ref.at[slot])]),
+            (in_a, along_a_pieces(row, a1_ref, a2_ref)),
+            (in_b, along_b_pieces(row, b1_ref, b2_ref)),
         ):
             guarded.append((guard, [
-                pltpu.make_async_copy(from_keys, stage.at[pl.ds(base, SPAN)], sem.at[row, 0]),
-                pltpu.make_async_copy(from_values, stage.at[pl.ds(base + SPAN, SPAN)], sem.at[row, 1]),
+                pltpu.make_async_copy(place, stage.at[pl.ds(base + n * SPAN + at, size)], sem.at[row, i])
+                for i, (n, at, size, place) in enumerate(parts)
             ]))
     start_guarded(guarded)
     pack[...] = far_ref[:PARTIAL, :]
@@ -344,11 +350,11 @@
         scratch_shapes=[
             pltpu.VMEM((4 * SPAN, WIDE), jnp.bfloat16),
             pltpu.VMEM((PARTIAL, HD), jnp.bfloat16),
-            pltpu.SemaphoreType.DMA((ROWS, 2)),
+            pltpu.SemaphoreType.DMA((ROWS, 3)),
             pltpu.SemaphoreType.DMA((ROWS, 2)),
         ],
         compiler_params=pltpu.CompilerParams(vmem_limit_bytes=PART),
-        cost_estimate=pl.CostEstimate(flops=2**32, bytes_accessed=2 * 2**20, transcendentals=2**14),
+        cost_estimate=pl.CostEstimate(flops=2**31, bytes_accessed=2 * 2**20, transcendentals=2**14),
     )(destination, lengths, queries, keys, values, a1, a2, b1, b2, far)
 
 
@@ -360,10 +366,9 @@
     guarded = []
     for row in range(ROWS):
         told = jnp.max(jnp.where(line == row * 3, note, 0.0)).astype(jnp.int32)
-        from_keys, from_values = along_a_places(row, c1_ref, c2_ref)
         guarded.append((told == x * ROWS + row + 1, [
-            pltpu.make_async_copy(from_keys, moved_keys_ref.at[row], sem.at[row, 0]),
-            pltpu.make_async_copy(from_values, moved_values_ref.at[row], sem.at[row, 1]),
+            pltpu.make_async_copy(place, (moved_keys_ref, moved_values_ref)[n].at[row].at[pl.ds(at, size)], sem.at[row, i])
+            for i, (n, at, size, place) in enumerate(along_a_pieces(row, c1_ref, c2_ref))
         ]))
     start_guarded(guarded)
     stats = [blocks_ref[b, STAT:PARTIAL, :].astype(jnp.float32) for b in range(TENSOR)]
@@ -403,7 +408,7 @@
         in_specs=[VMEM] * 6 + [HBM] * 2,
         out_specs=[VMEM, HBM, HBM],
         input_output_aliases={6: 1, 7: 2},
-        scratch_shapes=[pltpu.SemaphoreType.DMA((ROWS, 2))],
+        scratch_shapes=[pltpu.SemaphoreType.DMA((ROWS, 3))],
         compiler_params=pltpu.CompilerParams(vmem_limit_bytes=PART),
         cost_estimate=pl.CostEstimate(flops=2**20, bytes_accessed=2**20, transcendentals=2**16),
     )(far, blocks, own, own_values, c1, c2, moved_keys, moved_values)

time: 56.9 us -> 54.4 us (0.956)
  starting transfers between devices: 38.1 us -> 36.6 us
  waiting for transfers between devices: 9.34 us -> 8.15 us
    ppermute x1, waiting for transfers between devices: 1.55 us -> 0.01 us  [on_device(): a1 = lax.ppermute(a1, 'x', EDGE_A)]
    ppermute x1, starting transfers between devices: 8.6 us -> 7.33 us  [on_device(): c1 = lax.ppermute(a1, 'x', RELAY)]
    ppermute x1, waiting for transfers between devices: 2.43 us -> 1.86 us  [on_device(): c2 = lax.ppermute(a2, 'x', RELAY)]
    all_to_all x1, waiting for transfers between devices: 4.38 us -> 4.95 us  [on_device(): blocks = lax.all_to_all(partial, 't', 0, 0)]
  transfers between devices with their start and end apart: 9 -> 9, of which waited for: 4 -> 4; matrix products, arithmetic and copies ran while one was open for 0% -> 0% of each run, Pallas kernels for 7% -> 8%
where the time goes in v4:
time: 54.4 us; the launch traced here: 53.8 us
  starting transfers between devices  36.6 us (67%)
  waiting for transfers between devices  8.15 us (15%)
  Pallas kernels  8.09 us (15%)
  between operations  0.85 us (2%)
    all_to_all x1, starting transfers between devices, on_device(): blocks = lax.all_to_all(partial, 't', 0, 0)  8.39 us
    ppermute x1, starting transfers between devices, on_device(): asked = lax.ppermute(ask, 'x', ASK_C)  7.77 us
    ppermute x1, starting transfers between devices, on_device(): c1 = lax.ppermute(a1, 'x', RELAY)  7.33 us
    all_to_all x1, waiting for transfers between devices, on_device(): blocks = lax.all_to_all(partial, 't', 0, 0)  4.95 us
    ppermute x1, starting transfers between devices, on_device(): a1 = lax.ppermute(a1, 'x', EDGE_A)  4.42 us
    ppermute x1, starting transfers between devices, on_device(): c2 = lax.ppermute(a2, 'x', RELAY)  4.12 us
    pallas_call x1, Pallas kernels, attend(): pl.pallas_call(attend_kernel, out_shape=[jax.ShapeDtypeStruct((TENSOR, PA...  3.53 us
    pallas_call x1, Pallas kernels, send_buffers(): pl.pallas_call(send_kernel, out_shape=[buffer(2 * SPAN + CUT), buffer(2 *...  2.68 us
  transfers between devices with their start and end apart: 9, of which 4 were waited for; matrix products, arithmetic and copies ran while one was open for 0% of the time, Pallas kernels for 8%

profile of v4, /device:TPU:1, one launch (start us, length us, event | category | flops | bytes accessed | tf_op | source)
XLA Modules:
  0.0 53.8 jit_solution(59765149095822429)
XLA Ops:
  0.7 2.7 %shard_map.94 = (bf16[320,1024]{1,0:T(8,128)(2,1)}, bf16[208,1024]{1,0:T(8,128)(2,1)}, bf16[256,1024]{1,0:T(8,128)(2,1)}, bf16[272,1024]{1,0:T(8,128)(2,1)}, bf16[2,8192]{1,0:T(2,128)(2,1)}) custom-call(s32[4]{0:T(128)} %dest_ref.5, s32[4]{0:T(128)} %length_ref.5, bf16[4,128,1024]{2,1,0:T(8,128)(2,1)} %keys_ref.5, bf16[4,128,1024]{2,1,0:T(8,128)(2,1)} %values_ref.5, ...), custom_call_target="tpu_custom_call" | custom-call | bytes 4194304 | tf_op jit(solution)/shard_map/pallas_call | solution.py:128
  3.3 0.0 copy-start.6
  3.4 0.0 copy-start.5
  3.4 4.4 %collective-permute-start.2 = (bf16[320,1024]{1,0:T(8,128)(2,1)}, bf16[320,1024]{1,0:T(8,128)(2,1)S(1)}, u32[]{:S(2)}, u32[]{:S(2)}) collective-permute-start(bf16[320,1024]{1,0:T(8,128)(2,1)} %get-tuple-element.19), channel_id=1, source_target_pairs={{0,8},{8,0},{16,24},{24,16},{1,9},{9,1},{17,25},{25,17},{2,10},{10... | collective-permute-start | bytes 1966088 | tf_op jit(solution)/shard_map/ppermute | solution.py:420
  7.8 0.7 %collective-permute-start.5 = (bf16[272,1024]{1,0:T(8,128)(2,1)}, bf16[272,1024]{1,0:T(8,128)(2,1)S(1)}, u32[]{:S(2)}, u32[]{:S(2)}) collective-permute-start(bf16[272,1024]{1,0:T(8,128)(2,1)} %get-tuple-element.22), channel_id=1, source_target_pairs={{8,16},{16,8},{9,17},{17,9},{10,18},{18,10},{11,19},{19,11},{12,20... | collective-permute-start | bytes 1671176 | tf_op jit(solution)/shard_map/ppermute | solution.py:423
  8.5 0.7 %collective-permute-start.4 = (bf16[256,1024]{1,0:T(8,128)(2,1)}, bf16[256,1024]{1,0:T(8,128)(2,1)S(1)}, u32[]{:S(2)}, u32[]{:S(2)}) collective-permute-start(bf16[256,1024]{1,0:T(8,128)(2,1)} %get-tuple-element.21), channel_id=1, source_target_pairs={{8,16},{16,8},{9,17},{17,9},{10,18},{18,10},{11,19},{19,11},{12,20... | collective-permute-start | bytes 1572872 | tf_op jit(solution)/shard_map/ppermute | solution.py:422
  9.2 0.0 copy-start.3
  9.2 0.0 copy-start.4
  9.2 7.8 %collective-permute-start = (bf16[2,8192]{1,0:T(2,128)(2,1)}, bf16[2,8192]{1,0:T(2,128)(2,1)S(1)}, u32[]{:S(2)}, u32[]{:S(2)}) collective-permute-start(bf16[2,8192]{1,0:T(2,128)(2,1)} %get-tuple-element.17), channel_id=1, source_target_pairs={{24,8},{0,16},{25,9},{1,17},{26,10},{2,18},{27,11},{3,19},{28,12},... | collective-permute-start | bytes 98312 | tf_op jit(solution)/shard_map/ppermute | solution.py:419
  17.0 1.9 %collective-permute-start.3 = (bf16[208,1024]{1,0:T(8,128)(2,1)}, bf16[208,1024]{1,0:T(8,128)(2,1)}, u32[]{:S(2)}, u32[]{:S(2)}) collective-permute-start(bf16[208,1024]{1,0:T(8,128)(2,1)} %get-tuple-element.20), channel_id=1, source_target_pairs={{0,8},{8,0},{16,24},{24,16},{1,9},{9,1},{17,25},{25,17},{2,10},{10... | collective-permute-start | bytes 1277960 | tf_op jit(solution)/shard_map/ppermute | solution.py:421
  18.9 0.0 collective-permute-done.2.a1_ref
  19.0 7.3 %collective-permute-start.6 = (bf16[320,1024]{1,0:T(8,128)(2,1)S(1)}, bf16[320,1024]{1,0:T(8,128)(2,1)S(1)}, u32[]{:S(2)}, u32[]{:S(2)}) collective-permute-start(bf16[320,1024]{1,0:T(8,128)(2,1)S(1)} %collective-permute-done.2.a1_ref), channel_id=1, source_target_pairs={{0,24},{24,0},{1,25},{25,1},{2,26},{26,2},{3,27},{27,3},{4,28},{28... | collective-permute-start | bytes 1966088 | tf_op jit(solution)/shard_map/ppermute | solution.py:426
  26.3 0.0 collective-permute-done.asked_ref
  26.4 0.8 %shard_map.95 = (bf16[160,128]{1,0:T(8,128)(2,1)S(1)}, f32[8,128]{1,0:T(8,128)S(1)}, f32[2,64,128]{2,1,0:T(8,128)S(1)}) custom-call(s32[4]{0:T(128)S(1)} %copy-done.3, s32[4]{0:T(128)S(1)} %copy-done.4, bf16[2,8192]{1,0:T(2,128)(2,1)S(1)} %collective-permute-done.asked_ref, bf16[2,8192]{1,0:T(2,128)(2,1)S(1)} %copy-done.2, bf16[2,1024]{1,0:T(2,128)(2,1)S(1)} %copy-done.5, ...), custom_call_target="tpu_custom_call" | custom-call | flops 4294967296 | bytes 1048576 | tf_op jit(solution)/shard_map/pallas_call | solution.py:262
  27.2 1.3 %collective-permute-start.1 = (bf16[160,128]{1,0:T(8,128)(2,1)S(1)}, bf16[160,128]{1,0:T(8,128)(2,1)S(1)}, u32[]{:S(2)}, u32[]{:S(2)}) collective-permute-start(bf16[160,128]{1,0:T(8,128)(2,1)S(1)} %get-tuple-element.18), channel_id=1, source_target_pairs={{8,24},{16,0},{9,25},{17,1},{10,26},{18,2},{11,27},{19,3},{12,28},... | collective-permute-start | bytes 122888 | tf_op jit(solution)/shard_map/ppermute | solution.py:425
  28.5 0.5 collective-permute-done.3.a2_ref
  28.9 4.1 %collective-permute-start.7 = (bf16[208,1024]{1,0:T(8,128)(2,1)}, bf16[208,1024]{1,0:T(8,128)(2,1)S(1)}, u32[]{:S(2)}, u32[]{:S(2)}) collective-permute-start(bf16[208,1024]{1,0:T(8,128)(2,1)} %collective-permute-done.3.a2_ref), channel_id=1, source_target_pairs={{0,24},{24,0},{1,25},{25,1},{2,26},{26,2},{3,27},{27,3},{4,28},{28... | collective-permute-start | bytes 1277960 | tf_op jit(solution)/shard_map/ppermute | solution.py:427
  33.1 0.9 %collective-permute-done.1.far_ref = bf16[160,128]{1,0:T(8,128)(2,1)S(1)} collective-permute-done((bf16[160,128]{1,0:T(8,128)(2,1)S(1)}, bf16[160,128]{1,0:T(8,128)(2,1)S(1)}, u32[]{:S(2)}, u32[]{:S(2)}) %collective-permute-start.1) | collective-permute-done | bytes 40992 | tf_op jit(solution)/shard_map/ppermute | solution.py:425
  33.9 0.0 collective-permute-done.4.b1_ref
  33.9 3.5 %shard_map.96 = (bf16[8,144,128]{2,1,0:T(8,128)(2,1)}, bf16[2,128,1024]{2,1,0:T(8,128)(2,1)}, bf16[2,128,1024]{2,1,0:T(8,128)(2,1)}) custom-call(s32[4]{0:T(128)S(1)} %copy-done.3, s32[4]{0:T(128)S(1)} %copy-done.4, bf16[2,8192]{1,0:T(2,128)(2,1)S(1)} %copy-done.2, bf16[4,128,1024]{2,1,0:T(8,128)(2,1)S(1)} %copy-done, bf16[4,128,1024]{2,1,0:T(8,128)(2,1)S(1)} %copy-done.1, ...), custom_call_target="tpu_custom_call" | custom-call | flops 2147483648 | bytes 2097152 | tf_op jit(solution)/shard_map/pallas_call | solution.py:345
  37.5 8.4 %all-to-all-start = ((bf16[8,144,128]{2,1,0:T(8,128)(2,1)}), bf16[8,144,128]{2,1,0:T(8,128)(2,1)S(1)}, u32[]{:S(2)}, u32[]{:S(2)}) async-start(bf16[8,144,128]{2,1,0:T(8,128)(2,1)} %get-tuple-element.23), calls=%async_computation | async-start | bytes 589824 | tf_op jit(solution)/shard_map/all_to_all | solution.py:429
  45.8 1.9 %collective-permute-done.7.c2_ref = bf16[208,1024]{1,0:T(8,128)(2,1)S(1)} collective-permute-done((bf16[208,1024]{1,0:T(8,128)(2,1)}, bf16[208,1024]{1,0:T(8,128)(2,1)S(1)}, u32[]{:S(2)}, u32[]{:S(2)}) %collective-permute-start.7) | collective-permute-done | bytes 426016 | tf_op jit(solution)/shard_map/ppermute | solution.py:427
  47.7 4.9 %all-to-all-done.blocks_ref = bf16[8,144,128]{2,1,0:T(8,128)(2,1)S(1)} async-done(((bf16[8,144,128]{2,1,0:T(8,128)(2,1)}), bf16[8,144,128]{2,1,0:T(8,128)(2,1)S(1)}, u32[]{:S(2)}, u32[]{:S(2)}) %all-to-all-start) | async-done | bytes 294944 | tf_op jit(solution)/shard_map/all_to_all | solution.py:429
  52.7 1.1 %shard_map.97 = (bf16[2,8192]{1,0:T(2,128)(2,1)}, bf16[2,128,1024]{2,1,0:T(8,128)(2,1)}, bf16[2,128,1024]{2,1,0:T(8,128)(2,1)}) custom-call(bf16[160,128]{1,0:T(8,128)(2,1)S(1)} %collective-permute-done.1.far_ref, bf16[8,144,128]{2,1,0:T(8,128)(2,1)S(1)} %all-to-all-done.blocks_ref, ...), custom_call_target="tpu_custom_call", output_to_operand_aliasing={{1}: (6, {}), {2}: (7, {})} | custom-call | flops 1048576 | bytes 1048576 | tf_op jit(solution)/shard_map/pallas_call | solution.py:405
  (12 shorter events, 0.0 us)
Async XLA Ops:
  0.6 25.7 %copy-start.2 = (bf16[2,8192]{1,0:T(2,128)(2,1)S(1)}, bf16[2,8192]{1,0:T(2,128)(2,1)}, u32[]{:S(2)}) copy-start(bf16[2,8192]{1,0:T(2,128)(2,1)} %queries_ref.5) | copy-start | bytes 98308
  0.6 25.7 %copy-start = (bf16[4,128,1024]{2,1,0:T(8,128)(2,1)S(1)}, bf16[4,128,1024]{2,1,0:T(8,128)(2,1)}, u32[]{:S(2)}) copy-start(bf16[4,128,1024]{2,1,0:T(8,128)(2,1)} %keys_ref.5) | copy-start | bytes 3145732
  0.7 25.7 %copy-start.1 = (bf16[4,128,1024]{2,1,0:T(8,128)(2,1)S(1)}, bf16[4,128,1024]{2,1,0:T(8,128)(2,1)}, u32[]{:S(2)}) copy-start(bf16[4,128,1024]{2,1,0:T(8,128)(2,1)} %values_ref.5) | copy-start | bytes 3145732
  3.3 23.0 %copy-start.6 = (bf16[2,1024]{1,0:T(2,128)(2,1)S(1)}, bf16[2,1024]{1,0:T(2,128)(2,1)}, u32[]{:S(2)}) copy-start(bf16[2,1024]{1,0:T(2,128)(2,1)} %new_values_ref.1) | copy-start | bytes 12292
  3.4 23.0 %copy-start.5 = (bf16[2,1024]{1,0:T(2,128)(2,1)S(1)}, bf16[2,1024]{1,0:T(2,128)(2,1)}, u32[]{:S(2)}) copy-start(bf16[2,1024]{1,0:T(2,128)(2,1)} %new_keys_ref.1) | copy-start | bytes 12292
  3.4 15.6 %collective-permute-start.2 = (bf16[320,1024]{1,0:T(8,128)(2,1)}, bf16[320,1024]{1,0:T(8,128)(2,1)S(1)}, u32[]{:S(2)}, u32[]{:S(2)}) collective-permute-start(bf16[320,1024]{1,0:T(8,128)(2,1)} %get-tuple-element.19), channel_id=1, source_target_pairs={{0,8},{8,0},{16,24},{24,16},{1,9},{9,1},{17,25},{25,17},{2,10},{10... | collective-permute-start | bytes 1966088 | tf_op jit(solution)/shard_map/ppermute | solution.py:420
  7.8 26.1 %collective-permute-start.5 = (bf16[272,1024]{1,0:T(8,128)(2,1)}, bf16[272,1024]{1,0:T(8,128)(2,1)S(1)}, u32[]{:S(2)}, u32[]{:S(2)}) collective-permute-start(bf16[272,1024]{1,0:T(8,128)(2,1)} %get-tuple-element.22), channel_id=1, source_target_pairs={{8,16},{16,8},{9,17},{17,9},{10,18},{18,10},{11,19},{19,11},{12,20... | collective-permute-start | bytes 1671176 | tf_op jit(solution)/shard_map/ppermute | solution.py:423
  8.5 25.4 %collective-permute-start.4 = (bf16[256,1024]{1,0:T(8,128)(2,1)}, bf16[256,1024]{1,0:T(8,128)(2,1)S(1)}, u32[]{:S(2)}, u32[]{:S(2)}) collective-permute-start(bf16[256,1024]{1,0:T(8,128)(2,1)} %get-tuple-element.21), channel_id=1, source_target_pairs={{8,16},{16,8},{9,17},{17,9},{10,18},{18,10},{11,19},{19,11},{12,20... | collective-permute-start | bytes 1572872 | tf_op jit(solution)/shard_map/ppermute | solution.py:422
  9.2 17.1 %copy-start.3 = (s32[4]{0:T(128)S(1)}, s32[4]{0:T(128)}, u32[]{:S(2)}) copy-start(s32[4]{0:T(128)} %dest_ref.5) | copy-start | bytes 52
  9.2 17.1 %copy-start.4 = (s32[4]{0:T(128)S(1)}, s32[4]{0:T(128)}, u32[]{:S(2)}) copy-start(s32[4]{0:T(128)} %length_ref.5) | copy-start | bytes 52
  9.2 17.1 %collective-permute-start = (bf16[2,8192]{1,0:T(2,128)(2,1)}, bf16[2,8192]{1,0:T(2,128)(2,1)S(1)}, u32[]{:S(2)}, u32[]{:S(2)}) collective-permute-start(bf16[2,8192]{1,0:T(2,128)(2,1)} %get-tuple-element.17), channel_id=1, source_target_pairs={{24,8},{0,16},{25,9},{1,17},{26,10},{2,18},{27,11},{3,19},{28,12},... | collective-permute-start | bytes 98312 | tf_op jit(solution)/shard_map/ppermute | solution.py:419
  17.0 11.9 %collective-permute-start.3 = (bf16[208,1024]{1,0:T(8,128)(2,1)}, bf16[208,1024]{1,0:T(8,128)(2,1)}, u32[]{:S(2)}, u32[]{:S(2)}) collective-permute-start(bf16[208,1024]{1,0:T(8,128)(2,1)} %get-tuple-element.20), channel_id=1, source_target_pairs={{0,8},{8,0},{16,24},{24,16},{1,9},{9,1},{17,25},{25,17},{2,10},{10... | collective-permute-start | bytes 1277960 | tf_op jit(solution)/shard_map/ppermute | solution.py:421
  19.0 33.7 %collective-permute-start.6 = (bf16[320,1024]{1,0:T(8,128)(2,1)S(1)}, bf16[320,1024]{1,0:T(8,128)(2,1)S(1)}, u32[]{:S(2)}, u32[]{:S(2)}) collective-permute-start(bf16[320,1024]{1,0:T(8,128)(2,1)S(1)} %collective-permute-done.2.a1_ref), channel_id=1, source_target_pairs={{0,24},{24,0},{1,25},{25,1},{2,26},{26,2},{3,27},{27,3},{4,28},{28... | collective-permute-start | bytes 1966088 | tf_op jit(solution)/shard_map/ppermute | solution.py:426
  27.2 6.8 %collective-permute-start.1 = (bf16[160,128]{1,0:T(8,128)(2,1)S(1)}, bf16[160,128]{1,0:T(8,128)(2,1)S(1)}, u32[]{:S(2)}, u32[]{:S(2)}) collective-permute-start(bf16[160,128]{1,0:T(8,128)(2,1)S(1)} %get-tuple-element.18), channel_id=1, source_target_pairs={{8,24},{16,0},{9,25},{17,1},{10,26},{18,2},{11,27},{19,3},{12,28},... | collective-permute-start | bytes 122888 | tf_op jit(solution)/shard_map/ppermute | solution.py:425
  28.9 18.8 %collective-permute-start.7 = (bf16[208,1024]{1,0:T(8,128)(2,1)}, bf16[208,1024]{1,0:T(8,128)(2,1)S(1)}, u32[]{:S(2)}, u32[]{:S(2)}) collective-permute-start(bf16[208,1024]{1,0:T(8,128)(2,1)} %collective-permute-done.3.a2_ref), channel_id=1, source_target_pairs={{0,24},{24,0},{1,25},{25,1},{2,26},{26,2},{3,27},{27,3},{4,28},{28... | collective-permute-start | bytes 1277960 | tf_op jit(solution)/shard_map/ppermute | solution.py:427
  37.5 15.2 %all-to-all-start = ((bf16[8,144,128]{2,1,0:T(8,128)(2,1)}), bf16[8,144,128]{2,1,0:T(8,128)(2,1)S(1)}, u32[]{:S(2)}, u32[]{:S(2)}) async-start(bf16[8,144,128]{2,1,0:T(8,128)(2,1)} %get-tuple-element.23), calls=%async_computation | async-start | bytes 589824 | tf_op jit(solution)/shard_map/all_to_all | solution.py:429

commit v5 on v4

--- a/solution.py
+++ b/solution.py
@@ -182,10 +182,10 @@
     return jnp.where((head // PER) == (lane // HD), wide, 0.0).astype(jnp.bfloat16)
 
 
-def block_attention(query, keys, values, length):
+def block_attention(spread, keys, values, length):
     position = lax.axis_index("t") * SPAN + lax.broadcasted_iota(jnp.int32, (QH, SPAN), 1)
     scores = lax.dot_general(
-        spread_heads(query), keys, (((1,), (1,)), ((), ())), preferred_element_type=jnp.float32
+        spread, keys, (((1,), (1,)), ((), ())), preferred_element_type=jnp.float32
     ) * SCALE
     valid = position < length
     peak = jnp.max(jnp.where(valid, scores, FLOOR), axis=1, keepdims=True)
@@ -253,7 +253,7 @@
     for row, (found, length) in enumerate(far):
         @pl.when(found >= 0)
         def _(row=row, length=length):
-            peak, mass, partial = block_attention(heads_of(asked_ref, row), keys[row], values[row], length)
+            peak, mass, partial = block_attention(spread_heads(heads_of(asked_ref, row)), keys[row], values[row], length)
             far_ref[row * QH:(row + 1) * QH, :] = partial
             far_ref[STAT:PARTIAL, :] = jnp.where(mine(row), statistics(row, peak, mass), far_ref[STAT:PARTIAL, :])
 
@@ -279,7 +279,7 @@
 
 
 def attend_kernel(dest_ref, length_ref, queries_ref, keys_ref, values_ref, a1_ref, a2_ref, b1_ref, b2_ref, far_ref,
-                  out_ref, moved_keys_ref, moved_values_ref, stage, pack, sem, moved_sem):
+                  out_ref, moved_keys_ref, moved_values_ref, stage, pack, spread, sem, moved_sem):
     first, x = first_survivor(), replica_index()
     note_a = a2_ref[2 * SPAN - CUT:, :HD].astype(jnp.float32)
     note_b = b2_ref[2 * SPAN:, :HD].astype(jnp.float32)
@@ -314,6 +314,8 @@
             ]))
     start_guarded(guarded)
     pack[...] = far_ref[:PARTIAL, :]
+    for row in range(ROWS):
+        spread[row] = spread_heads(heads_of(queries_ref, row))
     wait_guarded(guarded)
     moves = []
     for row, (near, _) in enumerate(rows):
@@ -325,7 +327,7 @@
     start_guarded(moves)
     results = [
         block_attention(
-            heads_of(queries_ref, row), stage[2 * SPAN * row:2 * SPAN * row + SPAN],
+            spread[row], stage[2 * SPAN * row:2 * SPAN * row + SPAN],
             stage[2 * SPAN * row + SPAN:2 * SPAN * (row + 1)], length,
         )
         for row, (_, length) in enumerate(rows)
@@ -350,6 +352,7 @@
         scratch_shapes=[
             pltpu.VMEM((4 * SPAN, WIDE), jnp.bfloat16),
             pltpu.VMEM((PARTIAL, HD), jnp.bfloat16),
+            pltpu.VMEM((ROWS, QH, WIDE), jnp.bfloat16),
             pltpu.SemaphoreType.DMA((ROWS, 3)),
             pltpu.SemaphoreType.DMA((ROWS, 2)),
         ],
@@ -358,8 +361,7 @@
     )(destination, lengths, queries, keys, values, a1, a2, b1, b2, far)
 
 
-def finish_kernel(far_ref, blocks_ref, own_ref, own_values_ref, c1_ref, c2_ref, keys_in_ref, values_in_ref,
-                  attended_ref, moved_keys_ref, moved_values_ref, sem):
+def relayed_kernel(far_ref, c1_ref, c2_ref, keys_in_ref, values_in_ref, moved_keys_ref, moved_values_ref, sem):
     x = replica_index()
     note = far_ref[PARTIAL:, :].astype(jnp.float32)
     line = lax.broadcasted_iota(jnp.int32, (NOTE, HD), 0)
@@ -371,6 +373,24 @@
             for i, (n, at, size, place) in enumerate(along_a_pieces(row, c1_ref, c2_ref))
         ]))
     start_guarded(guarded)
+    wait_guarded(guarded)
+
+
+def place_relayed(far, c1, c2, moved_keys, moved_values):
+    moved = jax.ShapeDtypeStruct((ROWS, SPAN, WIDE), jnp.bfloat16)
+    return pl.pallas_call(
+        relayed_kernel,
+        out_shape=[moved, moved],
+        in_specs=[VMEM] * 3 + [HBM] * 2,
+        out_specs=[HBM, HBM],
+        input_output_aliases={3: 0, 4: 1},
+        scratch_shapes=[pltpu.SemaphoreType.DMA((ROWS, 3))],
+        compiler_params=pltpu.CompilerParams(vmem_limit_bytes=PART),
+        cost_estimate=pl.CostEstimate(flops=0, bytes_accessed=2**20, transcendentals=0),
+    )(far, c1, c2, moved_keys, moved_values)
+
+
+def finish_kernel(blocks_ref, own_ref, own_values_ref, attended_ref):
     stats = [blocks_ref[b, STAT:PARTIAL, :].astype(jnp.float32) for b in range(TENSOR)]
     columns = []
     for row in range(ROWS):
@@ -397,21 +417,17 @@
     for head in range(QH):
         both = jnp.concatenate([part[head:head + 1] for part in parts], axis=0)
         attended_ref[:, head * HD:(head + 1) * HD] = both.astype(jnp.bfloat16)
-    wait_guarded(guarded)
-
-
-def finish(far, blocks, own, own_values, c1, c2, moved_keys, moved_values):
-    moved = jax.ShapeDtypeStruct((ROWS, SPAN, WIDE), jnp.bfloat16)
+
+
+def finish(blocks, own, own_values):
     return pl.pallas_call(
         finish_kernel,
-        out_shape=[jax.ShapeDtypeStruct((ROWS, QH * HD), jnp.bfloat16), moved, moved],
-        in_specs=[VMEM] * 6 + [HBM] * 2,
-        out_specs=[VMEM, HBM, HBM],
-        input_output_aliases={6: 1, 7: 2},
-        scratch_shapes=[pltpu.SemaphoreType.DMA((ROWS, 3))],
+        out_shape=jax.ShapeDtypeStruct((ROWS, QH * HD), jnp.bfloat16),
+        in_specs=[VMEM] * 3,
+        out_specs=VMEM,
         compiler_params=pltpu.CompilerParams(vmem_limit_bytes=PART),
         cost_estimate=pl.CostEstimate(flops=2**20, bytes_accessed=2**20, transcendentals=2**16),
-    )(far, blocks, own, own_values, c1, c2, moved_keys, moved_values)
+    )(blocks, own, own_values)
 
 
 def on_device(keys, values, lengths, destination, queries, new_keys, new_values):
@@ -427,7 +443,8 @@
     c2 = lax.ppermute(a2, "x", RELAY)
     partial, moved_keys, moved_values = attend(destination, lengths, queries, keys, values, a1, a2, b1, b2, far)
     blocks = lax.all_to_all(partial, "t", 0, 0)
-    attended, moved_keys, moved_values = finish(far, blocks, own, own_values, c1, c2, moved_keys, moved_values)
+    moved_keys, moved_values = place_relayed(far, c1, c2, moved_keys, moved_values)
+    attended = finish(blocks, own, own_values)
     return moved_keys, moved_values, attended
 
 

time: 54.4 us -> 53.6 us (0.985)
  blocking collectives: 0 us -> 15.4 us
  starting transfers between devices: 36.6 us -> 26.9 us
  waiting for transfers between devices: 8.15 us -> 2.36 us
    all_to_all x0 -> x1, blocking collectives: none -> 15.4 us  [on_device(): blocks = lax.all_to_all(partial, 't', 0, 0)]
    all_to_all x1 -> x0, starting transfers between devices: 8.39 us -> none  [on_device(): blocks = lax.all_to_all(partial, 't', 0, 0)]
    all_to_all x1 -> x0, waiting for transfers between devices: 4.95 us -> none  [on_device(): blocks = lax.all_to_all(partial, 't', 0, 0)]
    ppermute x1, waiting for transfers between devices: 1.86 us -> 0.01 us  [on_device(): c2 = lax.ppermute(a2, 'x', RELAY)]
    pallas_call x1, Pallas kernels: 3.53 us -> 2.09 us  [attend(): pl.pallas_call(attend_kernel, out_shape=[jax.ShapeDtypeStruct((TENSOR, PA...]
    ppermute x1, starting transfers between devices: 4.12 us -> 3.1 us  [on_device(): c2 = lax.ppermute(a2, 'x', RELAY)]
    ppermute x1, waiting for transfers between devices: 0.86 us -> 1.88 us  [on_device(): far = lax.ppermute(far, 'x', EDGE_C)]
    pallas_call x1, Pallas kernels: 2.68 us -> 3.48 us  [send_buffers(): pl.pallas_call(send_kernel, out_shape=[buffer(2 * SPAN + CUT), buffer(2 *...]
  transfers between devices with their start and end apart: 9 -> 8, of which waited for: 4 -> 2; matrix products, arithmetic and copies ran while one was open for 0% -> 0% of each run, Pallas kernels for 8% -> 7%
where the time goes in v5:
time: 53.6 us; the launch traced here: 53.1 us
  starting transfers between devices  26.9 us (50%)
  blocking collectives  15.4 us (29%)
  Pallas kernels  7.59 us (14%)
  waiting for transfers between devices  2.36 us (4%)
  between operations  0.85 us (2%)
    all_to_all x1, blocking collectives, on_device(): blocks = lax.all_to_all(partial, 't', 0, 0)  15.4 us
    ppermute x1, starting transfers between devices, on_device(): asked = lax.ppermute(ask, 'x', ASK_C)  7.92 us
    ppermute x1, starting transfers between devices, on_device(): c1 = lax.ppermute(a1, 'x', RELAY)  7.33 us
    ppermute x1, starting transfers between devices, on_device(): a1 = lax.ppermute(a1, 'x', EDGE_A)  3.94 us
    pallas_call x1, Pallas kernels, send_buffers(): pl.pallas_call(send_kernel, out_shape=[buffer(2 * SPAN + CUT), buffer(2 *...  3.48 us
    ppermute x1, starting transfers between devices, on_device(): c2 = lax.ppermute(a2, 'x', RELAY)  3.1 us
    pallas_call x1, Pallas kernels, attend(): pl.pallas_call(attend_kernel, out_shape=[jax.ShapeDtypeStruct((TENSOR, PA...  2.09 us
    ppermute x1, starting transfers between devices, on_device(): a2 = lax.ppermute(a2, 'x', EDGE_A)  1.92 us
  transfers between devices with their start and end apart: 8, of which 2 were waited for; matrix products, arithmetic and copies ran while one was open for 0% of the time, Pallas kernels for 7%

profile of v5, /device:TPU:1, one launch (start us, length us, event | category | flops | bytes accessed | tf_op | source)
XLA Modules:
  0.0 53.1 jit_solution(2398573729914998827)
XLA Ops:
  0.7 3.5 %shard_map.94 = (bf16[320,1024]{1,0:T(8,128)(2,1)}, bf16[208,1024]{1,0:T(8,128)(2,1)}, bf16[256,1024]{1,0:T(8,128)(2,1)}, bf16[272,1024]{1,0:T(8,128)(2,1)}, bf16[2,8192]{1,0:T(2,128)(2,1)}) custom-call(s32[4]{0:T(128)} %dest_ref.5, s32[4]{0:T(128)} %length_ref.5, bf16[4,128,1024]{2,1,0:T(8,128)(2,1)} %keys_ref.5, bf16[4,128,1024]{2,1,0:T(8,128)(2,1)} %values_ref.5, ...), custom_call_target="tpu_custom_call" | custom-call | bytes 4194304 | tf_op jit(solution)/shard_map/pallas_call | solution.py:128
  4.1 0.0 copy-start.6
  4.2 0.0 copy-start.5
  4.2 3.9 %collective-permute-start.2 = (bf16[320,1024]{1,0:T(8,128)(2,1)}, bf16[320,1024]{1,0:T(8,128)(2,1)S(1)}, u32[]{:S(2)}, u32[]{:S(2)}) collective-permute-start(bf16[320,1024]{1,0:T(8,128)(2,1)} %get-tuple-element.18), channel_id=1, source_target_pairs={{0,8},{8,0},{16,24},{24,16},{1,9},{9,1},{17,25},{25,17},{2,10},{10... | collective-permute-start | bytes 1966088 | tf_op jit(solution)/shard_map/ppermute | solution.py:436
  8.1 0.7 %collective-permute-start.7 = (bf16[272,1024]{1,0:T(8,128)(2,1)}, bf16[272,1024]{1,0:T(8,128)(2,1)S(1)}, u32[]{:S(2)}, u32[]{:S(2)}) collective-permute-start(bf16[272,1024]{1,0:T(8,128)(2,1)} %get-tuple-element.21), channel_id=1, source_target_pairs={{8,16},{16,8},{9,17},{17,9},{10,18},{18,10},{11,19},{19,11},{12,20... | collective-permute-start | bytes 1671176 | tf_op jit(solution)/shard_map/ppermute | solution.py:439
  8.8 0.7 %collective-permute-start.6 = (bf16[256,1024]{1,0:T(8,128)(2,1)}, bf16[256,1024]{1,0:T(8,128)(2,1)S(1)}, u32[]{:S(2)}, u32[]{:S(2)}) collective-permute-start(bf16[256,1024]{1,0:T(8,128)(2,1)} %get-tuple-element.20), channel_id=1, source_target_pairs={{8,16},{16,8},{9,17},{17,9},{10,18},{18,10},{11,19},{19,11},{12,20... | collective-permute-start | bytes 1572872 | tf_op jit(solution)/shard_map/ppermute | solution.py:438
  9.5 0.0 copy-start.3
  9.5 0.0 copy-start.4
  9.5 7.9 %collective-permute-start = (bf16[2,8192]{1,0:T(2,128)(2,1)}, bf16[2,8192]{1,0:T(2,128)(2,1)S(1)}, u32[]{:S(2)}, u32[]{:S(2)}) collective-permute-start(bf16[2,8192]{1,0:T(2,128)(2,1)} %get-tuple-element.16), channel_id=1, source_target_pairs={{24,8},{0,16},{25,9},{1,17},{26,10},{2,18},{27,11},{3,19},{28,12},... | collective-permute-start | bytes 98312 | tf_op jit(solution)/shard_map/ppermute | solution.py:435
  17.5 1.9 %collective-permute-start.4 = (bf16[208,1024]{1,0:T(8,128)(2,1)}, bf16[208,1024]{1,0:T(8,128)(2,1)S(1)}, u32[]{:S(2)}, u32[]{:S(2)}) collective-permute-start(bf16[208,1024]{1,0:T(8,128)(2,1)} %get-tuple-element.19), channel_id=1, source_target_pairs={{0,8},{8,0},{16,24},{24,16},{1,9},{9,1},{17,25},{25,17},{2,10},{10... | collective-permute-start | bytes 1277960 | tf_op jit(solution)/shard_map/ppermute | solution.py:437
  19.4 0.0 collective-permute-done.2.a1_ref
  19.4 7.3 %collective-permute-start.3 = (bf16[320,1024]{1,0:T(8,128)(2,1)S(1)}, bf16[320,1024]{1,0:T(8,128)(2,1)S(1)}, u32[]{:S(2)}, u32[]{:S(2)}) collective-permute-start(bf16[320,1024]{1,0:T(8,128)(2,1)S(1)} %collective-permute-done.2.a1_ref), channel_id=1, source_target_pairs={{0,24},{24,0},{1,25},{25,1},{2,26},{26,2},{3,27},{27,3},{4,28},{28... | collective-permute-start | bytes 1966088 | tf_op jit(solution)/shard_map/ppermute | solution.py:442
  26.7 0.0 collective-permute-done.asked_ref
  26.8 0.8 %shard_map.95 = (bf16[160,128]{1,0:T(8,128)(2,1)S(1)}, f32[8,128]{1,0:T(8,128)S(1)}, f32[2,64,128]{2,1,0:T(8,128)S(1)}) custom-call(s32[4]{0:T(128)S(1)} %copy-done.3, s32[4]{0:T(128)S(1)} %copy-done.4, bf16[2,8192]{1,0:T(2,128)(2,1)S(1)} %collective-permute-done.asked_ref, bf16[2,8192]{1,0:T(2,128)(2,1)S(1)} %copy-done.2, bf16[2,1024]{1,0:T(2,128)(2,1)S(1)} %copy-done.5, ...), custom_call_target="tpu_custom_call" | custom-call | flops 4294967296 | bytes 1048576 | tf_op jit(solution)/shard_map/pallas_call | solution.py:262
  27.6 1.3 %collective-permute-start.1 = (bf16[160,128]{1,0:T(8,128)(2,1)S(1)}, bf16[160,128]{1,0:T(8,128)(2,1)S(1)}, u32[]{:S(2)}, u32[]{:S(2)}) collective-permute-start(bf16[160,128]{1,0:T(8,128)(2,1)S(1)} %get-tuple-element.17), channel_id=1, source_target_pairs={{8,24},{16,0},{9,25},{17,1},{10,26},{18,2},{11,27},{19,3},{12,28},... | collective-permute-start | bytes 122888 | tf_op jit(solution)/shard_map/ppermute | solution.py:441
  28.9 0.5 collective-permute-done.4.a2_ref
  29.4 3.1 %collective-permute-start.5 = (bf16[208,1024]{1,0:T(8,128)(2,1)S(1)}, bf16[208,1024]{1,0:T(8,128)(2,1)S(1)}, u32[]{:S(2)}, u32[]{:S(2)}) collective-permute-start(bf16[208,1024]{1,0:T(8,128)(2,1)S(1)} %collective-permute-done.4.a2_ref), channel_id=1, source_target_pairs={{0,24},{24,0},{1,25},{25,1},{2,26},{26,2},{3,27},{27,3},{4,28},{28... | collective-permute-start | bytes 1277960 | tf_op jit(solution)/shard_map/ppermute | solution.py:443
  32.5 1.9 %collective-permute-done.1.far_ref = bf16[160,128]{1,0:T(8,128)(2,1)S(1)} collective-permute-done((bf16[160,128]{1,0:T(8,128)(2,1)S(1)}, bf16[160,128]{1,0:T(8,128)(2,1)S(1)}, u32[]{:S(2)}, u32[]{:S(2)}) %collective-permute-start.1) | collective-permute-done | bytes 40992 | tf_op jit(solution)/shard_map/ppermute | solution.py:441
  34.4 2.1 %shard_map.96 = (bf16[8,144,128]{2,1,0:T(8,128)(2,1)S(1)}, bf16[2,128,1024]{2,1,0:T(8,128)(2,1)}, bf16[2,128,1024]{2,1,0:T(8,128)(2,1)}) custom-call(s32[4]{0:T(128)S(1)} %copy-done.3, s32[4]{0:T(128)S(1)} %copy-done.4, bf16[2,8192]{1,0:T(2,128)(2,1)S(1)} %copy-done.2, bf16[4,128,1024]{2,1,0:T(8,128)(2,1)S(1)} %copy-done, ...), custom_call_target="tpu_custom_call" | custom-call | flops 2147483648 | bytes 2097152 | tf_op jit(solution)/shard_map/pallas_call | solution.py:347
  36.5 15.4 %all_to_all.5.blocks_ref = bf16[8,144,128]{2,1,0:T(8,128)(2,1)S(1)} all-to-all(bf16[8,144,128]{2,1,0:T(8,128)(2,1)S(1)} %get-tuple-element.26), channel_id=1, replica_groups=mesh['z'=16,'x'=4,'t'=8] {'t'}, dimensions={0} | all-to-all | bytes 589824 | tf_op jit(solution)/shard_map/all_to_all | solution.py:445
  51.9 1.0 %shard_map.98 = bf16[2,8192]{1,0:T(2,128)(2,1)} custom-call(bf16[8,144,128]{2,1,0:T(8,128)(2,1)S(1)} %all_to_all.5.blocks_ref, f32[8,128]{1,0:T(8,128)S(1)} %get-tuple-element.27.own_ref, f32[2,64,128]{2,1,0:T(8,128)S(1)} %get-tuple-element.28.own_values_ref), custom_call_target="tpu_custom_call" | custom-call | flops 1048576 | bytes 1048576 | tf_op jit(solution)/shard_map/pallas_call | solution.py:423
  52.9 0.0 collective-permute-done.5.c2_ref
  52.9 0.0 collective-permute-done.3.c1_ref
  52.9 0.2 shard_map.97
  (12 shorter events, 0.0 us)
Async XLA Ops:
  0.6 26.1 %copy-start.2 = (bf16[2,8192]{1,0:T(2,128)(2,1)S(1)}, bf16[2,8192]{1,0:T(2,128)(2,1)}, u32[]{:S(2)}) copy-start(bf16[2,8192]{1,0:T(2,128)(2,1)} %queries_ref.5) | copy-start | bytes 98308
  0.6 26.1 %copy-start = (bf16[4,128,1024]{2,1,0:T(8,128)(2,1)S(1)}, bf16[4,128,1024]{2,1,0:T(8,128)(2,1)}, u32[]{:S(2)}) copy-start(bf16[4,128,1024]{2,1,0:T(8,128)(2,1)} %keys_ref.5) | copy-start | bytes 3145732
  0.7 26.1 %copy-start.1 = (bf16[4,128,1024]{2,1,0:T(8,128)(2,1)S(1)}, bf16[4,128,1024]{2,1,0:T(8,128)(2,1)}, u32[]{:S(2)}) copy-start(bf16[4,128,1024]{2,1,0:T(8,128)(2,1)} %values_ref.5) | copy-start | bytes 3145732
  4.1 22.6 %copy-start.6 = (bf16[2,1024]{1,0:T(2,128)(2,1)S(1)}, bf16[2,1024]{1,0:T(2,128)(2,1)}, u32[]{:S(2)}) copy-start(bf16[2,1024]{1,0:T(2,128)(2,1)} %new_values_ref.1) | copy-start | bytes 12292
  4.2 22.6 %copy-start.5 = (bf16[2,1024]{1,0:T(2,128)(2,1)S(1)}, bf16[2,1024]{1,0:T(2,128)(2,1)}, u32[]{:S(2)}) copy-start(bf16[2,1024]{1,0:T(2,128)(2,1)} %new_keys_ref.1) | copy-start | bytes 12292
  4.2 15.2 %collective-permute-start.2 = (bf16[320,1024]{1,0:T(8,128)(2,1)}, bf16[320,1024]{1,0:T(8,128)(2,1)S(1)}, u32[]{:S(2)}, u32[]{:S(2)}) collective-permute-start(bf16[320,1024]{1,0:T(8,128)(2,1)} %get-tuple-element.18), channel_id=1, source_target_pairs={{0,8},{8,0},{16,24},{24,16},{1,9},{9,1},{17,25},{25,17},{2,10},{10... | collective-permute-start | bytes 1966088 | tf_op jit(solution)/shard_map/ppermute | solution.py:436
  8.1 26.3 %collective-permute-start.7 = (bf16[272,1024]{1,0:T(8,128)(2,1)}, bf16[272,1024]{1,0:T(8,128)(2,1)S(1)}, u32[]{:S(2)}, u32[]{:S(2)}) collective-permute-start(bf16[272,1024]{1,0:T(8,128)(2,1)} %get-tuple-element.21), channel_id=1, source_target_pairs={{8,16},{16,8},{9,17},{17,9},{10,18},{18,10},{11,19},{19,11},{12,20... | collective-permute-start | bytes 1671176 | tf_op jit(solution)/shard_map/ppermute | solution.py:439
  8.8 25.6 %collective-permute-start.6 = (bf16[256,1024]{1,0:T(8,128)(2,1)}, bf16[256,1024]{1,0:T(8,128)(2,1)S(1)}, u32[]{:S(2)}, u32[]{:S(2)}) collective-permute-start(bf16[256,1024]{1,0:T(8,128)(2,1)} %get-tuple-element.20), channel_id=1, source_target_pairs={{8,16},{16,8},{9,17},{17,9},{10,18},{18,10},{11,19},{19,11},{12,20... | collective-permute-start | bytes 1572872 | tf_op jit(solution)/shard_map/ppermute | solution.py:438
  9.5 17.3 %copy-start.3 = (s32[4]{0:T(128)S(1)}, s32[4]{0:T(128)}, u32[]{:S(2)}) copy-start(s32[4]{0:T(128)} %dest_ref.5) | copy-start | bytes 52
  9.5 17.3 %copy-start.4 = (s32[4]{0:T(128)S(1)}, s32[4]{0:T(128)}, u32[]{:S(2)}) copy-start(s32[4]{0:T(128)} %length_ref.5) | copy-start | bytes 52
  9.5 17.2 %collective-permute-start = (bf16[2,8192]{1,0:T(2,128)(2,1)}, bf16[2,8192]{1,0:T(2,128)(2,1)S(1)}, u32[]{:S(2)}, u32[]{:S(2)}) collective-permute-start(bf16[2,8192]{1,0:T(2,128)(2,1)} %get-tuple-element.16), channel_id=1, source_target_pairs={{24,8},{0,16},{25,9},{1,17},{26,10},{2,18},{27,11},{3,19},{28,12},... | collective-permute-start | bytes 98312 | tf_op jit(solution)/shard_map/ppermute | solution.py:435
  17.5 11.9 %collective-permute-start.4 = (bf16[208,1024]{1,0:T(8,128)(2,1)}, bf16[208,1024]{1,0:T(8,128)(2,1)S(1)}, u32[]{:S(2)}, u32[]{:S(2)}) collective-permute-start(bf16[208,1024]{1,0:T(8,128)(2,1)} %get-tuple-element.19), channel_id=1, source_target_pairs={{0,8},{8,0},{16,24},{24,16},{1,9},{9,1},{17,25},{25,17},{2,10},{10... | collective-permute-start | bytes 1277960 | tf_op jit(solution)/shard_map/ppermute | solution.py:437
  19.4 33.5 %collective-permute-start.3 = (bf16[320,1024]{1,0:T(8,128)(2,1)S(1)}, bf16[320,1024]{1,0:T(8,128)(2,1)S(1)}, u32[]{:S(2)}, u32[]{:S(2)}) collective-permute-start(bf16[320,1024]{1,0:T(8,128)(2,1)S(1)} %collective-permute-done.2.a1_ref), channel_id=1, source_target_pairs={{0,24},{24,0},{1,25},{25,1},{2,26},{26,2},{3,27},{27,3},{4,28},{28... | collective-permute-start | bytes 1966088 | tf_op jit(solution)/shard_map/ppermute | solution.py:442
  27.6 6.8 %collective-permute-start.1 = (bf16[160,128]{1,0:T(8,128)(2,1)S(1)}, bf16[160,128]{1,0:T(8,128)(2,1)S(1)}, u32[]{:S(2)}, u32[]{:S(2)}) collective-permute-start(bf16[160,128]{1,0:T(8,128)(2,1)S(1)} %get-tuple-element.17), channel_id=1, source_target_pairs={{8,24},{16,0},{9,25},{17,1},{10,26},{18,2},{11,27},{19,3},{12,28},... | collective-permute-start | bytes 122888 | tf_op jit(solution)/shard_map/ppermute | solution.py:441
  29.4 23.5 %collective-permute-start.5 = (bf16[208,1024]{1,0:T(8,128)(2,1)S(1)}, bf16[208,1024]{1,0:T(8,128)(2,1)S(1)}, u32[]{:S(2)}, u32[]{:S(2)}) collective-permute-start(bf16[208,1024]{1,0:T(8,128)(2,1)S(1)} %collective-permute-done.4.a2_ref), channel_id=1, source_target_pairs={{0,24},{24,0},{1,25},{25,1},{2,26},{26,2},{3,27},{27,3},{4,28},{28... | collective-permute-start | bytes 1277960 | tf_op jit(solution)/shard_map/ppermute | solution.py:443

commit v6 on v5

--- a/solution.py
+++ b/solution.py
@@ -79,9 +79,11 @@
             pltpu.make_async_copy(keys_ref.at[slot], keys.at[slot], load_sem.at[0, slot]),
             pltpu.make_async_copy(values_ref.at[slot], values.at[slot], load_sem.at[1, slot]),
         ))
-    for pair in loads:
-        for load in pair:
-            load.start()
+    leaves = []
+    for slot in range(SLOTS):
+        host, _ = places(dest_ref, slot, first)
+        leaves.append((host >= 0) & (host != x))
+    start_guarded(list(zip(leaves, loads)))
     line = lax.broadcasted_iota(jnp.int32, (NOTE, WIDE), 0)
     guarded = []
     told = [jnp.zeros((NOTE, WIDE), jnp.int32) for _ in range(2)]
@@ -115,8 +117,7 @@
     for copy in notes:
         copy.start()
     for slot in range(SLOTS):
-        for load in loads[slot]:
-            load.wait()
+        wait_guarded([(leaves[slot], loads[slot])])
         start_guarded([(guard, copies) for guard, owner, copies in guarded if owner == slot])
     wait_guarded([(guard, copies) for guard, _, copies in guarded])
     for copy in notes:

time: 53.6 us -> 53.3 us (level)
  starting transfers between devices: 26.9 us -> 30.3 us
  blocking collectives: 15.4 us -> 14 us
  Pallas kernels: 7.59 us -> 6.29 us
  waiting for transfers between devices: 2.36 us -> 1.2 us
    ppermute x1, starting transfers between devices: 3.1 us -> 5.71 us  [on_device(): c2 = lax.ppermute(a2, 'x', RELAY)]
    ppermute x1, waiting for transfers between devices: 1.88 us -> 0.01 us  [on_device(): far = lax.ppermute(far, 'x', EDGE_C)]
    pallas_call x1, Pallas kernels: 3.48 us -> 1.83 us  [send_buffers(): pl.pallas_call(send_kernel, out_shape=[buffer(2 * SPAN + CUT), buffer(2 *...]
    all_to_all x1, blocking collectives: 15.4 us -> 14 us  [on_device(): blocks = lax.all_to_all(partial, 't', 0, 0)]
    ppermute x1, starting transfers between devices: 3.94 us -> 5.29 us  [on_device(): a1 = lax.ppermute(a1, 'x', EDGE_A)]
    ppermute x1, starting transfers between devices: 7.92 us -> 7.36 us  [on_device(): asked = lax.ppermute(ask, 'x', ASK_C)]
  transfers between devices with their start and end apart: 8 -> 8, of which waited for: 2 -> 2; matrix products, arithmetic and copies ran while one was open for 0% -> 0% of each run, Pallas kernels for 7% -> 8%
where the time goes in v6:
time: 53.3 us; the launch traced here: 52.6 us
  starting transfers between devices  30.3 us (57%)
  blocking collectives  14 us (26%)
  Pallas kernels  6.29 us (12%)
  waiting for transfers between devices  1.2 us (2%)
  between operations  0.86 us (2%)
    all_to_all x1, blocking collectives, on_device(): blocks = lax.all_to_all(partial, 't', 0, 0)  14 us
    ppermute x1, starting transfers between devices, on_device(): asked = lax.ppermute(ask, 'x', ASK_C)  7.36 us
    ppermute x1, starting transfers between devices, on_device(): c1 = lax.ppermute(a1, 'x', RELAY)  7.3 us
    ppermute x1, starting transfers between devices, on_device(): c2 = lax.ppermute(a2, 'x', RELAY)  5.71 us
    ppermute x1, starting transfers between devices, on_device(): a1 = lax.ppermute(a1, 'x', EDGE_A)  5.29 us
    pallas_call x1, Pallas kernels, attend(): pl.pallas_call(attend_kernel, out_shape=[jax.ShapeDtypeStruct((TENSOR, PA...  2.44 us
    ppermute x1, starting transfers between devices, on_device(): a2 = lax.ppermute(a2, 'x', EDGE_A)  1.92 us
    pallas_call x1, Pallas kernels, send_buffers(): pl.pallas_call(send_kernel, out_shape=[buffer(2 * SPAN + CUT), buffer(2 *...  1.83 us
  transfers between devices with their start and end apart: 8, of which 2 were waited for; matrix products, arithmetic and copies ran while one was open for 0% of the time, Pallas kernels for 8%

profile of v6, /device:TPU:1, one launch (start us, length us, event | category | flops | bytes accessed | tf_op | source)
XLA Modules:
  0.0 52.6 jit_solution(14234018072101559758)
XLA Ops:
  0.7 1.8 %shard_map.94 = (bf16[320,1024]{1,0:T(8,128)(2,1)}, bf16[208,1024]{1,0:T(8,128)(2,1)}, bf16[256,1024]{1,0:T(8,128)(2,1)}, bf16[272,1024]{1,0:T(8,128)(2,1)}, bf16[2,8192]{1,0:T(2,128)(2,1)}) custom-call(s32[4]{0:T(128)} %dest_ref.5, s32[4]{0:T(128)} %length_ref.5, bf16[4,128,1024]{2,1,0:T(8,128)(2,1)} %keys_ref.5, bf16[4,128,1024]{2,1,0:T(8,128)(2,1)} %values_ref.5, ...), custom_call_target="tpu_custom_call" | custom-call | bytes 4194304 | tf_op jit(solution)/shard_map/pallas_call | solution.py:129
  2.5 0.0 copy-start.6
  2.5 0.0 copy-start.5
  2.5 5.3 %collective-permute-start.2 = (bf16[320,1024]{1,0:T(8,128)(2,1)}, bf16[320,1024]{1,0:T(8,128)(2,1)S(1)}, u32[]{:S(2)}, u32[]{:S(2)}) collective-permute-start(bf16[320,1024]{1,0:T(8,128)(2,1)} %get-tuple-element.18), channel_id=1, source_target_pairs={{0,8},{8,0},{16,24},{24,16},{1,9},{9,1},{17,25},{25,17},{2,10},{10... | collective-permute-start | bytes 1966088 | tf_op jit(solution)/shard_map/ppermute | solution.py:437
  7.8 0.7 %collective-permute-start.7 = (bf16[272,1024]{1,0:T(8,128)(2,1)}, bf16[272,1024]{1,0:T(8,128)(2,1)S(1)}, u32[]{:S(2)}, u32[]{:S(2)}) collective-permute-start(bf16[272,1024]{1,0:T(8,128)(2,1)} %get-tuple-element.21), channel_id=1, source_target_pairs={{8,16},{16,8},{9,17},{17,9},{10,18},{18,10},{11,19},{19,11},{12,20... | collective-permute-start | bytes 1671176 | tf_op jit(solution)/shard_map/ppermute | solution.py:440
  8.5 0.7 %collective-permute-start.6 = (bf16[256,1024]{1,0:T(8,128)(2,1)}, bf16[256,1024]{1,0:T(8,128)(2,1)S(1)}, u32[]{:S(2)}, u32[]{:S(2)}) collective-permute-start(bf16[256,1024]{1,0:T(8,128)(2,1)} %get-tuple-element.20), channel_id=1, source_target_pairs={{8,16},{16,8},{9,17},{17,9},{10,18},{18,10},{11,19},{19,11},{12,20... | collective-permute-start | bytes 1572872 | tf_op jit(solution)/shard_map/ppermute | solution.py:439
  9.2 0.0 copy-start.3
  9.2 0.0 copy-start.4
  9.2 7.4 %collective-permute-start = (bf16[2,8192]{1,0:T(2,128)(2,1)}, bf16[2,8192]{1,0:T(2,128)(2,1)S(1)}, u32[]{:S(2)}, u32[]{:S(2)}) collective-permute-start(bf16[2,8192]{1,0:T(2,128)(2,1)} %get-tuple-element.16), channel_id=1, source_target_pairs={{24,8},{0,16},{25,9},{1,17},{26,10},{2,18},{27,11},{3,19},{28,12},... | collective-permute-start | bytes 98312 | tf_op jit(solution)/shard_map/ppermute | solution.py:436
  16.6 1.9 %collective-permute-start.4 = (bf16[208,1024]{1,0:T(8,128)(2,1)}, bf16[208,1024]{1,0:T(8,128)(2,1)S(1)}, u32[]{:S(2)}, u32[]{:S(2)}) collective-permute-start(bf16[208,1024]{1,0:T(8,128)(2,1)} %get-tuple-element.19), channel_id=1, source_target_pairs={{0,8},{8,0},{16,24},{24,16},{1,9},{9,1},{17,25},{25,17},{2,10},{10... | collective-permute-start | bytes 1277960 | tf_op jit(solution)/shard_map/ppermute | solution.py:438
  18.5 0.4 collective-permute-done.2.a1_ref
  18.9 7.3 %collective-permute-start.3 = (bf16[320,1024]{1,0:T(8,128)(2,1)S(1)}, bf16[320,1024]{1,0:T(8,128)(2,1)S(1)}, u32[]{:S(2)}, u32[]{:S(2)}) collective-permute-start(bf16[320,1024]{1,0:T(8,128)(2,1)S(1)} %collective-permute-done.2.a1_ref), channel_id=1, source_target_pairs={{0,24},{24,0},{1,25},{25,1},{2,26},{26,2},{3,27},{27,3},{4,28},{28... | collective-permute-start | bytes 1966088 | tf_op jit(solution)/shard_map/ppermute | solution.py:443
  26.3 0.8 %shard_map.95 = (bf16[160,128]{1,0:T(8,128)(2,1)S(1)}, f32[8,128]{1,0:T(8,128)S(1)}, f32[2,64,128]{2,1,0:T(8,128)S(1)}) custom-call(s32[4]{0:T(128)S(1)} %copy-done.3, s32[4]{0:T(128)S(1)} %copy-done.4, bf16[2,8192]{1,0:T(2,128)(2,1)S(1)} %collective-permute-done.asked_ref, bf16[2,8192]{1,0:T(2,128)(2,1)S(1)} %copy-done.2, bf16[2,1024]{1,0:T(2,128)(2,1)S(1)} %copy-done.5, ...), custom_call_target="tpu_custom_call" | custom-call | flops 4294967296 | bytes 1048576 | tf_op jit(solution)/shard_map/pallas_call | solution.py:263
  27.1 1.3 %collective-permute-start.1 = (bf16[160,128]{1,0:T(8,128)(2,1)S(1)}, bf16[160,128]{1,0:T(8,128)(2,1)S(1)}, u32[]{:S(2)}, u32[]{:S(2)}) collective-permute-start(bf16[160,128]{1,0:T(8,128)(2,1)S(1)} %get-tuple-element.17), channel_id=1, source_target_pairs={{8,24},{16,0},{9,25},{17,1},{10,26},{18,2},{11,27},{19,3},{12,28},... | collective-permute-start | bytes 122888 | tf_op jit(solution)/shard_map/ppermute | solution.py:442
  28.4 0.8 %collective-permute-done.4.a2_ref = bf16[208,1024]{1,0:T(8,128)(2,1)S(1)} collective-permute-done((bf16[208,1024]{1,0:T(8,128)(2,1)}, bf16[208,1024]{1,0:T(8,128)(2,1)S(1)}, u32[]{:S(2)}, u32[]{:S(2)}) %collective-permute-start.4) | collective-permute-done | bytes 426016 | tf_op jit(solution)/shard_map/ppermute | solution.py:438
  29.2 5.7 %collective-permute-start.5 = (bf16[208,1024]{1,0:T(8,128)(2,1)S(1)}, bf16[208,1024]{1,0:T(8,128)(2,1)S(1)}, u32[]{:S(2)}, u32[]{:S(2)}) collective-permute-start(bf16[208,1024]{1,0:T(8,128)(2,1)S(1)} %collective-permute-done.4.a2_ref), channel_id=1, source_target_pairs={{0,24},{24,0},{1,25},{25,1},{2,26},{26,2},{3,27},{27,3},{4,28},{28... | collective-permute-start | bytes 1277960 | tf_op jit(solution)/shard_map/ppermute | solution.py:444
  34.9 0.0 collective-permute-done.6.b1_ref
  34.9 0.0 collective-permute-done.7.b2_ref
  34.9 2.4 %shard_map.96 = (bf16[8,144,128]{2,1,0:T(8,128)(2,1)S(1)}, bf16[2,128,1024]{2,1,0:T(8,128)(2,1)}, bf16[2,128,1024]{2,1,0:T(8,128)(2,1)}) custom-call(s32[4]{0:T(128)S(1)} %copy-done.3, s32[4]{0:T(128)S(1)} %copy-done.4, bf16[2,8192]{1,0:T(2,128)(2,1)S(1)} %copy-done.2, bf16[4,128,1024]{2,1,0:T(8,128)(2,1)S(1)} %copy-done, ...), custom_call_target="tpu_custom_call" | custom-call | flops 2147483648 | bytes 2097152 | tf_op jit(solution)/shard_map/pallas_call | solution.py:348
  37.4 14.0 %all_to_all.5.blocks_ref = bf16[8,144,128]{2,1,0:T(8,128)(2,1)S(1)} all-to-all(bf16[8,144,128]{2,1,0:T(8,128)(2,1)S(1)} %get-tuple-element.26), channel_id=1, replica_groups=mesh['z'=16,'x'=4,'t'=8] {'t'}, dimensions={0} | all-to-all | bytes 589824 | tf_op jit(solution)/shard_map/all_to_all | solution.py:446
  51.4 1.0 %shard_map.98 = bf16[2,8192]{1,0:T(2,128)(2,1)} custom-call(bf16[8,144,128]{2,1,0:T(8,128)(2,1)S(1)} %all_to_all.5.blocks_ref, f32[8,128]{1,0:T(8,128)S(1)} %get-tuple-element.27.own_ref, f32[2,64,128]{2,1,0:T(8,128)S(1)} %get-tuple-element.28.own_values_ref), custom_call_target="tpu_custom_call" | custom-call | flops 1048576 | bytes 1048576 | tf_op jit(solution)/shard_map/pallas_call | solution.py:424
  52.4 0.0 collective-permute-done.5.c2_ref
  52.4 0.0 collective-permute-done.3.c1_ref
  52.4 0.2 shard_map.97
  (12 shorter events, 0.0 us)
Async XLA Ops:
  0.6 25.6 %copy-start.2 = (bf16[2,8192]{1,0:T(2,128)(2,1)S(1)}, bf16[2,8192]{1,0:T(2,128)(2,1)}, u32[]{:S(2)}) copy-start(bf16[2,8192]{1,0:T(2,128)(2,1)} %queries_ref.5) | copy-start | bytes 98308
  0.6 25.6 %copy-start = (bf16[4,128,1024]{2,1,0:T(8,128)(2,1)S(1)}, bf16[4,128,1024]{2,1,0:T(8,128)(2,1)}, u32[]{:S(2)}) copy-start(bf16[4,128,1024]{2,1,0:T(8,128)(2,1)} %keys_ref.5) | copy-start | bytes 3145732
  0.7 25.6 %copy-start.1 = (bf16[4,128,1024]{2,1,0:T(8,128)(2,1)S(1)}, bf16[4,128,1024]{2,1,0:T(8,128)(2,1)}, u32[]{:S(2)}) copy-start(bf16[4,128,1024]{2,1,0:T(8,128)(2,1)} %values_ref.5) | copy-start | bytes 3145732
  2.5 23.8 %copy-start.6 = (bf16[2,1024]{1,0:T(2,128)(2,1)S(1)}, bf16[2,1024]{1,0:T(2,128)(2,1)}, u32[]{:S(2)}) copy-start(bf16[2,1024]{1,0:T(2,128)(2,1)} %new_values_ref.1) | copy-start | bytes 12292
  2.5 23.8 %copy-start.5 = (bf16[2,1024]{1,0:T(2,128)(2,1)S(1)}, bf16[2,1024]{1,0:T(2,128)(2,1)}, u32[]{:S(2)}) copy-start(bf16[2,1024]{1,0:T(2,128)(2,1)} %new_keys_ref.1) | copy-start | bytes 12292
  2.5 16.4 %collective-permute-start.2 = (bf16[320,1024]{1,0:T(8,128)(2,1)}, bf16[320,1024]{1,0:T(8,128)(2,1)S(1)}, u32[]{:S(2)}, u32[]{:S(2)}) collective-permute-start(bf16[320,1024]{1,0:T(8,128)(2,1)} %get-tuple-element.18), channel_id=1, source_target_pairs={{0,8},{8,0},{16,24},{24,16},{1,9},{9,1},{17,25},{25,17},{2,10},{10... | collective-permute-start | bytes 1966088 | tf_op jit(solution)/shard_map/ppermute | solution.py:437
  7.8 27.1 %collective-permute-start.7 = (bf16[272,1024]{1,0:T(8,128)(2,1)}, bf16[272,1024]{1,0:T(8,128)(2,1)S(1)}, u32[]{:S(2)}, u32[]{:S(2)}) collective-permute-start(bf16[272,1024]{1,0:T(8,128)(2,1)} %get-tuple-element.21), channel_id=1, source_target_pairs={{8,16},{16,8},{9,17},{17,9},{10,18},{18,10},{11,19},{19,11},{12,20... | collective-permute-start | bytes 1671176 | tf_op jit(solution)/shard_map/ppermute | solution.py:440
  8.5 26.4 %collective-permute-start.6 = (bf16[256,1024]{1,0:T(8,128)(2,1)}, bf16[256,1024]{1,0:T(8,128)(2,1)S(1)}, u32[]{:S(2)}, u32[]{:S(2)}) collective-permute-start(bf16[256,1024]{1,0:T(8,128)(2,1)} %get-tuple-element.20), channel_id=1, source_target_pairs={{8,16},{16,8},{9,17},{17,9},{10,18},{18,10},{11,19},{19,11},{12,20... | collective-permute-start | bytes 1572872 | tf_op jit(solution)/shard_map/ppermute | solution.py:439
  9.2 17.0 %copy-start.3 = (s32[4]{0:T(128)S(1)}, s32[4]{0:T(128)}, u32[]{:S(2)}) copy-start(s32[4]{0:T(128)} %dest_ref.5) | copy-start | bytes 52
  9.2 17.0 %copy-start.4 = (s32[4]{0:T(128)S(1)}, s32[4]{0:T(128)}, u32[]{:S(2)}) copy-start(s32[4]{0:T(128)} %length_ref.5) | copy-start | bytes 52
  9.2 17.0 %collective-permute-start = (bf16[2,8192]{1,0:T(2,128)(2,1)}, bf16[2,8192]{1,0:T(2,128)(2,1)S(1)}, u32[]{:S(2)}, u32[]{:S(2)}) collective-permute-start(bf16[2,8192]{1,0:T(2,128)(2,1)} %get-tuple-element.16), channel_id=1, source_target_pairs={{24,8},{0,16},{25,9},{1,17},{26,10},{2,18},{27,11},{3,19},{28,12},... | collective-permute-start | bytes 98312 | tf_op jit(solution)/shard_map/ppermute | solution.py:436
  16.6 12.6 %collective-permute-start.4 = (bf16[208,1024]{1,0:T(8,128)(2,1)}, bf16[208,1024]{1,0:T(8,128)(2,1)S(1)}, u32[]{:S(2)}, u32[]{:S(2)}) collective-permute-start(bf16[208,1024]{1,0:T(8,128)(2,1)} %get-tuple-element.19), channel_id=1, source_target_pairs={{0,8},{8,0},{16,24},{24,16},{1,9},{9,1},{17,25},{25,17},{2,10},{10... | collective-permute-start | bytes 1277960 | tf_op jit(solution)/shard_map/ppermute | solution.py:438
  18.9 33.5 %collective-permute-start.3 = (bf16[320,1024]{1,0:T(8,128)(2,1)S(1)}, bf16[320,1024]{1,0:T(8,128)(2,1)S(1)}, u32[]{:S(2)}, u32[]{:S(2)}) collective-permute-start(bf16[320,1024]{1,0:T(8,128)(2,1)S(1)} %collective-permute-done.2.a1_ref), channel_id=1, source_target_pairs={{0,24},{24,0},{1,25},{25,1},{2,26},{26,2},{3,27},{27,3},{4,28},{28... | collective-permute-start | bytes 1966088 | tf_op jit(solution)/shard_map/ppermute | solution.py:443
  27.1 7.8 %collective-permute-start.1 = (bf16[160,128]{1,0:T(8,128)(2,1)S(1)}, bf16[160,128]{1,0:T(8,128)(2,1)S(1)}, u32[]{:S(2)}, u32[]{:S(2)}) collective-permute-start(bf16[160,128]{1,0:T(8,128)(2,1)S(1)} %get-tuple-element.17), channel_id=1, source_target_pairs={{8,24},{16,0},{9,25},{17,1},{10,26},{18,2},{11,27},{19,3},{12,28},... | collective-permute-start | bytes 122888 | tf_op jit(solution)/shard_map/ppermute | solution.py:442
  29.2 23.2 %collective-permute-start.5 = (bf16[208,1024]{1,0:T(8,128)(2,1)S(1)}, bf16[208,1024]{1,0:T(8,128)(2,1)S(1)}, u32[]{:S(2)}, u32[]{:S(2)}) collective-permute-start(bf16[208,1024]{1,0:T(8,128)(2,1)S(1)} %collective-permute-done.4.a2_ref), channel_id=1, source_target_pairs={{0,24},{24,0},{1,25},{25,1},{2,26},{26,2},{3,27},{27,3},{4,28},{28... | collective-permute-start | bytes 1277960 | tf_op jit(solution)/shard_map/ppermute | solution.py:444
